TPU v7x, 32 devices: a whole 2x2x4 slice. The times are simulated.
32 devices in a mesh: seq: 8 (over z, x), head: 4 (over y, core).
Axes of the slice: x: 2, y: 2, z: 4, core: 2. Of those that a mesh axis runs over, the one named last changes fastest.
Arguments:
- x_in: bfloat16 [8, 1024, 1536], P(None, 'seq'), may hold values from -6 to 6
- seg_ids: int32 [8, 1024], P(None, 'seq'), may hold values from 0 to 31, as said below
- norm1_gain: float32 [1536], P('seq'), may hold values from 0.5 to 1.5
- w_in_x: float32 [1536, 3072], P('seq', 'head'), may hold values from -0.15625 to 0.15625
- w_in_z: float32 [1536, 3072], P('seq', 'head'), may hold values from -0.15625 to 0.15625
- conv_w: float32 [4, 3072], P(None, ('head', 'seq')), may hold values from -3 to 3
- conv_b: float32 [3072], P(('head', 'seq')), may hold values from -3 to 3
- w_xproj: float32 [3072, 128], P(('head', 'seq')), may hold values from -0.109375 to 0.109375
- ssm_gain: float32 [128], P('seq'), may hold values from 0.5 to 1.5
- w_dt: float32 [96, 3072], P(None, ('head', 'seq')), may hold values from -0.625 to 0.625
- dt_bias: float32 [3072], P(('head', 'seq')), may hold values from -14 to -2
- a_log: float32 [3072, 16], P(('head', 'seq')), may hold values from -1 to 1.5
- d_skip: float32 [3072], P(('head', 'seq')), may hold values from 0.5 to 2
- w_out: float32 [3072, 1536], P('head', 'seq'), may hold values from -0.109375 to 0.109375
- norm2_gain: float32 [1536], P('seq'), may hold values from 0.5 to 1.5
- w_gate: float32 [1536, 4096], P('seq', 'head'), may hold values from -0.15625 to 0.15625
- w_up: float32 [1536, 4096], P('seq', 'head'), may hold values from -0.15625 to 0.15625
- w_down: float32 [4096, 1536], P('head', 'seq'), may hold values from -0.09375 to 0.09375
- d_out: bfloat16 [8, 1024, 1536], P(None, 'seq'), may hold values from -6 to 6
Outputs:
- block_out: bfloat16 [8, 1024, 1536], P(None, 'seq')
- grad_input: float32 [8, 1024, 1536], P(None, 'seq')
- grad_norm1_gain: float32 [1536], P('seq')
- grad_w_in_x: float32 [1536, 3072], P('seq', 'head')
- grad_w_in_z: float32 [1536, 3072], P('seq', 'head')
- grad_conv_w: float32 [4, 3072], P(None, ('head', 'seq'))
- grad_conv_b: float32 [3072], P(('head', 'seq'))
- grad_w_xproj: float32 [3072, 128], P(('head', 'seq'))
- grad_ssm_gain: float32 [128], P('seq')
- grad_w_dt: float32 [96, 3072], P(None, ('head', 'seq'))
- grad_dt_bias: float32 [3072], P(('head', 'seq'))
- grad_a_log: float32 [3072, 16], P(('head', 'seq'))
- grad_d_skip: float32 [3072], P(('head', 'seq'))
- grad_w_out: float32 [3072, 1536], P('head', 'seq')
- grad_norm2_gain: float32 [1536], P('seq')
- grad_w_gate: float32 [1536, 4096], P('seq', 'head')
- grad_w_up: float32 [1536, 4096], P('seq', 'head')
- grad_w_down: float32 [4096, 1536], P('head', 'seq')
Inputs may be any that keep to these rules, and one draw needn't show every extreme that they name: `seg_ids`: document numbers never fall along a sequence; a document begins where the number changes. The last document of every sequence has number 31. One sequence, chosen by the seed, is a single document. Documents other than a sequence's last have 1024 // 20 to 512 tokens.
All inputs are finite; a program needn't handle non-finite values.
Results may differ from a plain program's by a relative error of at most 0.015.
The roundings to bfloat16 on the way count: a program that leaves them out, or rounds other values in their place, can miss the bound.
Values may be sent and summed in bfloat16 or wider, within the bound.
A program may use at most 192 MiB of HBM per device.

v0:
```python
import jax
import jax.numpy as jnp
from jax import lax
from jax.sharding import PartitionSpec as P

EPS = 1e-06
HIGH = lax.Precision.HIGHEST


def shifted(value, axis, steps):
    count = lax.axis_size(axis)
    initial, last = (max(0, -steps), min(count, count - steps))
    return lax.ppermute(value, axis, [(source, source + steps) for source in range(initial, last)])


def entering(part, axis, combine, identity, reverse):
    count = lax.axis_size(axis)
    place = lax.axis_index(axis)
    ahead = count - 1 - place if reverse else place
    gathered = jax.tree.map(lambda a: lax.all_gather(a, axis), part)
    state = jax.tree.map(lambda a, e: jnp.zeros_like(a) + jnp.asarray(e, a.dtype), part, identity)

    def one(hop, state):
        source = count - 1 - hop if reverse else hop
        return combine(
            state, jax.tree.map(lambda a: lax.dynamic_index_in_dim(a, source, 0, False), gathered)
        )

    return lax.fori_loop(0, ahead, one, state)


def norm_rows(values, gain_vec):
    inv_rms = lax.rsqrt(jnp.mean(values * values, axis=-1, keepdims=True) + EPS)
    return (values * inv_rms * gain_vec, inv_rms)


def norm_back(values, inv_rms, gain_vec, grad_rows):
    normed = values * inv_rms
    gain_grad = jnp.sum(grad_rows * normed, axis=0)
    scaled = grad_rows * gain_vec
    value_grad = inv_rms * (scaled - normed * jnp.mean(scaled * normed, axis=-1, keepdims=True))
    return (value_grad, gain_grad)


def silu_slope(values):
    logistic = jax.nn.sigmoid(values)
    return logistic * (1.0 + values * (1.0 - logistic))


def state_run(inputs_u, step_size, b_norm, c_norm, decay_rates, keep_flag, initial):
    shard_len = inputs_u.shape[1]
    unroll = 8

    def to_blocks(member):
        leading = jnp.moveaxis(member, 1, 0)
        return leading.reshape((shard_len // unroll, unroll) + leading.shape[1:])

    def block_fn(carried, block_items):
        u_blk, step_blk, b_blk, c_blk, keep_blk = block_items
        outputs = []
        for offset in range(unroll):
            decay_now = keep_blk[offset][:, None, None] * jnp.exp(
                step_blk[offset][:, :, None] * decay_rates[None]
            )
            carried = (
                decay_now * carried
                + (step_blk[offset] * u_blk[offset])[:, :, None] * b_blk[offset][:, None, :]
            )
            outputs.append(jnp.einsum("sen,sn->se", carried, c_blk[offset], precision=HIGH))
        return (carried, jnp.stack(outputs))

    block_items = tuple(
        (to_blocks(member) for member in (inputs_u, step_size, b_norm, c_norm, keep_flag))
    )
    final_state, results = lax.scan(jax.checkpoint(block_fn), initial, block_items)
    results = results.reshape((shard_len,) + results.shape[2:])
    return (jnp.moveaxis(results, 0, 1), final_state)


def carry_forward(earlier, latter):
    return (earlier[0] * latter[0], earlier[1] * latter[0] + latter[1])


def carry_backward(earlier, latter):
    return (latter[0] * earlier[0], latter[1] + latter[0] * earlier[1])


def shards(
    x_in,
    seg_ids,
    norm1_gain,
    w_in_x,
    w_in_z,
    conv_w,
    conv_b,
    w_xproj,
    ssm_gain,
    w_dt,
    dt_bias,
    a_log,
    d_skip,
    w_out,
    norm2_gain,
    w_gate,
    w_up,
    w_down,
    d_out,
):
    bf16 = jnp.bfloat16
    (
        full_norm1,
        full_in_x,
        full_in_z,
        full_conv_w,
        full_conv_b,
        full_xproj,
        full_ssm_gain,
        full_w_dt,
        full_dt_bias,
        full_a_log,
        full_d_skip,
        full_w_out,
        full_norm2,
        full_gate,
        full_up,
        full_down,
    ) = (
        lax.all_gather(norm1_gain.astype(bf16), "seq", axis=0, tiled=True),
        lax.all_gather(w_in_x.astype(bf16), "seq", axis=0, tiled=True),
        lax.all_gather(w_in_z.astype(bf16), "seq", axis=0, tiled=True),
        lax.all_gather(conv_w.astype(bf16), "seq", axis=1, tiled=True),
        lax.all_gather(conv_b.astype(bf16), "seq", axis=0, tiled=True),
        lax.all_gather(w_xproj.astype(bf16), "seq", axis=0, tiled=True),
        lax.all_gather(ssm_gain.astype(bf16), "seq", axis=0, tiled=True),
        lax.all_gather(w_dt.astype(bf16), "seq", axis=1, tiled=True),
        lax.all_gather(dt_bias.astype(bf16), "seq", axis=0, tiled=True),
        lax.all_gather(a_log.astype(bf16), "seq", axis=0, tiled=True),
        lax.all_gather(d_skip.astype(bf16), "seq", axis=0, tiled=True),
        lax.all_gather(w_out.astype(bf16), "seq", axis=1, tiled=True),
        lax.all_gather(norm2_gain.astype(bf16), "seq", axis=0, tiled=True),
        lax.all_gather(w_gate.astype(bf16), "seq", axis=0, tiled=True),
        lax.all_gather(w_up.astype(bf16), "seq", axis=0, tiled=True),
        lax.all_gather(w_down.astype(bf16), "seq", axis=1, tiled=True),
    )
    seq_count, shard_len, model_width = x_in.shape
    row_count = seq_count * shard_len
    kernel = full_conv_w.shape[0]
    step_rank = full_w_dt.shape[0]
    state_dim = full_a_log.shape[1]
    inner_dim = full_in_x.shape[1]
    norm1_vec = full_norm1.astype(jnp.float32)
    x_rows = x_in.astype(jnp.float32).reshape(row_count, model_width)
    normed1, scale_one = norm_rows(x_rows, norm1_vec)
    x_norm = normed1.astype(bf16)
    x_inner = jnp.dot(x_norm, full_in_x, preferred_element_type=jnp.float32).astype(bf16)
    z_gate = jnp.dot(x_norm, full_in_z, preferred_element_type=jnp.float32)
    inner_seq = x_inner.reshape(seq_count, shard_len, inner_dim)
    prev_tail, prev_ids = shifted(
        (inner_seq[:, shard_len - kernel + 1 :], seg_ids[:, shard_len - kernel + 1 :]), "seq", 1
    )
    extended = jnp.concatenate([prev_tail, inner_seq], axis=1).astype(jnp.float32)
    ext_ids = jnp.concatenate([prev_ids, seg_ids], axis=1)
    conv_weight = full_conv_w.astype(jnp.float32)
    x_conv = jnp.zeros((seq_count, shard_len, inner_dim), jnp.float32) + full_conv_b.astype(
        jnp.float32
    )
    same_docs = []
    for offset in range(kernel):
        first_row = kernel - 1 - offset
        same_doc = (ext_ids[:, first_row : first_row + shard_len] == seg_ids).astype(jnp.float32)
        same_docs.append(same_doc)
        x_conv = (
            x_conv
            + conv_weight[offset]
            * extended[:, first_row : first_row + shard_len]
            * same_doc[:, :, None]
        )
    u_low = jax.nn.silu(x_conv).astype(bf16)
    u_rows = u_low.reshape(row_count, inner_dim)
    projected = lax.psum(jnp.dot(u_rows, full_xproj, preferred_element_type=jnp.float32), "head")
    ssm_vec = full_ssm_gain.astype(jnp.float32)
    b_end = step_rank + state_dim
    dt_normed, dt_scale = norm_rows(projected[:, :step_rank], ssm_vec[:step_rank])
    b_normed, b_scale = norm_rows(projected[:, step_rank:b_end], ssm_vec[step_rank:b_end])
    c_normed, c_scale = norm_rows(projected[:, b_end:], ssm_vec[b_end:])
    dt_low = dt_normed.astype(bf16)
    dt_pre = jnp.dot(dt_low, full_w_dt, preferred_element_type=jnp.float32) + full_dt_bias.astype(
        jnp.float32
    )
    step_size = jax.nn.softplus(dt_pre)
    decay_rates = -jnp.exp(full_a_log.astype(jnp.float32))
    earlier_ids = jnp.concatenate([prev_ids[:, -1:], seg_ids[:, :-1]], axis=1)
    keep_flag = (seg_ids == earlier_ids).astype(jnp.float32)
    u_seq = u_low.astype(jnp.float32)
    step_seq = step_size.reshape(seq_count, shard_len, inner_dim)
    b_seq = b_normed.reshape(seq_count, shard_len, state_dim)
    c_seq = c_normed.reshape(seq_count, shard_len, state_dim)
    zero_state = jnp.zeros((seq_count, inner_dim, state_dim), jnp.float32)
    y_local, local_end = state_run(
        u_seq, step_seq, b_seq, c_seq, decay_rates, keep_flag, zero_state
    )
    lower_ones = (jnp.arange(shard_len)[:, None] >= jnp.arange(shard_len)[None, :]).astype(
        jnp.float32
    )
    cum_step = jnp.einsum("tq,sqe->ste", lower_ones, step_seq, precision=HIGH)
    alive_mask = jnp.cumprod(keep_flag, axis=1)
    total_decay = alive_mask[:, -1][:, None, None] * jnp.exp(
        cum_step[:, -1][:, :, None] * decay_rates[None]
    )
    unused_decay, start_state = entering(
        (total_decay, local_end),
        "seq",
        carry_forward,
        (jnp.ones_like(total_decay), jnp.zeros_like(local_end)),
        False,
    )

    def correction(arrays):
        cum_one, alive_one, c_one, start_one = arrays
        decays = jnp.exp(cum_one[:, :, None] * decay_rates[None]) * alive_one[:, None, None]
        return jnp.einsum("ten,tn,en->te", decays, c_one, start_one, precision=HIGH)

    y_state = y_local + lax.map(correction, (cum_step, alive_mask, c_seq, start_state))
    skip_vec = full_d_skip.astype(jnp.float32)
    y_full = y_state.reshape(row_count, inner_dim) + skip_vec * u_seq.reshape(row_count, inner_dim)
    silu_z = jax.nn.silu(z_gate)
    g_low = (y_full * silu_z).astype(bf16)
    mixer_term = jnp.dot(g_low, full_w_out, preferred_element_type=jnp.float32)
    norm2_vec = full_norm2.astype(jnp.float32)
    hidden = x_rows + lax.psum(mixer_term, "head")
    normed2, scale_two = norm_rows(hidden, norm2_vec)
    x_norm2 = normed2.astype(bf16)
    gate_proj = jnp.dot(x_norm2, full_gate, preferred_element_type=jnp.float32)
    up_proj = jnp.dot(x_norm2, full_up, preferred_element_type=jnp.float32)
    silu_gate = jax.nn.silu(gate_proj)
    act_low = (silu_gate * up_proj).astype(bf16)
    ffn_term = jnp.dot(act_low, full_down, preferred_element_type=jnp.float32)
    ffn_out = lax.psum(ffn_term, "head")
    block_out = (hidden + ffn_out).astype(bf16).reshape(seq_count, shard_len, model_width)
    grad_low = d_out.reshape(row_count, model_width)
    grad_rows = grad_low.astype(jnp.float32)
    grad_down = jnp.einsum("rf,rd->fd", act_low, grad_low, preferred_element_type=jnp.float32)
    d_act = jnp.einsum("rd,fd->rf", grad_low, full_down, preferred_element_type=jnp.float32)
    d_gate = (d_act * up_proj * silu_slope(gate_proj)).astype(bf16)
    d_up = (d_act * silu_gate).astype(bf16)
    grad_gate = jnp.einsum("rd,rf->df", x_norm2, d_gate, preferred_element_type=jnp.float32)
    grad_up = jnp.einsum("rd,rf->df", x_norm2, d_up, preferred_element_type=jnp.float32)
    norm2_term = jnp.einsum(
        "rf,df->rd", d_gate, full_gate, preferred_element_type=jnp.float32
    ) + jnp.einsum("rf,df->rd", d_up, full_up, preferred_element_type=jnp.float32)
    d_norm2 = lax.psum(norm2_term, "head")
    d_hidden_part, grad_norm2 = norm_back(hidden, scale_two, norm2_vec, d_norm2)
    d_hidden = grad_rows + d_hidden_part
    d_mix = d_hidden.astype(bf16)
    grad_out_w = jnp.einsum("re,rd->ed", g_low, d_mix, preferred_element_type=jnp.float32)
    d_g = jnp.einsum("rd,ed->re", d_mix, full_w_out, preferred_element_type=jnp.float32)
    d_y = d_g * silu_z
    d_z = (d_g * y_full * silu_slope(z_gate)).astype(bf16)
    grad_skip = jnp.sum(d_y * u_seq.reshape(row_count, inner_dim), axis=0)
    d_y_seq = d_y.reshape(seq_count, shard_len, inner_dim)

    def own_term(arrays):
        cum_one, alive_one, c_one, dy_one = arrays
        decays = jnp.exp(cum_one[:, :, None] * decay_rates[None]) * alive_one[:, None, None]
        return jnp.einsum("ten,tn,te->en", decays, c_one, dy_one, precision=HIGH)

    own_adjoint = lax.map(own_term, (cum_step, alive_mask, c_seq, d_y_seq))
    unused_back, end_adjoint = entering(
        (total_decay, own_adjoint),
        "seq",
        carry_backward,
        (jnp.ones_like(total_decay), jnp.zeros_like(own_adjoint)),
        True,
    )

    def local_state(inputs_u, steps_in, b_in, c_in, rate_in, start_in):
        return state_run(inputs_u, steps_in, b_in, c_in, rate_in, keep_flag, start_in)

    unused_out, pullback = jax.vjp(
        local_state, u_seq, step_seq, b_seq, c_seq, decay_rates, start_state
    )
    d_u_state, d_step, d_b, d_c, d_rates, unused_start = pullback((d_y_seq, end_adjoint))
    grad_alog = d_rates * decay_rates
    d_pre = d_step.reshape(row_count, inner_dim) * jax.nn.sigmoid(dt_pre)
    grad_bias = jnp.sum(d_pre, axis=0)
    d_pre_low = d_pre.astype(bf16)
    grad_step_w = jnp.einsum("rk,re->ke", dt_low, d_pre_low, preferred_element_type=jnp.float32)
    d_dt_part = jnp.einsum("re,ke->rk", d_pre_low, full_w_dt, preferred_element_type=jnp.float32)
    d_stats = lax.psum(
        jnp.concatenate(
            [d_dt_part, d_b.reshape(row_count, state_dim), d_c.reshape(row_count, state_dim)],
            axis=1,
        ),
        "head",
    )
    d_dt_raw, grad_dt_gain = norm_back(
        projected[:, :step_rank], dt_scale, ssm_vec[:step_rank], d_stats[:, :step_rank]
    )
    d_b_raw, grad_b_gain = norm_back(
        projected[:, step_rank:b_end],
        b_scale,
        ssm_vec[step_rank:b_end],
        d_stats[:, step_rank:b_end],
    )
    d_c_raw, grad_c_gain = norm_back(
        projected[:, b_end:], c_scale, ssm_vec[b_end:], d_stats[:, b_end:]
    )
    d_proj = jnp.concatenate([d_dt_raw, d_b_raw, d_c_raw], axis=1)
    grad_ssm = jnp.concatenate([grad_dt_gain, grad_b_gain, grad_c_gain])
    grad_xproj = jnp.einsum("re,rk->ek", u_rows, d_proj, preferred_element_type=jnp.float32)
    d_u = (
        d_y * skip_vec
        + d_u_state.reshape(row_count, inner_dim)
        + jnp.einsum("rk,ek->re", d_proj, full_xproj, preferred_element_type=jnp.float32)
    )
    d_conv = d_u.reshape(seq_count, shard_len, inner_dim) * silu_slope(x_conv)
    grad_conv_b = jnp.sum(d_conv, axis=(0, 1))
    d_extended = jnp.zeros((seq_count, shard_len + kernel - 1, inner_dim), jnp.float32)
    conv_grads = []
    for offset in range(kernel):
        first_row = kernel - 1 - offset
        masked = d_conv * same_docs[offset][:, :, None]
        conv_grads.append(
            jnp.sum(masked * extended[:, first_row : first_row + shard_len], axis=(0, 1))
        )
        d_extended = d_extended + jnp.pad(
            conv_weight[offset] * masked, ((0, 0), (first_row, kernel - 1 - first_row), (0, 0))
        )
    grad_conv_w = jnp.stack(conv_grads)
    from_next = shifted(d_extended[:, : kernel - 1].astype(jnp.bfloat16), "seq", -1).astype(
        jnp.float32
    )
    d_inner = d_extended[:, kernel - 1 :] + jnp.pad(
        from_next, ((0, 0), (shard_len - kernel + 1, 0), (0, 0))
    )
    d_inner_low = d_inner.astype(bf16).reshape(row_count, inner_dim)
    grad_in_x = jnp.einsum("rd,re->de", x_norm, d_inner_low, preferred_element_type=jnp.float32)
    grad_in_z = jnp.einsum("rd,re->de", x_norm, d_z, preferred_element_type=jnp.float32)
    d_norm1 = lax.psum(
        jnp.einsum("re,de->rd", d_inner_low, full_in_x, preferred_element_type=jnp.float32)
        + jnp.einsum("re,de->rd", d_z, full_in_z, preferred_element_type=jnp.float32),
        "head",
    )
    d_input_part, grad_norm1 = norm_back(x_rows, scale_one, norm1_vec, d_norm1)
    grad_input = (d_hidden + d_input_part).reshape(seq_count, shard_len, model_width)
    summed = tuple(
        (
            lax.psum_scatter(grad_norm1, "seq", scatter_dimension=0, tiled=True),
            lax.psum_scatter(grad_in_x, "seq", scatter_dimension=0, tiled=True),
            lax.psum_scatter(grad_in_z, "seq", scatter_dimension=0, tiled=True),
            lax.psum_scatter(grad_conv_w, "seq", scatter_dimension=1, tiled=True),
            lax.psum_scatter(grad_conv_b, "seq", scatter_dimension=0, tiled=True),
            lax.psum_scatter(grad_xproj, "seq", scatter_dimension=0, tiled=True),
            lax.psum_scatter(grad_ssm, "seq", scatter_dimension=0, tiled=True),
            lax.psum_scatter(grad_step_w, "seq", scatter_dimension=1, tiled=True),
            lax.psum_scatter(grad_bias, "seq", scatter_dimension=0, tiled=True),
            lax.psum_scatter(grad_alog, "seq", scatter_dimension=0, tiled=True),
            lax.psum_scatter(grad_skip, "seq", scatter_dimension=0, tiled=True),
            lax.psum_scatter(grad_out_w, "seq", scatter_dimension=1, tiled=True),
            lax.psum_scatter(grad_norm2, "seq", scatter_dimension=0, tiled=True),
            lax.psum_scatter(grad_gate, "seq", scatter_dimension=0, tiled=True),
            lax.psum_scatter(grad_up, "seq", scatter_dimension=0, tiled=True),
            lax.psum_scatter(grad_down, "seq", scatter_dimension=1, tiled=True),
        )
    )
    return (block_out, grad_input) + summed


def solution(mesh):
    placed = (
        P(None, "seq", None),
        P(None, "seq"),
        P("seq"),
        P("seq", "head"),
        P("seq", "head"),
        P(None, ("head", "seq")),
        P(("head", "seq")),
        P(("head", "seq"), None),
        P("seq"),
        P(None, ("head", "seq")),
        P(("head", "seq")),
        P(("head", "seq"), None),
        P(("head", "seq")),
        P("head", "seq"),
        P("seq"),
        P("seq", "head"),
        P("seq", "head"),
        P("head", "seq"),
        P(None, "seq", None),
    )
    return jax.shard_map(
        shards,
        mesh=mesh,
        in_specs=placed,
        out_specs=(
            P(None, "seq", None),
            P(None, "seq", None),
            P("seq"),
            P("seq", "head"),
            P("seq", "head"),
            P(None, ("head", "seq")),
            P(("head", "seq")),
            P(("head", "seq"), None),
            P("seq"),
            P(None, ("head", "seq")),
            P(("head", "seq")),
            P(("head", "seq"), None),
            P(("head", "seq")),
            P("head", "seq"),
            P("seq"),
            P("seq", "head"),
            P("seq", "head"),
            P("head", "seq"),
        ),
        check_vma=False,
    )
```

profile of v0, /device:TPU:0, one launch (start us, length us, event | category | flops | bytes accessed | tf_op | source)
XLA Modules:
  0.0 2734.5 jit_solution(13742197058807433871)
XLA Ops:
  23.4 36.3 %all-reduce.59 = (bf16[1536]{0:T(1024)(128)(2,1)S(1)}, bf16[768]{0:T(1024)(128)(2,1)S(1)}, bf16[128]{0:T(256)(128)(2,1)S(1)}, bf16[768]{0:T(1024)(128)(2,1)S(1)}...) all-reduce(bf16[1536]{0:T(1024)(128)(2,1)S(1)} %dynamic-update-slice.1, ...), channel_id=1, replica_groups=mesh['seq'=8,'head'=4] {'seq'}, use_global_device_ids=true, to_apply=%add.46 | all-reduce | flops 5504 | bytes 22016
  60.5 16.4 all-gather.2
  79.4 30.4 %all-gather.3 = bf16[8,96,16]{1,2,0:T(8,128)(2,1)S(1)} all-gather(bf16[1,96,16]{1,2,0:T(8,128)(2,1)S(1)} %convert_bitcast_fusion.1), channel_id=1, replica_groups=mesh['seq'=8,'head'=4] {'seq'}, dimensions={0}, use_global_device_ids=true | all-gather | bytes 27648 | tf_op jit(solution)/shard_map/all_gather | solution.py:137
  110.5 30.6 %all_gather.70 = bf16[768,128]{1,0:T(8,128)(2,1)S(1)} all-gather(bf16[96,128]{1,0:T(8,128)(2,1)S(1)} %convert_element_type.170), channel_id=1, replica_groups=mesh['seq'=8,'head'=4] {'seq'}, dimensions={0}, use_global_device_ids=true | all-gather | bytes 221184 | tf_op jit(solution)/shard_map/all_gather | solution.py:133
  163.1 32.0 %all_gather.72 = bf16[96,768]{0,1:T(8,128)(2,1)S(1)} all-gather(bf16[96,96]{0,1:T(8,128)(2,1)S(1)} %copy.175), channel_id=1, replica_groups=mesh['seq'=8,'head'=4] {'seq'}, dimensions={1}, use_global_device_ids=true | all-gather | bytes 165888 | tf_op jit(solution)/shard_map/all_gather | solution.py:135
  216.6 251.1 %while.102 = (s32[]{:T(128)}, f32[8,768,16]{1,2,0:T(8,128)}, f32[16,8,8,768]{3,2,1,0:T(8,128)}, f32[16,8,8]{2,1,0:T(8,128)}, f32[16,8,8,768]{3,2,1,0:T(8,128)}, ...) while((s32[]{:T(128)}, f32[8,768,16]{1,2,0:T(8,128)}, ...), condition=%wide.region_6.7_spmd.clone, body=%wide.region_5.6_spmd.clone.sunk | while | flops 16171018 | bytes 9573613 | solution.py:75
  480.2 48.5 %all-gather.28.cloned.1.call-done = f32[64,768,16]{1,2,0:T(8,128)} async-done(((f32[8,768,16]{1,2,0:T(8,128)}), f32[64,768,16]{1,2,0:T(8,128)}) %all-gather.28.cloned.1.call-update) | async-done | bytes 3145744 | tf_op jit(solution)/shard_map/all_gather | solution.py:20
  528.6 61.7 %all-gather.16.cloned.1.call-done = f32[8,8,768,16]{2,3,1,0:T(8,128)} async-done(((f32[1,8,768,16]{2,3,1,0:T(8,128)}), f32[8,8,768,16]{2,3,1,0:T(8,128)}) %all-gather.16.cloned.1.call-update) | async-done | bytes 3145744 | tf_op jit(solution)/shard_map/all_gather | solution.py:20
  591.1 53.3 %while.98 = (s32[]{:T(128)}, f32[8,128,768]{2,1,0:T(8,128)}, f32[8,128,768]{2,1,0:T(8,128)}, f32[768,16]{0,1:T(8,128)S(1)}, f32[8,128]{1,0:T(8,128)S(1)}, /*inde...) while((s32[]{:T(128)}, f32[8,128,768]{2,1,0:T(8,128)}, f32[8,128,768]{2,1,0:T(8,128)}, ...), condition=%wide.region_11.12_spmd, body=%wide.region_10.11_spmd.sunk | while | flops 7766018 | bytes 2599013 | solution.py:223
  650.1 9.4 multiply_convert_fusion.5
  659.5 36.9 %all-gather.20.cloned.1.call-done = bf16[768,1536]{0,1:T(8,128)(2,1)} async-done(((bf16[768,192]{0,1:T(8,128)(2,1)}), bf16[768,1536]{0,1:T(8,128)(2,1)}) %all-gather.20.cloned.1.call-update) | async-done | bytes 2359312 | tf_op jit(solution)/shard_map/all_gather | solution.py:139
  710.2 112.0 %all-reduce.68.cloned.1.call-done = f32[1024,1536]{1,0:T(8,128)} async-done(((f32[1024,1536]{1,0:T(8,128)}), f32[1024,1536]{1,0:T(8,128)}) %all-reduce.68.cloned.1.call-update) | async-done | bytes 6291472 | tf_op jit(solution)/shard_map/psum | solution.py:230
  829.2 56.5 %all-gather.22.cloned.1.call-done = bf16[1536,1024]{1,0:T(8,128)(2,1)} async-done(((bf16[192,1024]{1,0:T(8,128)(2,1)}), bf16[1536,1024]{1,0:T(8,128)(2,1)}) %all-gather.22.cloned.1.call-update) | async-done | bytes 3145744 | tf_op jit(solution)/shard_map/all_gather | solution.py:141
  892.6 54.9 %all-gather.24.cloned.1.call-done = bf16[1536,1024]{1,0:T(8,128)(2,1)} async-done(((bf16[192,1024]{1,0:T(8,128)(2,1)}), bf16[1536,1024]{1,0:T(8,128)(2,1)}) %all-gather.24.cloned.1.call-update) | async-done | bytes 3145744 | tf_op jit(solution)/shard_map/all_gather | solution.py:142
  955.7 53.5 %all-gather.26.cloned.1.call-done = bf16[1024,1536]{0,1:T(8,128)(2,1)} async-done(((bf16[1024,192]{0,1:T(8,128)(2,1)}), bf16[1024,1536]{0,1:T(8,128)(2,1)}) %all-gather.26.cloned.1.call-update) | async-done | bytes 3145744 | tf_op jit(solution)/shard_map/all_gather | solution.py:143
  1009.2 9.3 multiply_convert_fusion.1
  1028.4 117.4 %all-reduce.70.cloned.1.call-done = f32[1024,1536]{1,0:T(8,128)} async-done(((f32[1024,1536]{1,0:T(8,128)}), f32[1024,1536]{1,0:T(8,128)}) %all-reduce.70.cloned.1.call-update) | async-done | bytes 6291472 | tf_op jit(solution)/shard_map/psum | solution.py:251
  1167.4 31.4 %while.99 = (s32[]{:T(128)}, f32[8,768,16]{1,2,0:T(8,128)}, f32[8,128,768]{2,1,0:T(8,128)}, f32[8,128,768]{2,1,0:T(8,128)}, f32[768,16]{0,1:T(8,128)S(1)}, /*ind...) while((s32[]{:T(128)}, f32[8,768,16]{1,2,0:T(8,128)}, f32[8,128,768]{2,1,0:T(8,128)}, ...), condition=%wide.region_18.19_spmd, body=%wide.region_17.18_spmd.sunk | while | flops 7852034 | bytes 2795617 | solution.py:267
  1199.0 70.9 %while.101 = (s32[]{:T(128)}, f32[8,768,16]{1,2,0:T(8,128)S(1)}, f32[16,8,768,16]{2,3,1,0:T(8,128)}, f32[16,8,8]{2,1,0:T(8,128)S(1)}, f32[16,8,8,768]{3,2,1,0:T(...) while((s32[]{:T(128)}, f32[8,768,16]{1,2,0:T(8,128)S(1)}, ...), condition=%wide.region_22.23_spmd, body=%wide.region_21.22_spmd.sunk | while | flops 3981321 | bytes 3012693 | solution.py:75
  1275.2 9.4 while.100
  1289.6 260.1 %while.103 = (s32[]{:T(128)}, f32[768,16]{0,1:T(8,128)S(1)}, f32[8,768,16]{1,2,0:T(8,128)S(1)}, f32[16,8,8,768]{3,2,1,0:T(8,128)}, f32[16,8,8,768]{3,2,1,0:T(8,1...) while((s32[]{:T(128)}, f32[768,16]{0,1:T(8,128)S(1)}, ...), condition=%wide.region_56.57_spmd.clone, body=%wide.region_23.56_spmd.clone.sunk | while | flops 33104900 | bytes 20806336 | solution.py:75
  1571.4 15.1 all-reduce.72.cloned.1.call-done
  1674.2 40.4 %reduce-scatter.31.cloned.1.call-done = f32[96,4]{1,0:T(8,128)} async-done(((f32[768,4]{1,0:T(8,128)}), f32[96,4]{1,0:T(8,128)}) %reduce-scatter.31.cloned.1.call-update) | async-done | bytes 1552
  1716.0 62.1 %reduce-scatter.33.cloned.1.call-done = f32[96,96]{1,0:T(8,128)} async-done(((f32[768,96]{1,0:T(8,128)}), f32[96,96]{1,0:T(8,128)}) %reduce-scatter.33.cloned.1.call-update) | async-done | bytes 36880
  1779.6 221.1 %all-reduce.74.cloned.1.call-done = (f32[1024,1536]{1,0:T(8,128)}, f32[1024,1536]{1,0:T(8,128)}) async-done(((f32[1024,1536]{1,0:T(8,128)}, f32[1024,1536]{1,0:T(8,128)}), (f32[1024,1536]{1,0:T(8,128)}, f32[1024,1536]{1,0:T(8,128)})) %all-reduce.74.cloned.1.call-update) | async-done | bytes 12582928 | tf_op jit(solution)/shard_map/psum | solution.py:238
  2004.6 37.1 %all-reduce.57 = (f32[1536]{0:T(1024)S(1)}, f32[768]{0:T(1024)S(1)}, f32[128]{0:T(128)S(1)}, f32[768]{0:T(1024)S(1)}, f32[768]{0:T(1024)S(1)}, /*index=5*/f32[1536]{0:T(1024)S(1)}) all-reduce(f32[1536]{0:T(1024)S(1)} %get-tuple-element.901, f32[768]{0:T(1024)S(1)} %get-tuple-element.907, ...), channel_id=4, replica_groups=mesh['seq'=8,'head'=4] {'seq'}, use_global_device_ids=true, to_apply=%region_64.65.clone | all-reduce | flops 5504 | bytes 44032
  2066.0 98.8 %reduce-scatter.23.cloned.1.call-done = f32[768,192]{0,1:T(8,128)} async-done(((f32[768,1536]{0,1:T(8,128)}), f32[768,192]{0,1:T(8,128)}) %reduce-scatter.23.cloned.1.call-update) | async-done | bytes 589840 | tf_op jit(solution)/shard_map/reduce_scatter | solution.py:359
  2164.7 121.7 %reduce-scatter.25.cloned.1.call-done = f32[192,1024]{1,0:T(8,128)} async-done(((f32[1536,1024]{1,0:T(8,128)}), f32[192,1024]{1,0:T(8,128)}) %reduce-scatter.25.cloned.1.call-update) | async-done | bytes 786448 | tf_op jit(solution)/shard_map/reduce_scatter | solution.py:361
  2286.4 121.3 %reduce-scatter.27.cloned.1.call-done = f32[192,1024]{1,0:T(8,128)} async-done(((f32[1536,1024]{1,0:T(8,128)}), f32[192,1024]{1,0:T(8,128)}) %reduce-scatter.27.cloned.1.call-update) | async-done | bytes 786448 | tf_op jit(solution)/shard_map/reduce_scatter | solution.py:362
  2407.7 98.8 %reduce-scatter.19.cloned.1.call-done = f32[192,768]{1,0:T(8,128)} async-done(((f32[1536,768]{1,0:T(8,128)}), f32[192,768]{1,0:T(8,128)}) %reduce-scatter.19.cloned.1.call-update) | async-done | bytes 589840 | tf_op jit(solution)/shard_map/reduce_scatter | solution.py:350
  2506.6 121.9 %reduce-scatter.29.cloned.1.call-done = f32[1024,192]{0,1:T(8,128)} async-done(((f32[1024,1536]{0,1:T(8,128)}), f32[1024,192]{0,1:T(8,128)}) %reduce-scatter.29.cloned.1.call-update) | async-done | bytes 786448 | tf_op jit(solution)/shard_map/reduce_scatter | solution.py:363
  2628.5 98.7 %reduce-scatter.17.cloned.1.call-done = f32[192,768]{1,0:T(8,128)} async-done(((f32[1536,768]{1,0:T(8,128)}), f32[192,768]{1,0:T(8,128)}) %reduce-scatter.17.cloned.1.call-update) | async-done | bytes 589840 | tf_op jit(solution)/shard_map/reduce_scatter | solution.py:349
  (1725 shorter events, 964.6 us)
Async XLA Ops:
  7.2 137.8 %copy-start.3 = (bf16[8,128,1536]{2,1,0:T(8,128)(2,1)S(1)}, bf16[8,128,1536]{2,1,0:T(8,128)(2,1)}, u32[]{:S(2)}) copy-start(bf16[8,128,1536]{2,1,0:T(8,128)(2,1)} %param.33) | copy-start | bytes 9437188
  7.2 140.3 %all-gather.14.cloned.1.call-start = ((), (), s32[]{:S(2)}) async-start(), calls=%async_computation.10 | async-start | bytes 2654208 | tf_op jit(solution)/shard_map/all_gather | solution.py:129
  9.2 192.0 %all-reduce.66.cloned.1.call-start = ((), (), s32[]{:S(2)}) async-start(), calls=%async_computation.11 | async-start | bytes 1048576 | tf_op jit(solution)/shard_map/psum | solution.py:180
  10.0 137.4 %collective-permute-start = (s32[8,3]{1,0:T(8,128)S(1)}, s32[8,3]{1,0:T(8,128)S(1)}, u32[]{:S(2)}, u32[]{:S(2)}) collective-permute-start(s32[8,3]{1,0:T(8,128)S(1)} %slice.803), channel_id=1, source_target_pairs={{0,4},{4,8},{8,12},{12,16},{16,20},{20,24},{24,28},{1,5},{5,9},{9,... | collective-permute-start | bytes 296 | tf_op jit(solution)/shard_map/ppermute | solution.py:13
  77.7 129.8 %copy-start.78 = (f32[96]{0:T(128)}, f32[96]{0:T(128)S(1)}, u32[]{:S(2)}) copy-start(f32[96]{0:T(128)S(1)} %slice.819) | copy-start | bytes 1156
  77.8 129.8 %copy-start.72 = (f32[768]{0:T(1024)}, f32[768]{0:T(1024)S(1)}, u32[]{:S(2)}) copy-start(f32[768]{0:T(1024)S(1)} %convert_element_type.176) | copy-start | bytes 9220
  152.8 3.1 collective-permute-start.1
  163.0 365.6 %all-gather.28.cloned.1.call-start = ((), (), s32[]{:S(2)}) async-start(), calls=%async_computation.28 | async-start | bytes 3538944 | tf_op jit(solution)/shard_map/all_gather | solution.py:20
  467.7 122.7 %all-gather.16.cloned.1.call-start = ((), (), s32[]{:S(2)}) async-start(), calls=%async_computation.12 | async-start | bytes 3538944 | tf_op jit(solution)/shard_map/all_gather | solution.py:20
  475.1 175.0 %all-gather.18.cloned.1.call-start = ((), (), s32[]{:S(2)}) async-start(), calls=%async_computation.13 | async-start | bytes 2654208 | tf_op jit(solution)/shard_map/all_gather | solution.py:130
  477.0 219.4 %all-gather.20.cloned.1.call-start = ((), (), s32[]{:S(2)}) async-start(), calls=%async_computation.14 | async-start | bytes 2654208 | tf_op jit(solution)/shard_map/all_gather | solution.py:139
  478.9 343.3 %all-reduce.68.cloned.1.call-start = ((), (), s32[]{:S(2)}) async-start(), calls=%async_computation.15 | async-start | bytes 12582912 | tf_op jit(solution)/shard_map/psum | solution.py:230
  703.9 181.7 %all-gather.22.cloned.1.call-start = ((), (), s32[]{:S(2)}) async-start(), calls=%async_computation.16 | async-start | bytes 3538944 | tf_op jit(solution)/shard_map/all_gather | solution.py:141
  705.9 241.6 %all-gather.24.cloned.1.call-start = ((), (), s32[]{:S(2)}) async-start(), calls=%async_computation.17 | async-start | bytes 3538944 | tf_op jit(solution)/shard_map/all_gather | solution.py:142
  707.9 301.3 %all-gather.26.cloned.1.call-start = ((), (), s32[]{:S(2)}) async-start(), calls=%async_computation.18 | async-start | bytes 3538944 | tf_op jit(solution)/shard_map/all_gather | solution.py:143
  710.1 435.7 %all-reduce.70.cloned.1.call-start = ((), (), s32[]{:S(2)}) async-start(), calls=%async_computation.19 | async-start | bytes 12582912 | tf_op jit(solution)/shard_map/psum | solution.py:251
  892.6 116.6 %copy-start.22 = (bf16[8,128,1536]{2,1,0:T(8,128)(2,1)S(1)}, bf16[8,128,1536]{2,1,0:T(8,128)(2,1)}, u32[]{:S(2)}) copy-start(bf16[8,128,1536]{2,1,0:T(8,128)(2,1)} %param.51) | copy-start | bytes 9437188
  1027.5 247.7 %all-gather.30.cloned.1.call-start = ((), (), s32[]{:S(2)}) async-start(), calls=%async_computation.29 | async-start | bytes 3538944 | tf_op jit(solution)/shard_map/all_gather | solution.py:20
  1198.9 387.6 %all-reduce.72.cloned.1.call-start = ((), (), s32[]{:S(2)}) async-start(), calls=%async_computation.20 | async-start | bytes 1048576 | tf_op jit(solution)/shard_map/psum | solution.py:289
  1556.8 115.8 %reduce-scatter.35.cloned.1.call-start = ((), (), s32[]{:S(2)}) async-start(), calls=%async_computation.32 | async-start | bytes 442368
  1571.4 143.2 %reduce-scatter.31.cloned.1.call-start = ((), (), s32[]{:S(2)}) async-start(), calls=%async_computation.30 | async-start | bytes 442368
  1604.5 6.0 collective-permute-start.2
  1605.8 172.3 %reduce-scatter.33.cloned.1.call-start = ((), (), s32[]{:S(2)}) async-start(), calls=%async_computation.31 | async-start | bytes 442368
  1609.0 391.7 %all-reduce.74.cloned.1.call-start = ((), (), s32[]{:S(2)}) async-start(), calls=%async_computation.33 | async-start | bytes 25165824 | tf_op jit(solution)/shard_map/psum | solution.py:238
  1620.2 445.8 %reduce-scatter.21.cloned.1.call-start = ((), (), s32[]{:S(2)}) async-start(), calls=%async_computation.23 | async-start | bytes 442368 | tf_op jit(solution)/shard_map/reduce_scatter | solution.py:353
  1621.8 542.9 %reduce-scatter.23.cloned.1.call-start = ((), (), s32[]{:S(2)}) async-start(), calls=%async_computation.24 | async-start | bytes 5308416 | tf_op jit(solution)/shard_map/reduce_scatter | solution.py:359
  1630.1 656.4 %reduce-scatter.25.cloned.1.call-start = ((), (), s32[]{:S(2)}) async-start(), calls=%async_computation.25 | async-start | bytes 7077888 | tf_op jit(solution)/shard_map/reduce_scatter | solution.py:361
  1639.0 768.7 %reduce-scatter.27.cloned.1.call-start = ((), (), s32[]{:S(2)}) async-start(), calls=%async_computation.26 | async-start | bytes 7077888 | tf_op jit(solution)/shard_map/reduce_scatter | solution.py:362
  1646.1 860.4 %reduce-scatter.19.cloned.1.call-start = ((), (), s32[]{:S(2)}) async-start(), calls=%async_computation.22 | async-start | bytes 5308416 | tf_op jit(solution)/shard_map/reduce_scatter | solution.py:350
  1653.8 974.7 %reduce-scatter.29.cloned.1.call-start = ((), (), s32[]{:S(2)}) async-start(), calls=%async_computation.27 | async-start | bytes 7077888 | tf_op jit(solution)/shard_map/reduce_scatter | solution.py:363
  1662.7 1064.6 %reduce-scatter.17.cloned.1.call-start = ((), (), s32[]{:S(2)}) async-start(), calls=%async_computation.21 | async-start | bytes 5308416 | tf_op jit(solution)/shard_map/reduce_scatter | solution.py:349
  1670.6 330.0 %copy-start.52 = (f32[1024]{0:T(1024)S(1)}, f32[1024]{0:T(1024)}, u32[]{:S(2)}) copy-start(f32[1024]{0:T(1024)} %copy-done.51) | copy-start | bytes 12292
  (192 other events, 1391.4 us)
Sparse Core Ops, SparseCore 0:
  10.8 55.2 all-gather.13
  163.1 34.7 all-reduce.65
  467.8 60.8 all-gather.27
  531.3 59.0 all-gather.15
  593.0 50.6 all-gather.17
  645.7 50.5 all-gather.19
  704.0 118.1 all-reduce.67
  824.9 60.6 all-gather.21
  888.4 59.0 all-gather.23
  950.1 59.0 all-gather.25
  1027.6 118.1 all-reduce.69
  1199.0 60.6 all-gather.29
  1556.9 29.5 all-reduce.71
  1589.6 61.3 reduce-scatter.34
  1654.1 60.3 reduce-scatter.30
  1717.7 60.3 reduce-scatter.32
  1780.6 220.0 all-reduce.73
  2004.4 61.5 reduce-scatter.20
  2070.2 94.5 reduce-scatter.22
  2168.7 117.6 reduce-scatter.24
  2290.6 117.0 reduce-scatter.26
  2412.0 94.5 reduce-scatter.18
  2510.7 117.7 reduce-scatter.28
  2632.6 94.5 reduce-scatter.16
where the time goes:
time: 2750 us; the launch traced here: 2730 us
  waiting for transfers between devices  1550 us (56%)
  other arithmetic  342 us (12%)
  local copies, waits for them, and re-layouts  324 us (12%)
  matrix products  297 us (11%)
  blocking collectives  183 us (7%)
    psum x1, waiting for transfers between devices, shards(): ffn_out = lax.psum(ffn_term, 'head')  221 us
    dot_general x256, matrix products, block_fn(): jnp.einsum('sen,sn->se', carried, c_blk[offset], precision=HIGH)  165 us
    reduce_scatter x1, waiting for transfers between devices, shards(): lax.psum_scatter(grad_down, 'seq', scatter_dimension=1, tiled=True)  122 us
    reduce_scatter x1, waiting for transfers between devices, shards(): lax.psum_scatter(grad_gate, 'seq', scatter_dimension=0, tiled=True)  122 us
    reduce_scatter x1, waiting for transfers between devices, shards(): lax.psum_scatter(grad_up, 'seq', scatter_dimension=0, tiled=True)  121 us
    psum x1, waiting for transfers between devices, shards(): d_norm2 = lax.psum(norm2_term, 'head')  117 us
    psum x1, waiting for transfers between devices, shards(): hidden = x_rows + lax.psum(mixer_term, 'head')  112 us
    all_gather x3, waiting for transfers between devices, entering(): gathered = jax.tree.map(lambda a: lax.all_gather(a, axis), part)  110 us
  transfers between devices with their start and end apart: 27, of which 21 were waited for; matrix products, arithmetic and copies ran while one was open for 11% of the time, Pallas kernels for 0%

commit v1 on v0

v1 whole, which is shorter than its diff:
```python
import functools

import jax
import jax.numpy as jnp
from jax import lax
from jax.experimental import pallas as pl
from jax.experimental.pallas import tpu as pltpu
from jax.sharding import PartitionSpec as P

EPS = 1e-06
LOG2E = 1.4426950408889634
LN2 = 0.6931471805599453
STOP = 1e30
LANES = 128
BF = jnp.bfloat16
F32 = jnp.float32


def shifted(value, axis, steps):
    count = lax.axis_size(axis)
    initial, last = (max(0, -steps), min(count, count - steps))
    return lax.ppermute(value, axis, [(source, source + steps) for source in range(initial, last)])


def norm_rows(values, gain_vec):
    inv_rms = lax.rsqrt(jnp.mean(values * values, axis=-1, keepdims=True) + EPS)
    return (values * inv_rms * gain_vec, inv_rms)


def norm_back(values, inv_rms, gain_vec, grad_rows):
    normed = values * inv_rms
    gain_grad = jnp.sum(grad_rows * normed, axis=0)
    scaled = grad_rows * gain_vec
    value_grad = inv_rms * (scaled - normed * jnp.mean(scaled * normed, axis=-1, keepdims=True))
    return (value_grad, gain_grad)


def silu_slope(values):
    logistic = jax.nn.sigmoid(values)
    return logistic * (1.0 + values * (1.0 - logistic))


def spread(column_ref, seqs, tokens, first, count, target):
    def one(token, carry):
        block = column_ref[pl.ds(pl.multiple_of(token * seqs, seqs), seqs), :]
        for n in range(count):
            column = block[:, first + n : first + n + 1]
            target[token * count + n] = jnp.broadcast_to(column, (seqs, LANES))
        return carry

    lax.fori_loop(0, tokens, one, 0)


def pair_rows(ref, pair, seqs):
    both = ref[pl.ds(pl.multiple_of(pair * 2 * seqs, 2 * seqs), 2 * seqs), :]
    both = both.astype(F32)
    return both[:seqs], both[seqs:]


def token_rows(ref, token, seqs):
    return ref[pl.ds(pl.multiple_of(token * seqs, seqs), seqs), :]


def end_kernel(seqs, tokens, states, bc_ref, step_ref, u_ref, rate_ref, end_ref, sum_ref, bb, pen):
    @pl.when(pl.program_id(0) == 0)
    def _():
        spread(bc_ref, seqs, tokens, 0, states, bb)
        spread(bc_ref, seqs, tokens, 2 * states, 1, pen)

    def one(pair, carry):
        state, total = carry
        u_pair = pair_rows(u_ref, pair, seqs)
        for half in range(2):
            token = pair * 2 + half
            step = token_rows(step_ref, token, seqs)
            drive = step * u_pair[half]
            stop = step + pen[token]
            total = total + stop
            fresh = []
            for n in range(states):
                decay = jnp.exp2(stop * rate_ref[pl.ds(n * seqs, seqs), :])
                fresh.append(decay * state[n] + drive * bb[token * states + n])
            state = tuple(fresh)
        return state, total

    zero = jnp.zeros((seqs, LANES), F32)
    state, total = lax.fori_loop(0, tokens // 2, one, ((zero,) * states, zero))
    for n in range(states):
        end_ref[pl.ds(n * seqs, seqs), :] = state[n].astype(end_ref.dtype)
    sum_ref[...] = total


def out_kernel(
    seqs, tokens, states, bc_ref, step_ref, u_ref, rate_ref, start_ref, y_ref, bb, cc, pen
):
    @pl.when(pl.program_id(0) == 0)
    def _():
        spread(bc_ref, seqs, tokens, 0, states, bb)
        spread(bc_ref, seqs, tokens, states, states, cc)
        spread(bc_ref, seqs, tokens, 2 * states, 1, pen)

    def one(pair, state):
        u_pair = pair_rows(u_ref, pair, seqs)
        for half in range(2):
            token = pair * 2 + half
            step = token_rows(step_ref, token, seqs)
            drive = step * u_pair[half]
            stop = step + pen[token]
            fresh = []
            out = jnp.zeros((seqs, LANES), F32)
            for n in range(states):
                decay = jnp.exp2(stop * rate_ref[pl.ds(n * seqs, seqs), :])
                value = decay * state[n] + drive * bb[token * states + n]
                out = out + value * cc[token * states + n]
                fresh.append(value)
            y_ref[pl.ds(pl.multiple_of(token * seqs, seqs), seqs), :] = out
            state = tuple(fresh)
        return state

    initial = tuple(start_ref[pl.ds(n * seqs, seqs), :] for n in range(states))
    lax.fori_loop(0, tokens // 2, one, initial)


def own_kernel(seqs, tokens, states, bc_ref, step_ref, dy_ref, rate_ref, own_ref, cc, pen):
    @pl.when(pl.program_id(0) == 0)
    def _():
        spread(bc_ref, seqs, tokens, states, states, cc)
        spread(bc_ref, seqs, tokens, 2 * states, 1, pen)

    def one(back, grads):
        for half in range(2):
            token = tokens - 1 - (back * 2 + half)
            stop = token_rows(step_ref, token, seqs) + pen[token]
            dy = token_rows(dy_ref, token, seqs)
            fresh = []
            for n in range(states):
                decay = jnp.exp2(stop * rate_ref[pl.ds(n * seqs, seqs), :])
                fresh.append(decay * (grads[n] + dy * cc[token * states + n]))
            grads = tuple(fresh)
        return grads

    zero = jnp.zeros((seqs, LANES), F32)
    grads = lax.fori_loop(0, tokens // 2, one, (zero,) * states)
    for n in range(states):
        own_ref[pl.ds(n * seqs, seqs), :] = grads[n].astype(own_ref.dtype)


def back_kernel(
    seqs,
    tokens,
    states,
    bc_ref,
    step_ref,
    u_ref,
    dy_ref,
    rate_ref,
    start_ref,
    last_ref,
    du_ref,
    dstep_ref,
    dbc_ref,
    dlog_ref,
    bb,
    cc,
    pen,
    held,
    acc_b,
    acc_c,
):
    tile = pl.program_id(0)

    @pl.when(tile == 0)
    def _():
        spread(bc_ref, seqs, tokens, 0, states, bb)
        spread(bc_ref, seqs, tokens, states, states, cc)
        spread(bc_ref, seqs, tokens, 2 * states, 1, pen)

        def clear(token, carry):
            for n in range(states):
                acc_b[token * states + n] = jnp.zeros((seqs, LANES), F32)
                acc_c[token * states + n] = jnp.zeros((seqs, LANES), F32)
            return carry

        lax.fori_loop(0, tokens, clear, 0)

    def again(pair, state):
        u_pair = pair_rows(u_ref, pair, seqs)
        for half in range(2):
            token = pair * 2 + half
            step = token_rows(step_ref, token, seqs)
            drive = step * u_pair[half]
            stop = step + pen[token]
            fresh = []
            for n in range(states):
                held[token * states + n] = state[n]
                decay = jnp.exp2(stop * rate_ref[pl.ds(n * seqs, seqs), :])
                fresh.append(decay * state[n] + drive * bb[token * states + n])
            state = tuple(fresh)
        return state

    initial = tuple(start_ref[pl.ds(n * seqs, seqs), :] for n in range(states))
    state = lax.fori_loop(0, tokens // 2, again, initial)
    for n in range(states):
        held[tokens * states + n] = state[n]

    def one(back, carry):
        grads, logs = carry
        pair = tokens // 2 - 1 - back
        u_pair = pair_rows(u_ref, pair, seqs)
        for half in (1, 0):
            token = pair * 2 + half
            step = token_rows(step_ref, token, seqs)
            dy = token_rows(dy_ref, token, seqs)
            u_one = u_pair[half]
            drive = step * u_one
            stop = step + pen[token]
            fresh = []
            fresh_logs = []
            on_b = jnp.zeros((seqs, LANES), F32)
            on_rate = jnp.zeros((seqs, LANES), F32)
            for n in range(states):
                at = token * states + n
                rate = rate_ref[pl.ds(n * seqs, seqs), :]
                decay = jnp.exp2(stop * rate)
                lam = grads[n] + dy * cc[at]
                carried = lam * decay
                fresh.append(carried)
                kept = carried * held[at]
                on_b = on_b + lam * bb[at]
                on_rate = on_rate + kept * rate
                fresh_logs.append(logs[n] + kept * step)
                acc_b[at] = acc_b[at] + lam * drive
                acc_c[at] = acc_c[at] + dy * held[at + states]
            rows = pl.ds(pl.multiple_of(token * seqs, seqs), seqs)
            du_ref[rows, :] = step * on_b
            dstep_ref[rows, :] = on_rate * LN2 + u_one * on_b
            grads = tuple(fresh)
            logs = tuple(fresh_logs)
        return grads, logs

    zero = jnp.zeros((seqs, LANES), F32)
    grads = tuple(last_ref[pl.ds(n * seqs, seqs), :] for n in range(states))
    grads, logs = lax.fori_loop(0, tokens // 2, one, (grads, (zero,) * states))
    for n in range(states):
        dlog_ref[pl.ds(n, 1), :] = jnp.sum(logs[n], axis=0, keepdims=True)

    @pl.when(tile == pl.num_programs(0) - 1)
    def _():
        lane = lax.broadcasted_iota(jnp.int32, (seqs, LANES), 1)

        def gather(token, carry):
            block = jnp.zeros((seqs, LANES), F32)
            for n in range(states):
                sum_b = jnp.sum(acc_b[token * states + n], axis=1, keepdims=True)
                block = jnp.where(lane == n, sum_b, block)
                sum_c = jnp.sum(acc_c[token * states + n], axis=1, keepdims=True)
                block = jnp.where(lane == states + n, sum_c, block)
            dbc_ref[pl.ds(pl.multiple_of(token * seqs, seqs), seqs), :] = block
            return carry

        lax.fori_loop(0, tokens, gather, 0)


def state_call(body, seqs, tokens, states, channels, ins, outs, scratch, cost):
    def spec(shape, shared):
        if shared:
            return pl.BlockSpec(shape, lambda tile: (0, 0))
        return pl.BlockSpec((shape[0], LANES), lambda tile: (0, tile))

    return pl.pallas_call(
        functools.partial(body, seqs, tokens, states),
        grid=(channels // LANES,),
        in_specs=[spec(value.shape, shared) for value, shared in ins],
        out_specs=tuple(spec(value.shape, shared) for value, shared in outs),
        out_shape=tuple(value for value, _ in outs),
        scratch_shapes=[pltpu.VMEM((count, seqs, LANES), F32) for count in scratch],
        compiler_params=pltpu.CompilerParams(vmem_limit_bytes=58 * 1024 * 1024),
        cost_estimate=pl.CostEstimate(flops=cost, bytes_accessed=16 * 1024 * 1024, transcendentals=0),
    )(*[value for value, _ in ins])


def shards(
    x_in,
    seg_ids,
    norm1_gain,
    w_in_x,
    w_in_z,
    conv_w,
    conv_b,
    w_xproj,
    ssm_gain,
    w_dt,
    dt_bias,
    a_log,
    d_skip,
    w_out,
    norm2_gain,
    w_gate,
    w_up,
    w_down,
    d_out,
):
    gathered = lambda value, axis: lax.all_gather(value.astype(BF), "seq", axis=axis, tiled=True)
    full_norm1 = gathered(norm1_gain, 0)
    full_in_x = gathered(w_in_x, 0)
    full_in_z = gathered(w_in_z, 0)
    full_conv_w = gathered(conv_w, 1)
    full_conv_b = gathered(conv_b, 0)
    full_xproj = gathered(w_xproj, 0)
    full_ssm_gain = gathered(ssm_gain, 0)
    full_w_dt = gathered(w_dt, 1)
    full_dt_bias = gathered(dt_bias, 0)
    full_a_log = gathered(a_log, 0)
    full_d_skip = gathered(d_skip, 0)
    full_w_out = gathered(w_out, 1)
    full_norm2 = gathered(norm2_gain, 0)
    full_gate = gathered(w_gate, 0)
    full_up = gathered(w_up, 0)
    full_down = gathered(w_down, 1)
    count = lax.axis_size("seq")
    place = lax.axis_index("seq")
    seqs, tokens, width = x_in.shape
    rows = seqs * tokens
    taps = full_conv_w.shape[0]
    rank = full_w_dt.shape[0]
    states = full_a_log.shape[1]
    channels = full_in_x.shape[1]
    halo = (taps - 1) * seqs
    head_sum = lambda value: lax.psum(value.astype(BF), "head").astype(F32)

    norm1_vec = full_norm1.astype(F32)
    x_rows = x_in.transpose(1, 0, 2).reshape(rows, width).astype(F32)
    ids = seg_ids.T.reshape(rows)
    normed1, scale_one = norm_rows(x_rows, norm1_vec)
    x_norm = normed1.astype(BF)
    x_inner = jnp.dot(x_norm, full_in_x, preferred_element_type=F32).astype(BF)
    z_gate = jnp.dot(x_norm, full_in_z, preferred_element_type=F32)
    prev_tail, prev_ids = shifted((x_inner[rows - halo :], ids[rows - halo :]), "seq", 1)
    extended = jnp.concatenate([prev_tail, x_inner], axis=0).astype(F32)
    ext_ids = jnp.concatenate([prev_ids, ids])
    conv_weight = full_conv_w.astype(F32)
    x_conv = full_conv_b.astype(F32)[None, :]
    same_docs = []
    for offset in range(taps):
        first = (taps - 1 - offset) * seqs
        same = (ext_ids[first : first + rows] == ids).astype(F32)[:, None]
        same_docs.append(same)
        x_conv = x_conv + conv_weight[offset] * extended[first : first + rows] * same
    u_low = jax.nn.silu(x_conv).astype(BF)
    projected = head_sum(jnp.dot(u_low, full_xproj, preferred_element_type=F32))
    ssm_vec = full_ssm_gain.astype(F32)
    b_end = rank + states
    dt_normed, dt_scale = norm_rows(projected[:, :rank], ssm_vec[:rank])
    b_normed, b_scale = norm_rows(projected[:, rank:b_end], ssm_vec[rank:b_end])
    c_normed, c_scale = norm_rows(projected[:, b_end:], ssm_vec[b_end:])
    dt_low = dt_normed.astype(BF)
    dt_pre = jnp.dot(dt_low, full_w_dt, preferred_element_type=F32) + full_dt_bias.astype(F32)
    step = jax.nn.softplus(dt_pre)
    rates = -jnp.exp(full_a_log.astype(F32))
    rate_rows = jnp.repeat((rates * LOG2E).T, seqs, axis=0)
    pen = (1.0 - same_docs[1]) * STOP
    bc = jnp.concatenate(
        [b_normed, c_normed, pen, jnp.zeros((rows, LANES - 2 * states - 1), F32)], axis=1
    )
    run = lambda body, ins, outs, scratch, ops: state_call(
        body, seqs, tokens, states, channels, ins, outs, scratch, ops * rows * channels * states
    )
    shape = jax.ShapeDtypeStruct
    per_token = tokens * states
    state_rows = states * seqs
    local_end, step_sum = run(
        end_kernel,
        [(bc, True), (step, False), (u_low, False), (rate_rows, False)],
        [(shape((state_rows, channels), BF), False), (shape((seqs, channels), F32), False)],
        [per_token, tokens],
        6,
    )
    all_ends = lax.all_gather(local_end, "seq")
    all_sums = lax.all_gather(step_sum, "seq")

    def passed(sum_one):
        whole = sum_one[None] * (rates * LOG2E).T[:, None, :]
        return jnp.exp2(whole).reshape(state_rows, channels)

    start = jnp.zeros((state_rows, channels), F32)
    for source in range(count - 1):
        moved = start * passed(all_sums[source]) + all_ends[source].astype(F32)
        start = jnp.where(source < place, moved, start)
    (y_state,) = run(
        out_kernel,
        [(bc, True), (step, False), (u_low, False), (rate_rows, False), (start, False)],
        [(shape((rows, channels), F32), False)],
        [per_token, per_token, tokens],
        8,
    )
    skip_vec = full_d_skip.astype(F32)
    u_rows = u_low.astype(F32)
    y_full = y_state + skip_vec * u_rows
    silu_z = jax.nn.silu(z_gate)
    g_low = (y_full * silu_z).astype(BF)
    norm2_vec = full_norm2.astype(F32)
    hidden = x_rows + head_sum(jnp.dot(g_low, full_w_out, preferred_element_type=F32))
    normed2, scale_two = norm_rows(hidden, norm2_vec)
    x_norm2 = normed2.astype(BF)
    gate_proj = jnp.dot(x_norm2, full_gate, preferred_element_type=F32)
    up_proj = jnp.dot(x_norm2, full_up, preferred_element_type=F32)
    silu_gate = jax.nn.silu(gate_proj)
    act_low = (silu_gate * up_proj).astype(BF)
    ffn_out = head_sum(jnp.dot(act_low, full_down, preferred_element_type=F32))
    block_out = (hidden + ffn_out).astype(BF).reshape(tokens, seqs, width).transpose(1, 0, 2)
    grad_low = d_out.transpose(1, 0, 2).reshape(rows, width)
    grad_rows = grad_low.astype(F32)
    grad_down = jnp.einsum("rf,rd->fd", act_low, grad_low, preferred_element_type=F32)
    d_act = jnp.einsum("rd,fd->rf", grad_low, full_down, preferred_element_type=F32)
    d_gate = (d_act * up_proj * silu_slope(gate_proj)).astype(BF)
    d_up = (d_act * silu_gate).astype(BF)
    grad_gate = jnp.einsum("rd,rf->df", x_norm2, d_gate, preferred_element_type=F32)
    grad_up = jnp.einsum("rd,rf->df", x_norm2, d_up, preferred_element_type=F32)
    d_norm2 = head_sum(
        jnp.einsum("rf,df->rd", d_gate, full_gate, preferred_element_type=F32)
        + jnp.einsum("rf,df->rd", d_up, full_up, preferred_element_type=F32)
    )
    d_hidden_part, grad_norm2 = norm_back(hidden, scale_two, norm2_vec, d_norm2)
    d_hidden = grad_rows + d_hidden_part
    d_mix = d_hidden.astype(BF)
    grad_out_w = jnp.einsum("re,rd->ed", g_low, d_mix, preferred_element_type=F32)
    d_g = jnp.einsum("rd,ed->re", d_mix, full_w_out, preferred_element_type=F32)
    d_y = d_g * silu_z
    d_z = (d_g * y_full * silu_slope(z_gate)).astype(BF)
    grad_skip = jnp.sum(d_y * u_rows, axis=0)
    (own,) = run(
        own_kernel,
        [(bc, True), (step, False), (d_y, False), (rate_rows, False)],
        [(shape((state_rows, channels), BF), False)],
        [per_token, tokens],
        6,
    )
    all_own = lax.all_gather(own, "seq")
    last = jnp.zeros((state_rows, channels), F32)
    for source in range(count - 1, 0, -1):
        moved = last * passed(all_sums[source]) + all_own[source].astype(F32)
        last = jnp.where(source > place, moved, last)
    d_u_state, d_step, d_bc, d_log = run(
        back_kernel,
        [
            (bc, True),
            (step, False),
            (u_low, False),
            (d_y, False),
            (rate_rows, False),
            (start, False),
            (last, False),
        ],
        [
            (shape((rows, channels), F32), False),
            (shape((rows, channels), F32), False),
            (shape((rows, LANES), F32), True),
            (shape((states, channels), F32), False),
        ],
        [per_token, per_token, tokens, per_token + states, per_token, per_token],
        24,
    )
    grad_alog = d_log.T * rates
    d_pre = d_step * jax.nn.sigmoid(dt_pre)
    grad_bias = jnp.sum(d_pre, axis=0)
    d_pre_low = d_pre.astype(BF)
    grad_step_w = jnp.einsum("rk,re->ke", dt_low, d_pre_low, preferred_element_type=F32)
    d_dt_part = jnp.einsum("re,ke->rk", d_pre_low, full_w_dt, preferred_element_type=F32)
    d_stats = head_sum(jnp.concatenate([d_dt_part, d_bc[:, : 2 * states]], axis=1))
    d_dt_raw, grad_dt_gain = norm_back(
        projected[:, :rank], dt_scale, ssm_vec[:rank], d_stats[:, :rank]
    )
    d_b_raw, grad_b_gain = norm_back(
        projected[:, rank:b_end], b_scale, ssm_vec[rank:b_end], d_stats[:, rank:b_end]
    )
    d_c_raw, grad_c_gain = norm_back(
        projected[:, b_end:], c_scale, ssm_vec[b_end:], d_stats[:, b_end:]
    )
    d_proj = jnp.concatenate([d_dt_raw, d_b_raw, d_c_raw], axis=1)
    grad_ssm = jnp.concatenate([grad_dt_gain, grad_b_gain, grad_c_gain])
    grad_xproj = jnp.einsum("re,rk->ek", u_low, d_proj, preferred_element_type=F32)
    d_u = (
        d_y * skip_vec
        + d_u_state
        + jnp.einsum("rk,ek->re", d_proj, full_xproj, preferred_element_type=F32)
    )
    d_conv = d_u * silu_slope(x_conv)
    grad_conv_b = jnp.sum(d_conv, axis=0)
    d_extended = jnp.zeros((rows + halo, channels), F32)
    conv_grads = []
    for offset in range(taps):
        first = (taps - 1 - offset) * seqs
        masked = d_conv * same_docs[offset]
        conv_grads.append(jnp.sum(masked * extended[first : first + rows], axis=0))
        d_extended = d_extended + jnp.pad(
            conv_weight[offset] * masked, ((first, halo - first), (0, 0))
        )
    grad_conv_w = jnp.stack(conv_grads)
    from_next = shifted(d_extended[:halo].astype(BF), "seq", -1).astype(F32)
    d_inner = d_extended[halo:] + jnp.pad(from_next, ((rows - halo, 0), (0, 0)))
    d_inner_low = d_inner.astype(BF)
    grad_in_x = jnp.einsum("rd,re->de", x_norm, d_inner_low, preferred_element_type=F32)
    grad_in_z = jnp.einsum("rd,re->de", x_norm, d_z, preferred_element_type=F32)
    d_norm1 = head_sum(
        jnp.einsum("re,de->rd", d_inner_low, full_in_x, preferred_element_type=F32)
        + jnp.einsum("re,de->rd", d_z, full_in_z, preferred_element_type=F32)
    )
    d_input_part, grad_norm1 = norm_back(x_rows, scale_one, norm1_vec, d_norm1)
    grad_input = (d_hidden + d_input_part).reshape(tokens, seqs, width).transpose(1, 0, 2)
    scattered = lambda value, axis: lax.psum_scatter(
        value, "seq", scatter_dimension=axis, tiled=True
    )
    shrunk = lambda value, axis: scattered(value.astype(BF), axis).astype(F32)
    return (
        block_out,
        grad_input,
        scattered(grad_norm1, 0),
        shrunk(grad_in_x, 0),
        shrunk(grad_in_z, 0),
        scattered(grad_conv_w, 1),
        scattered(grad_conv_b, 0),
        shrunk(grad_xproj, 0),
        scattered(grad_ssm, 0),
        shrunk(grad_step_w, 1),
        scattered(grad_bias, 0),
        scattered(grad_alog, 0),
        scattered(grad_skip, 0),
        shrunk(grad_out_w, 1),
        scattered(grad_norm2, 0),
        shrunk(grad_gate, 0),
        shrunk(grad_up, 0),
        shrunk(grad_down, 1),
    )


def solution(mesh):
    placed = (
        P(None, "seq", None),
        P(None, "seq"),
        P("seq"),
        P("seq", "head"),
        P("seq", "head"),
        P(None, ("head", "seq")),
        P(("head", "seq")),
        P(("head", "seq"), None),
        P("seq"),
        P(None, ("head", "seq")),
        P(("head", "seq")),
        P(("head", "seq"), None),
        P(("head", "seq")),
        P("head", "seq"),
        P("seq"),
        P("seq", "head"),
        P("seq", "head"),
        P("head", "seq"),
        P(None, "seq", None),
    )
    return jax.shard_map(
        shards,
        mesh=mesh,
        in_specs=placed,
        out_specs=(
            P(None, "seq", None),
            P(None, "seq", None),
            P("seq"),
            P("seq", "head"),
            P("seq", "head"),
            P(None, ("head", "seq")),
            P(("head", "seq")),
            P(("head", "seq"), None),
            P("seq"),
            P(None, ("head", "seq")),
            P(("head", "seq")),
            P(("head", "seq"), None),
            P(("head", "seq")),
            P("head", "seq"),
            P("seq"),
            P("seq", "head"),
            P("seq", "head"),
            P("head", "seq"),
        ),
        check_vma=False,
    )
```

time: 2750 us -> 1830 us (0.67)
  waiting for transfers between devices: 1550 us -> 1080 us
  local copies, waits for them, and re-layouts: 324 us -> 38.3 us
  other arithmetic: 342 us -> 103 us
  Pallas kernels: 0 us -> 219 us
  matrix products: 297 us -> 134 us
  blocking collectives: 183 us -> 215 us
    reduce_scatter x7, waiting for transfers between devices: 669 us -> 430 us  [shards(): lax.psum_scatter(value, 'seq', scatter_dimension=axis, tiled=True)]
    pallas_call x0 -> x4, Pallas kernels: none -> 219 us  [state_call(): pl.pallas_call(functools.partial(body, seqs, tokens, states), grid=(chann...]
    psum x5, waiting for transfers between devices: 466 us -> 279 us  [shards(): head_sum = lambda value: lax.psum(value.astype(BF), 'head').astype(F32)]
    dot_general x280 -> x24, matrix products: 294 us -> 134 us  [the longest x1 12.1 us: shards(): jnp.einsum('rd,fd->rf', grad_low, full_down, preferred_element_type=F32)]
    mul x176 -> x1, local copies, waits for them, and re-layouts: 109 us -> 0.22 us  [shards(): pen = (1.0 - same_docs[1]) * STOP]
    add x42 -> x1, other arithmetic: 81.3 us -> 0.81 us  [shards(): d_extended + jnp.pad(conv_weight[offset] * masked, ((first, halo - first)...]
    reduce_sum x65 -> x0, other arithmetic: 70.7 us -> none  [the longest x48 47 us: block_fn(): (step_blk[offset] * u_blk[offset])[:, :, None] * b_blk[offset][:, None, :]]
    squeeze x136 -> x0, local copies, waits for them, and re-layouts: 69.3 us -> none  [the longest x80 61.1 us: state_run(): lax.scan(jax.checkpoint(block_fn), initial, block_items)]
  transfers between devices with their start and end apart: 27 -> 26, of which waited for: 21 -> 22; matrix products, arithmetic and copies ran while one was open for 11% -> 10% of each run, Pallas kernels for 0% -> 3%
where the time goes in v1:
time: 1830 us; the launch traced here: 1820 us
  waiting for transfers between devices  1080 us (59%)
  Pallas kernels  219 us (12%)
  blocking collectives  215 us (12%)
  matrix products  134 us (7%)
  other arithmetic  103 us (6%)
  local copies, waits for them, and re-layouts  38.3 us (2%)
  between operations  19.7 us (1%)
    reduce_scatter x7, waiting for transfers between devices, shards(): lax.psum_scatter(value, 'seq', scatter_dimension=axis, tiled=True)  430 us
    psum x5, waiting for transfers between devices, shards(): head_sum = lambda value: lax.psum(value.astype(BF), 'head').astype(F32)  279 us
    pallas_call x4, Pallas kernels, state_call(): pl.pallas_call(functools.partial(body, seqs, tokens, states), grid=(chann...  219 us
    all_gather x6, waiting for transfers between devices, shards(): lax.all_gather(value.astype(BF), 'seq', axis=axis, tiled=True)  203 us
    all_gather x4, blocking collectives, shards(): lax.all_gather(value.astype(BF), 'seq', axis=axis, tiled=True)  109 us
    unnamed x26, waiting for transfers between devices  108 us
    unnamed x2, blocking collectives  74.1 us
    all_gather x1, waiting for transfers between devices, shards(): all_own = lax.all_gather(own, 'seq')  44.4 us
  transfers between devices with their start and end apart: 26, of which 22 were waited for; matrix products, arithmetic and copies ran while one was open for 10% of the time, Pallas kernels for 3%

profile of v1, /device:TPU:0, one launch (start us, length us, event | category | flops | bytes accessed | tf_op | source)
XLA Modules:
  0.0 1817.2 jit_solution(4671532923873383775)
XLA Ops:
  25.5 36.0 %all-reduce.18 = (bf16[1536]{0:T(1024)(128)(2,1)S(1)}, bf16[768]{0:T(1024)(128)(2,1)S(1)}, bf16[128]{0:T(256)(128)(2,1)}, bf16[768]{0:T(1024)(128)(2,1)}, bf16[7...) all-reduce(bf16[1536]{0:T(1024)(128)(2,1)S(1)} %dynamic-update-slice.1, ...), channel_id=1, replica_groups=mesh['seq'=8,'head'=4] {'seq'}, use_global_device_ids=true, to_apply=%add.6 | all-reduce | flops 5504 | bytes 22016
  64.9 16.3 all-gather.3
  81.3 30.4 %all-gather.4 = bf16[8,96,16]{1,2,0:T(8,128)(2,1)S(1)} all-gather(bf16[1,96,16]{1,2,0:T(8,128)(2,1)S(1)} %convert_bitcast_fusion.1), channel_id=1, replica_groups=mesh['seq'=8,'head'=4] {'seq'}, dimensions={0}, use_global_device_ids=true | all-gather | bytes 27648 | tf_op jit(solution)/shard_map/all_gather | solution.py:303
  111.9 30.6 %all_gather.70 = bf16[768,128]{1,0:T(8,128)(2,1)S(1)} all-gather(bf16[96,128]{1,0:T(8,128)(2,1)S(1)} %convert_element_type.341), channel_id=1, replica_groups=mesh['seq'=8,'head'=4] {'seq'}, dimensions={0}, use_global_device_ids=true | all-gather | bytes 221184 | tf_op jit(solution)/shard_map/all_gather | solution.py:303
  165.1 31.9 %all_gather.72 = bf16[96,768]{0,1:T(8,128)(2,1)S(1)} all-gather(bf16[96,96]{0,1:T(8,128)(2,1)S(1)} %copy.74), channel_id=1, replica_groups=mesh['seq'=8,'head'=4] {'seq'}, dimensions={1}, use_global_device_ids=true | all-gather | bytes 165888 | tf_op jit(solution)/shard_map/all_gather | solution.py:303
  206.7 34.7 %shard_map.322 = (bf16[128,768]{1,0:T(8,128)(2,1)}, f32[8,768]{1,0:T(8,128)}) custom-call(f32[1024,128]{1,0:T(8,128)} %maximum_maximum_fusion.bc_ref, f32[1024,768]{1,0:T(8,128)} %get-tuple-element.103.step_ref, bf16[1024,768]{1,0:T(8,128)(2,1)} %copy-done.4, f32[128,768]{1,0:T(8,128)} %broadcast_bitcast_fusion.rate_ref), custom_call_target="tpu_custom_call" | custom-call | flops 75497472 | bytes 16777216 | tf_op jit(solution)/shard_map/pallas_call | solution.py:270
  243.2 31.3 %all-gather = f32[64,768]{1,0:T(8,128)S(1)} all-gather(f32[8,768]{1,0:T(8,128)} %get-tuple-element.24), channel_id=2, replica_groups=mesh['seq'=8,'head'=4] {'seq'}, dimensions={0}, use_global_device_ids=true | all-gather | bytes 221184 | tf_op jit(solution)/shard_map/all_gather | solution.py:379
  275.1 10.8 all-gather.26.cloned.1.call-done
  288.8 52.1 %shard_map.323 = f32[1024,768]{1,0:T(8,128)} custom-call(f32[1024,128]{1,0:T(8,128)} %maximum_maximum_fusion.bc_ref, f32[1024,768]{1,0:T(8,128)} %get-tuple-element.103.step_ref, bf16[1024,768]{1,0:T(8,128)(2,1)} %copy-done.4, f32[128,768]{1,0:T(8,128)} %broadcast_bitcast_fusion.rate_ref, f32[128,768]{1,0:T(8,128)} %fusion.56.start_ref), custom_call_target="tpu_custom_call" | custom-call | flops 100663296 | bytes 16777216 | tf_op jit(solution)/shard_map/pallas_call | solution.py:270
  349.6 43.9 %all-gather.18.cloned.1.call-done = bf16[768,1536]{0,1:T(8,128)(2,1)} async-done(((bf16[768,192]{0,1:T(8,128)(2,1)}), bf16[768,1536]{0,1:T(8,128)(2,1)}) %all-gather.18.cloned.1.call-update) | async-done | bytes 2359312 | tf_op jit(solution)/shard_map/all_gather | solution.py:303
  406.5 60.6 %all-reduce.28.cloned.1.call-done = bf16[1024,1536]{1,0:T(8,128)(2,1)} async-done(((bf16[1024,1536]{1,0:T(8,128)(2,1)}), bf16[1024,1536]{1,0:T(8,128)(2,1)}) %all-reduce.28.cloned.1.call-update) | async-done | bytes 3145744 | tf_op jit(solution)/shard_map/psum | solution.py:329
  479.4 51.2 %all-gather.20.cloned.1.call-done = bf16[1536,1024]{1,0:T(8,128)(2,1)} async-done(((bf16[192,1024]{1,0:T(8,128)(2,1)}), bf16[1536,1024]{1,0:T(8,128)(2,1)}) %all-gather.20.cloned.1.call-update) | async-done | bytes 3145744 | tf_op jit(solution)/shard_map/all_gather | solution.py:303
  538.8 53.9 %all-gather.22.cloned.1.call-done = bf16[1536,1024]{1,0:T(8,128)(2,1)} async-done(((bf16[192,1024]{1,0:T(8,128)(2,1)}), bf16[1536,1024]{1,0:T(8,128)(2,1)}) %all-gather.22.cloned.1.call-update) | async-done | bytes 3145744 | tf_op jit(solution)/shard_map/all_gather | solution.py:303
  601.0 53.8 %all-gather.24.cloned.1.call-done = bf16[1024,1536]{0,1:T(8,128)(2,1)} async-done(((bf16[1024,192]{0,1:T(8,128)(2,1)}), bf16[1024,1536]{0,1:T(8,128)(2,1)}) %all-gather.24.cloned.1.call-update) | async-done | bytes 3145744 | tf_op jit(solution)/shard_map/all_gather | solution.py:303
  654.8 12.1 multiply_convert_fusion.2
  675.5 67.2 %all-reduce.30.cloned.1.call-done = bf16[1024,1536]{1,0:T(8,128)(2,1)} async-done(((bf16[1024,1536]{1,0:T(8,128)(2,1)}), bf16[1024,1536]{1,0:T(8,128)(2,1)}) %all-reduce.30.cloned.1.call-update) | async-done | bytes 3145744 | tf_op jit(solution)/shard_map/psum | solution.py:329
  748.2 10.6 fusion.10
  764.9 35.1 %shard_map.324 = bf16[128,768]{1,0:T(8,128)(2,1)} custom-call(f32[1024,128]{1,0:T(8,128)} %maximum_maximum_fusion.bc_ref, f32[1024,768]{1,0:T(8,128)} %get-tuple-element.103.step_ref, f32[1024,768]{1,0:T(8,128)} %get-tuple-element.68.dy_ref, f32[128,768]{1,0:T(8,128)} %broadcast_bitcast_fusion.rate_ref), custom_call_target="tpu_custom_call" | custom-call | flops 75497472 | bytes 16777216 | tf_op jit(solution)/shard_map/pallas_call | solution.py:270
  800.1 44.4 %all-gather.28.cloned.1.call-done = bf16[1024,768]{1,0:T(8,128)(2,1)} async-done(((bf16[128,768]{1,0:T(8,128)(2,1)}), bf16[1024,768]{1,0:T(8,128)(2,1)}) %all-gather.28.cloned.1.call-update) | async-done | bytes 1572880 | tf_op jit(solution)/shard_map/all_gather | solution.py:438
  847.4 97.3 %shard_map.325 = (f32[1024,768]{1,0:T(8,128)}, f32[1024,768]{1,0:T(8,128)}, f32[1024,128]{1,0:T(8,128)}, f32[16,768]{1,0:T(8,128)}) custom-call(f32[1024,128]{1,0:T(8,128)} %maximum_maximum_fusion.bc_ref, f32[1024,768]{1,0:T(8,128)} %get-tuple-element.103.step_ref, bf16[1024,768]{1,0:T(8,128)(2,1)} %copy-done.4, f32[1024,768]{1,0:T(8,128)} %get-tuple-element.68.dy_ref, ...), custom_call_target="tpu_custom_call" | custom-call | flops 301989888 | bytes 16777216 | tf_op jit(solution)/shard_map/pallas_call | solution.py:270
  952.8 29.5 %all-reduce.32.cloned.1.call-done = bf16[1024,128]{1,0:T(8,128)(2,1)} async-done(((bf16[1024,128]{1,0:T(8,128)(2,1)}), bf16[1024,128]{1,0:T(8,128)(2,1)}) %all-reduce.32.cloned.1.call-update) | async-done | bytes 262160 | tf_op jit(solution)/shard_map/psum | solution.py:329
  1066.5 45.2 %reduce-scatter.31.cloned.1.call-done = f32[96,4]{1,0:T(8,128)} async-done(((f32[768,4]{1,0:T(8,128)}), f32[96,4]{1,0:T(8,128)}) %reduce-scatter.31.cloned.1.call-update) | async-done | bytes 1552
  1113.1 62.3 %reduce-scatter.33.cloned.1.call-done = bf16[96,96]{1,0:T(8,128)(2,1)} async-done(((bf16[768,96]{1,0:T(8,128)(2,1)}), bf16[96,96]{1,0:T(8,128)(2,1)}) %reduce-scatter.33.cloned.1.call-update) | async-done | bytes 18448
  1176.9 62.4 %reduce-scatter.21.cloned.1.call-done = bf16[96,128]{1,0:T(8,128)(2,1)} async-done(((bf16[768,128]{1,0:T(8,128)(2,1)}), bf16[96,128]{1,0:T(8,128)(2,1)}) %reduce-scatter.21.cloned.1.call-update) | async-done | bytes 24592 | tf_op jit(solution)/shard_map/reduce_scatter | solution.py:510
  1240.6 70.3 %reduce-scatter.23.cloned.1.call-done = bf16[768,192]{0,1:T(8,128)(2,1)} async-done(((bf16[768,1536]{0,1:T(8,128)(2,1)}), bf16[768,192]{0,1:T(8,128)(2,1)}) %reduce-scatter.23.cloned.1.call-update) | async-done | bytes 294928 | tf_op jit(solution)/shard_map/reduce_scatter | solution.py:510
  1312.7 74.9 %reduce-scatter.25.cloned.1.call-done = bf16[192,1024]{1,0:T(8,128)(2,1)} async-done(((bf16[1536,1024]{1,0:T(8,128)(2,1)}), bf16[192,1024]{1,0:T(8,128)(2,1)}) %reduce-scatter.25.cloned.1.call-update) | async-done | bytes 393232 | tf_op jit(solution)/shard_map/reduce_scatter | solution.py:510
  1389.6 75.2 %reduce-scatter.27.cloned.1.call-done = bf16[192,1024]{1,0:T(8,128)(2,1)} async-done(((bf16[1536,1024]{1,0:T(8,128)(2,1)}), bf16[192,1024]{1,0:T(8,128)(2,1)}) %reduce-scatter.27.cloned.1.call-update) | async-done | bytes 393232 | tf_op jit(solution)/shard_map/reduce_scatter | solution.py:510
  1466.7 69.6 %reduce-scatter.19.cloned.1.call-done = bf16[192,768]{1,0:T(8,128)(2,1)} async-done(((bf16[1536,768]{1,0:T(8,128)(2,1)}), bf16[192,768]{1,0:T(8,128)(2,1)}) %reduce-scatter.19.cloned.1.call-update) | async-done | bytes 294928 | tf_op jit(solution)/shard_map/reduce_scatter | solution.py:510
  1538.1 75.3 %reduce-scatter.29.cloned.1.call-done = bf16[1024,192]{0,1:T(8,128)(2,1)} async-done(((bf16[1024,1536]{0,1:T(8,128)(2,1)}), bf16[1024,192]{0,1:T(8,128)(2,1)}) %reduce-scatter.29.cloned.1.call-update) | async-done | bytes 393232 | tf_op jit(solution)/shard_map/reduce_scatter | solution.py:510
  1615.3 120.0 %all-reduce.34.cloned.1.call-done = (bf16[1024,1536]{1,0:T(8,128)(2,1)}, bf16[1024,1536]{1,0:T(8,128)(2,1)}) async-done(((bf16[1024,1536]{1,0:T(8,128)(2,1)}, bf16[1024,1536]{1,0:T(8,128)(2,1)}), (bf16[1024,1536]{1,0:T(8,128)(2,1)}, bf16[1024,1536]{1,0:T(8,128)(2,1)})) %all-reduce.34.cloned.1.call-update) | async-done | bytes 6291472 | tf_op jit(solution)/shard_map/psum | solution.py:329
  1744.3 38.1 %all-reduce.17 = (f32[1536]{0:T(1024)S(1)}, f32[768]{0:T(1024)S(1)}, f32[128]{0:T(128)S(1)}, f32[768]{0:T(1024)S(1)}, f32[768]{0:T(1024)S(1)}, /*index=5*/f32[1536]{0:T(1024)S(1)}) all-reduce(f32[1536]{0:T(1024)S(1)} %get-tuple-element.32, f32[768]{0:T(1024)S(1)} %get-tuple-element.38, ...), channel_id=5, replica_groups=mesh['seq'=8,'head'=4] {'seq'}, use_global_device_ids=true, to_apply=%region_17.18.clone | all-reduce | flops 5504 | bytes 44032
  1785.5 9.5 fusion.7
  (359 shorter events, 261.3 us)
Async XLA Ops:
  7.2 136.2 %copy-start.10 = (bf16[8,128,1536]{2,1,0:T(8,128)(2,1)S(1)}, bf16[8,128,1536]{2,1,0:T(8,128)(2,1)}, u32[]{:S(2)}) copy-start(bf16[8,128,1536]{2,1,0:T(8,128)(2,1)} %param.19) | copy-start | bytes 9437188
  7.2 144.8 %all-gather.14.cloned.1.call-start = ((), (), s32[]{:S(2)}) async-start(), calls=%async_computation.10 | async-start | bytes 2654208 | tf_op jit(solution)/shard_map/all_gather | solution.py:303
  9.3 189.4 %all-reduce.26.cloned.1.call-start = ((), (), s32[]{:S(2)}) async-start(), calls=%async_computation.11 | async-start | bytes 524288 | tf_op jit(solution)/shard_map/psum | solution.py:329
  10.8 140.5 %collective-permute-start.1 = (s32[24]{0:T(128)}, s32[24]{0:T(128)}, u32[]{:S(2)}, u32[]{:S(2)}) collective-permute-start(s32[24]{0:T(128)} %slice.172), channel_id=1, source_target_pairs={{0,4},{4,8},{8,12},{12,16},{16,20},{20,24},{24,28},{1,5},{5,9},{9,... | collective-permute-start | bytes 296 | tf_op jit(solution)/shard_map/ppermute | solution.py:22
  61.5 82.7 %copy-start.26 = (f32[1536]{0:T(1024)}, f32[1536]{0:T(1024)S(1)}, u32[]{:S(2)}) copy-start(f32[1536]{0:T(1024)S(1)} %convert_element_type.332) | copy-start | bytes 18436
  64.3 79.9 %copy-start.29 = (f32[1024]{0:T(1024)}, f32[1024]{0:T(1024)S(1)}, u32[]{:S(2)}) copy-start(f32[1024]{0:T(1024)S(1)} %rsqrt.44) | copy-start | bytes 12292
  156.5 2.9 collective-permute-start
  164.8 121.2 %all-gather.26.cloned.1.call-start = ((), (), s32[]{:S(2)}) async-start(), calls=%async_computation.27 | async-start | bytes 1769472 | tf_op jit(solution)/shard_map/all_gather | solution.py:378
  241.5 99.4 %all-gather.16.cloned.1.call-start = ((), (), s32[]{:S(2)}) async-start(), calls=%async_computation.12 | async-start | bytes 2654208 | tf_op jit(solution)/shard_map/all_gather | solution.py:303
  242.3 151.2 %all-gather.18.cloned.1.call-start = ((), (), s32[]{:S(2)}) async-start(), calls=%async_computation.13 | async-start | bytes 2654208 | tf_op jit(solution)/shard_map/all_gather | solution.py:303
  243.1 223.9 %all-reduce.28.cloned.1.call-start = ((), (), s32[]{:S(2)}) async-start(), calls=%async_computation.14 | async-start | bytes 6291456 | tf_op jit(solution)/shard_map/psum | solution.py:329
  243.2 97.7 %copy-start.58 = (f32[768]{0:T(1024)}, f32[768]{0:T(1024)S(1)}, u32[]{:S(2)}) copy-start(f32[768]{0:T(1024)S(1)} %convert_element_type.367) | copy-start | bytes 9220
  399.9 130.7 %all-gather.20.cloned.1.call-start = ((), (), s32[]{:S(2)}) async-start(), calls=%async_computation.15 | async-start | bytes 3538944 | tf_op jit(solution)/shard_map/all_gather | solution.py:303
  401.8 190.9 %all-gather.22.cloned.1.call-start = ((), (), s32[]{:S(2)}) async-start(), calls=%async_computation.16 | async-start | bytes 3538944 | tf_op jit(solution)/shard_map/all_gather | solution.py:303
  403.8 251.0 %all-gather.24.cloned.1.call-start = ((), (), s32[]{:S(2)}) async-start(), calls=%async_computation.17 | async-start | bytes 3538944 | tf_op jit(solution)/shard_map/all_gather | solution.py:303
  405.9 336.7 %all-reduce.30.cloned.1.call-start = ((), (), s32[]{:S(2)}) async-start(), calls=%async_computation.18 | async-start | bytes 6291456 | tf_op jit(solution)/shard_map/psum | solution.py:329
  675.4 169.1 %all-gather.28.cloned.1.call-start = ((), (), s32[]{:S(2)}) async-start(), calls=%async_computation.28 | async-start | bytes 1769472 | tf_op jit(solution)/shard_map/all_gather | solution.py:438
  800.1 182.2 %all-reduce.32.cloned.1.call-start = ((), (), s32[]{:S(2)}) async-start(), calls=%async_computation.19 | async-start | bytes 524288 | tf_op jit(solution)/shard_map/psum | solution.py:329
  951.3 113.6 %reduce-scatter.35.cloned.1.call-start = ((), (), s32[]{:S(2)}) async-start(), calls=%async_computation.31 | async-start | bytes 442368
  952.3 159.3 %reduce-scatter.31.cloned.1.call-start = ((), (), s32[]{:S(2)}) async-start(), calls=%async_computation.29 | async-start | bytes 442368
  996.2 179.2 %reduce-scatter.33.cloned.1.call-start = ((), (), s32[]{:S(2)}) async-start(), calls=%async_computation.30 | async-start | bytes 221184
  999.1 240.1 %reduce-scatter.21.cloned.1.call-start = ((), (), s32[]{:S(2)}) async-start(), calls=%async_computation.22 | async-start | bytes 221184 | tf_op jit(solution)/shard_map/reduce_scatter | solution.py:510
  1000.7 310.2 %reduce-scatter.23.cloned.1.call-start = ((), (), s32[]{:S(2)}) async-start(), calls=%async_computation.23 | async-start | bytes 2654208 | tf_op jit(solution)/shard_map/reduce_scatter | solution.py:510
  1008.3 379.3 %reduce-scatter.25.cloned.1.call-start = ((), (), s32[]{:S(2)}) async-start(), calls=%async_computation.24 | async-start | bytes 3538944 | tf_op jit(solution)/shard_map/reduce_scatter | solution.py:510
  1014.8 449.9 %reduce-scatter.27.cloned.1.call-start = ((), (), s32[]{:S(2)}) async-start(), calls=%async_computation.25 | async-start | bytes 3538944 | tf_op jit(solution)/shard_map/reduce_scatter | solution.py:510
  1021.4 514.9 %reduce-scatter.19.cloned.1.call-start = ((), (), s32[]{:S(2)}) async-start(), calls=%async_computation.21 | async-start | bytes 2654208 | tf_op jit(solution)/shard_map/reduce_scatter | solution.py:510
  1028.7 584.7 %reduce-scatter.29.cloned.1.call-start = ((), (), s32[]{:S(2)}) async-start(), calls=%async_computation.26 | async-start | bytes 3538944 | tf_op jit(solution)/shard_map/reduce_scatter | solution.py:510
  1037.0 698.3 %all-reduce.34.cloned.1.call-start = ((), (), s32[]{:S(2)}) async-start(), calls=%async_computation.32 | async-start | bytes 12582912 | tf_op jit(solution)/shard_map/psum | solution.py:329
  1046.4 6.1 collective-permute-start.2
  1056.7 751.8 %reduce-scatter.17.cloned.1.call-start = ((), (), s32[]{:S(2)}) async-start(), calls=%async_computation.20 | async-start | bytes 2654208 | tf_op jit(solution)/shard_map/reduce_scatter | solution.py:510
  1062.9 672.4 %copy-start.27 = (f32[1536]{0:T(1024)S(1)}, f32[1536]{0:T(1024)}, u32[]{:S(2)}) copy-start(f32[1536]{0:T(1024)} %copy-done.26) | copy-start | bytes 18436
  1062.9 672.4 %copy-start.30 = (f32[1024]{0:T(1024)S(1)}, f32[1024]{0:T(1024)}, u32[]{:S(2)}) copy-start(f32[1024]{0:T(1024)} %copy-done.29) | copy-start | bytes 12292
  (71 other events, 1106.8 us)
Sparse Core Ops, SparseCore 0:
  10.8 55.2 all-gather.13
  164.9 33.6 all-reduce.25
  241.6 44.2 all-gather.25
  288.8 51.1 all-gather.15
  342.8 50.6 all-gather.17
  400.0 66.9 all-reduce.27
  470.0 60.5 all-gather.19
  533.6 59.0 all-gather.21
  595.7 59.0 all-gather.23
  675.5 67.0 all-reduce.29
  800.2 44.2 all-gather.27
  951.4 30.7 all-reduce.31
  986.1 61.4 reduce-scatter.34
  1051.2 60.3 reduce-scatter.30
  1115.3 60.0 reduce-scatter.32
  1179.1 60.0 reduce-scatter.20
  1242.6 68.2 reduce-scatter.22
  1314.3 73.2 reduce-scatter.24
  1391.2 73.5 reduce-scatter.26
  1468.1 68.1 reduce-scatter.18
  1539.9 73.4 reduce-scatter.28
  1616.4 118.9 all-reduce.33
  1738.8 69.5 reduce-scatter.16

commit v2 on v1

--- a/solution.py
+++ b/solution.py
@@ -279,6 +279,162 @@
     )(*[value for value, _ in ins])
 
 
+def pairs_of(axis):
+    return lax.axis_size(axis) // 2
+
+
+def hop(value, steps):
+    count = lax.axis_size("seq")
+    return lax.ppermute(value, "seq", [(s, (s + 2 * steps) % count) for s in range(count)])
+
+
+def swap(value, axis, bit):
+    return lax.ppermute(value, axis, [(s, s ^ bit) for s in range(lax.axis_size(axis))])
+
+
+def gather_rows(value):
+    size = value.shape[0]
+    place = lax.axis_index("seq")
+    around = pairs_of("seq")
+    low, high = place % 2, place // 2
+    own = [value] + [hop(value, steps) for steps in range(1, around)]
+    other = [swap(part, "seq", 1) for part in own]
+    full = jnp.zeros((2 * around * size,) + value.shape[1:], value.dtype)
+    for steps in range(around):
+        source = (high - steps + around) % around * 2
+        full = lax.dynamic_update_slice_in_dim(full, own[steps], (source + low) * size, 0)
+        full = lax.dynamic_update_slice_in_dim(full, other[steps], (source + 1 - low) * size, 0)
+    return full
+
+
+def scatter_rows(value, kind=BF):
+    place = lax.axis_index("seq")
+    around = pairs_of("seq")
+    low, high = place % 2, place // 2
+    size = value.shape[0] // (2 * around)
+    blocks = value.astype(kind).reshape((around, 2, size) + value.shape[1:])
+    theirs = lax.dynamic_index_in_dim(blocks, 1 - low, 1, False)
+    mine = lax.dynamic_index_in_dim(blocks, low, 1, False)
+    half = mine.astype(F32) + swap(theirs, "seq", 1).astype(F32)
+    total = lax.dynamic_index_in_dim(half, high, 0, False)
+    half = half.astype(kind)
+    for steps in range(1, around):
+        part = lax.dynamic_index_in_dim(half, (high + steps) % around, 0, False)
+        total = total + hop(part, steps).astype(F32)
+    return total
+
+
+def head_bits():
+    return (lax.axis_size("head") - 1).bit_length()
+
+
+def head_scatter(value):
+    place = lax.axis_index("head")
+    for k in range(head_bits()):
+        bit = place // 2**k % 2
+        halves = value.astype(BF).reshape((2, value.shape[0] // 2) + value.shape[1:])
+        keep = lax.dynamic_index_in_dim(halves, bit, 0, False)
+        send = lax.dynamic_index_in_dim(halves, 1 - bit, 0, False)
+        value = keep.astype(F32) + swap(send, "head", 2**k).astype(F32)
+    return value
+
+
+def head_part(value):
+    place = lax.axis_index("head")
+    for k in range(head_bits()):
+        size = value.shape[0] // 2
+        value = lax.dynamic_slice_in_dim(value, place // 2**k % 2 * size, size, 0)
+    return value
+
+
+def head_gather(value):
+    place = lax.axis_index("head")
+    for k in reversed(range(head_bits())):
+        got = swap(value, "head", 2**k)
+        first = (place // 2**k % 2 == 0)
+        value = jnp.concatenate([jnp.where(first, value, got), jnp.where(first, got, value)])
+    return value
+
+
+def head_total(value, kind):
+    for k in range(head_bits()):
+        value = value.astype(kind)
+        value = value.astype(F32) + swap(value, "head", 2**k).astype(F32)
+    return value
+
+
+def first_kernel(count, *refs):
+    kinds = (len(refs) - 5) // 2
+    sources, targets = refs[:kinds], refs[kinds : 2 * kinds]
+    hop_send, hop_recv, swap_send, swap_recv, local_sem = refs[2 * kinds :]
+    place = lax.axis_index("seq")
+    around = count // 2
+    low, high = lax.rem(place, 2), place // 2
+    mate = high * 2 + 1 - low
+    at = lambda steps: lax.rem(high + steps + around, around) * 2 + low
+    barrier = pltpu.get_barrier_semaphore()
+
+    def greet(device):
+        pl.semaphore_signal(
+            barrier, inc=1, device_id={"seq": device}, device_id_type=pl.DeviceIdType.MESH
+        )
+
+    for steps in range(1, around):
+        greet(at(steps))
+    greet(mate)
+    pl.semaphore_wait(barrier, around)
+
+    def send(source, target, sems, device):
+        copy = pltpu.make_async_remote_copy(
+            src_ref=source,
+            dst_ref=target,
+            send_sem=sems[0],
+            recv_sem=sems[1],
+            device_id={"seq": device},
+            device_id_type=pl.DeviceIdType.MESH,
+        )
+        copy.start()
+        return copy
+
+    hops, swaps, own = {}, {}, []
+    for k in range(kinds):
+        copy = pltpu.make_async_copy(sources[k], targets[k].at[place], local_sem.at[k])
+        copy.start()
+        own.append(copy)
+        for steps in range(1, around):
+            sems = hop_send.at[k, steps], hop_recv.at[k, steps]
+            hops[k, steps] = send(sources[k], targets[k].at[place], sems, at(steps))
+        sems = swap_send.at[k, 0], swap_recv.at[k, 0]
+        swaps[k, 0] = send(sources[k], targets[k].at[place], sems, mate)
+    for k in range(kinds):
+        for steps in range(1, around):
+            hops[k, steps].wait_recv()
+            block = targets[k].at[at(-steps)]
+            sems = swap_send.at[k, steps], swap_recv.at[k, steps]
+            swaps[k, steps] = send(block, block, sems, mate)
+    for k in range(kinds):
+        own[k].wait()
+        for steps in range(1, around):
+            hops[k, steps].wait_send()
+        for steps in range(around):
+            swaps[k, steps].wait()
+
+
+def first_gather(*values):
+    count = lax.axis_size("seq")
+    around = count // 2
+    kinds = len(values)
+    sems = pltpu.SemaphoreType.DMA
+    return pl.pallas_call(
+        functools.partial(first_kernel, count),
+        out_shape=tuple(jax.ShapeDtypeStruct((count,) + v.shape, v.dtype) for v in values),
+        in_specs=[pl.BlockSpec(memory_space=pl.ANY)] * kinds,
+        out_specs=tuple([pl.BlockSpec(memory_space=pl.ANY)] * kinds),
+        scratch_shapes=[sems((kinds, around))] * 4 + [sems((kinds,))],
+        compiler_params=pltpu.CompilerParams(collective_id=0, has_side_effects=True),
+    )(*values)
+
+
 def shards(
     x_in,
     seg_ids,
@@ -300,33 +456,63 @@
     w_down,
     d_out,
 ):
-    gathered = lambda value, axis: lax.all_gather(value.astype(BF), "seq", axis=axis, tiled=True)
-    full_norm1 = gathered(norm1_gain, 0)
-    full_in_x = gathered(w_in_x, 0)
-    full_in_z = gathered(w_in_z, 0)
-    full_conv_w = gathered(conv_w, 1)
-    full_conv_b = gathered(conv_b, 0)
-    full_xproj = gathered(w_xproj, 0)
-    full_ssm_gain = gathered(ssm_gain, 0)
-    full_w_dt = gathered(w_dt, 1)
-    full_dt_bias = gathered(dt_bias, 0)
-    full_a_log = gathered(a_log, 0)
-    full_d_skip = gathered(d_skip, 0)
-    full_w_out = gathered(w_out, 1)
-    full_norm2 = gathered(norm2_gain, 0)
-    full_gate = gathered(w_gate, 0)
-    full_up = gathered(w_up, 0)
-    full_down = gathered(w_down, 1)
     count = lax.axis_size("seq")
     place = lax.axis_index("seq")
     seqs, tokens, width = x_in.shape
     rows = seqs * tokens
-    taps = full_conv_w.shape[0]
-    rank = full_w_dt.shape[0]
-    states = full_a_log.shape[1]
-    channels = full_in_x.shape[1]
+    taps = conv_w.shape[0]
+    rank = w_dt.shape[0]
+    states = a_log.shape[1]
+    channels = w_in_x.shape[1]
     halo = (taps - 1) * seqs
-    head_sum = lambda value: lax.psum(value.astype(BF), "head").astype(F32)
+
+    per = channels // count
+    fields = [w_xproj, w_dt.T, a_log, conv_w.T, conv_b[:, None], dt_bias[:, None], d_skip[:, None]]
+    starts = [0]
+    for field in fields:
+        starts.append(starts[-1] + field.shape[1])
+    pack_width = -(-starts[-1] // LANES) * LANES
+    gains = [norm1_gain, norm2_gain, ssm_gain]
+    gain_starts = [0]
+    for gain in gains:
+        gain_starts.append(gain_starts[-1] + gain.shape[0])
+    pack_rows = -(-(per + -(-gain_starts[-1] // pack_width)) // 16) * 16
+
+    def pack(channel_fields, gain_fields):
+        table = jnp.concatenate([f.astype(F32) for f in channel_fields], axis=1)
+        table = jnp.pad(table, ((0, 0), (0, pack_width - table.shape[1])))
+        table = table.reshape(-1, per, pack_width)
+        rest = jnp.concatenate([g.astype(F32).reshape(table.shape[0], -1) for g in gain_fields], 1)
+        rest = jnp.pad(rest, ((0, 0), (0, (pack_rows - per) * pack_width - rest.shape[1])))
+        return jnp.concatenate([table, rest.reshape(-1, pack_rows - per, pack_width)], axis=1)
+
+    def unpack(block):
+        table = block[:, :per].reshape(-1, pack_width)
+        rest = block[:, per:].reshape(block.shape[0], -1)
+        return (
+            [table[:, starts[k] : starts[k + 1]] for k in range(len(fields))],
+            [rest[:, gain_starts[k] : gain_starts[k + 1]].reshape(-1) for k in range(len(gains))],
+        )
+
+    in_x_blocks, pack_blocks = first_gather(w_in_x.astype(BF), pack(fields, gains)[0].astype(BF))
+    full_in_x = in_x_blocks.reshape(width, channels)
+    fulls, full_gains = unpack(pack_blocks)
+    full_xproj, w_dt_cols, full_a_log, conv_cols, conv_b_col, bias_col, skip_col = fulls
+    full_w_dt = w_dt_cols.T
+    full_conv_w = conv_cols.T
+    full_conv_b, full_dt_bias, full_d_skip = conv_b_col[:, 0], bias_col[:, 0], skip_col[:, 0]
+    full_norm1, full_norm2, full_ssm_gain = full_gains
+
+    w_mix = jnp.concatenate([w_in_z.astype(BF), w_out.astype(BF).T], axis=1)
+    w_ffn = jnp.concatenate([w_gate.astype(BF), w_up.astype(BF), w_down.astype(BF).T], axis=1)
+    w_mix, w_ffn, full_in_x = lax.optimization_barrier((w_mix, w_ffn, full_in_x))
+    full_mix = gather_rows(w_mix)
+    full_ffn = gather_rows(w_ffn)
+    full_in_z, full_out_t = full_mix[:, :channels], full_mix[:, channels:]
+    hidden_units = w_gate.shape[1]
+    full_gate, full_up, full_down_t = (
+        full_ffn[:, k * hidden_units : (k + 1) * hidden_units] for k in range(3)
+    )
 
     norm1_vec = full_norm1.astype(F32)
     x_rows = x_in.transpose(1, 0, 2).reshape(rows, width).astype(F32)
@@ -347,7 +533,7 @@
         same_docs.append(same)
         x_conv = x_conv + conv_weight[offset] * extended[first : first + rows] * same
     u_low = jax.nn.silu(x_conv).astype(BF)
-    projected = head_sum(jnp.dot(u_low, full_xproj, preferred_element_type=F32))
+    projected = head_total(jnp.dot(u_low, full_xproj, preferred_element_type=F32), BF)
     ssm_vec = full_ssm_gain.astype(F32)
     b_end = rank + states
     dt_normed, dt_scale = norm_rows(projected[:, :rank], ssm_vec[:rank])
@@ -399,32 +585,34 @@
     silu_z = jax.nn.silu(z_gate)
     g_low = (y_full * silu_z).astype(BF)
     norm2_vec = full_norm2.astype(F32)
-    hidden = x_rows + head_sum(jnp.dot(g_low, full_w_out, preferred_element_type=F32))
+    mixed = jnp.einsum("re,de->rd", g_low, full_out_t, preferred_element_type=F32)
+    hidden = head_part(x_rows) + head_scatter(mixed)
     normed2, scale_two = norm_rows(hidden, norm2_vec)
-    x_norm2 = normed2.astype(BF)
+    x_norm2 = head_gather(normed2.astype(BF))
     gate_proj = jnp.dot(x_norm2, full_gate, preferred_element_type=F32)
     up_proj = jnp.dot(x_norm2, full_up, preferred_element_type=F32)
     silu_gate = jax.nn.silu(gate_proj)
     act_low = (silu_gate * up_proj).astype(BF)
-    ffn_out = head_sum(jnp.dot(act_low, full_down, preferred_element_type=F32))
-    block_out = (hidden + ffn_out).astype(BF).reshape(tokens, seqs, width).transpose(1, 0, 2)
+    ffn_part = jnp.einsum("rf,df->rd", act_low, full_down_t, preferred_element_type=F32)
+    block_rows = head_gather((hidden + head_scatter(ffn_part)).astype(BF))
+    block_out = block_rows.reshape(tokens, seqs, width).transpose(1, 0, 2)
     grad_low = d_out.transpose(1, 0, 2).reshape(rows, width)
     grad_rows = grad_low.astype(F32)
-    grad_down = jnp.einsum("rf,rd->fd", act_low, grad_low, preferred_element_type=F32)
-    d_act = jnp.einsum("rd,fd->rf", grad_low, full_down, preferred_element_type=F32)
+    grad_down = jnp.einsum("rd,rf->df", grad_low, act_low, preferred_element_type=F32)
+    d_act = jnp.dot(grad_low, full_down_t, preferred_element_type=F32)
     d_gate = (d_act * up_proj * silu_slope(gate_proj)).astype(BF)
     d_up = (d_act * silu_gate).astype(BF)
     grad_gate = jnp.einsum("rd,rf->df", x_norm2, d_gate, preferred_element_type=F32)
     grad_up = jnp.einsum("rd,rf->df", x_norm2, d_up, preferred_element_type=F32)
-    d_norm2 = head_sum(
+    d_norm2 = head_scatter(
         jnp.einsum("rf,df->rd", d_gate, full_gate, preferred_element_type=F32)
         + jnp.einsum("rf,df->rd", d_up, full_up, preferred_element_type=F32)
     )
     d_hidden_part, grad_norm2 = norm_back(hidden, scale_two, norm2_vec, d_norm2)
-    d_hidden = grad_rows + d_hidden_part
-    d_mix = d_hidden.astype(BF)
-    grad_out_w = jnp.einsum("re,rd->ed", g_low, d_mix, preferred_element_type=F32)
-    d_g = jnp.einsum("rd,ed->re", d_mix, full_w_out, preferred_element_type=F32)
+    d_hidden = head_part(grad_rows) + d_hidden_part
+    d_mix = head_gather(d_hidden.astype(BF))
+    grad_out_w = jnp.einsum("rd,re->de", d_mix, g_low, preferred_element_type=F32)
+    d_g = jnp.dot(d_mix, full_out_t, preferred_element_type=F32)
     d_y = d_g * silu_z
     d_z = (d_g * y_full * silu_slope(z_gate)).astype(BF)
     grad_skip = jnp.sum(d_y * u_rows, axis=0)
@@ -466,7 +654,7 @@
     d_pre_low = d_pre.astype(BF)
     grad_step_w = jnp.einsum("rk,re->ke", dt_low, d_pre_low, preferred_element_type=F32)
     d_dt_part = jnp.einsum("re,ke->rk", d_pre_low, full_w_dt, preferred_element_type=F32)
-    d_stats = head_sum(jnp.concatenate([d_dt_part, d_bc[:, : 2 * states]], axis=1))
+    d_stats = head_total(jnp.concatenate([d_dt_part, d_bc[:, : 2 * states]], axis=1), BF)
     d_dt_raw, grad_dt_gain = norm_back(
         projected[:, :rank], dt_scale, ssm_vec[:rank], d_stats[:, :rank]
     )
@@ -501,35 +689,55 @@
     d_inner_low = d_inner.astype(BF)
     grad_in_x = jnp.einsum("rd,re->de", x_norm, d_inner_low, preferred_element_type=F32)
     grad_in_z = jnp.einsum("rd,re->de", x_norm, d_z, preferred_element_type=F32)
-    d_norm1 = head_sum(
+    d_norm1 = head_scatter(
         jnp.einsum("re,de->rd", d_inner_low, full_in_x, preferred_element_type=F32)
         + jnp.einsum("re,de->rd", d_z, full_in_z, preferred_element_type=F32)
     )
-    d_input_part, grad_norm1 = norm_back(x_rows, scale_one, norm1_vec, d_norm1)
-    grad_input = (d_hidden + d_input_part).reshape(tokens, seqs, width).transpose(1, 0, 2)
-    scattered = lambda value, axis: lax.psum_scatter(
-        value, "seq", scatter_dimension=axis, tiled=True
-    )
-    shrunk = lambda value, axis: scattered(value.astype(BF), axis).astype(F32)
+    d_input_part, grad_norm1 = norm_back(head_part(x_rows), head_part(scale_one), norm1_vec, d_norm1)
+    input_rows = head_gather((d_hidden + d_input_part).astype(BF)).astype(F32)
+    grad_input = input_rows.reshape(tokens, seqs, width).transpose(1, 0, 2)
+
+    grad_ssm = grad_ssm * (lax.axis_index("head") == 0).astype(F32)
+    small = pack(
+        [
+            grad_xproj,
+            grad_step_w.T,
+            grad_alog,
+            grad_conv_w.T,
+            grad_conv_b[:, None],
+            grad_bias[:, None],
+            grad_skip[:, None],
+        ],
+        [grad_norm1, grad_norm2, grad_ssm],
+    )
+    small = scatter_rows(small.reshape(-1, pack_width), F32)
+    small = jnp.concatenate([small[:per], head_total(small[per:], F32)])[None]
+    small_fields, small_gains = unpack(small)
+    own_down = scatter_rows(grad_down)
+    own_gate = scatter_rows(grad_gate)
+    own_up = scatter_rows(grad_up)
+    own_out = scatter_rows(grad_out_w)
+    own_in_z = scatter_rows(grad_in_z)
+    own_in_x = scatter_rows(grad_in_x)
     return (
         block_out,
         grad_input,
-        scattered(grad_norm1, 0),
-        shrunk(grad_in_x, 0),
-        shrunk(grad_in_z, 0),
-        scattered(grad_conv_w, 1),
-        scattered(grad_conv_b, 0),
-        shrunk(grad_xproj, 0),
-        scattered(grad_ssm, 0),
-        shrunk(grad_step_w, 1),
-        scattered(grad_bias, 0),
-        scattered(grad_alog, 0),
-        scattered(grad_skip, 0),
-        shrunk(grad_out_w, 1),
-        scattered(grad_norm2, 0),
-        shrunk(grad_gate, 0),
-        shrunk(grad_up, 0),
-        shrunk(grad_down, 1),
+        small_gains[0],
+        own_in_x,
+        own_in_z,
+        small_fields[3].T,
+        small_fields[4][:, 0],
+        small_fields[0],
+        small_gains[2],
+        small_fields[1].T,
+        small_fields[5][:, 0],
+        small_fields[2],
+        small_fields[6][:, 0],
+        own_out.T,
+        small_gains[1],
+        own_gate,
+        own_up,
+        own_down.T,
     )
 
 

time: 1830 us -> 1110 us (0.61)
  waiting for transfers between devices: 1080 us -> 293 us
  starting transfers between devices: 10.7 us -> 147 us
  blocking collectives: 215 us -> 83.5 us
  local copies, waits for them, and re-layouts: 38.3 us -> 85.3 us
  Pallas kernels: 219 us -> 261 us
    reduce_scatter x7 -> x0, waiting for transfers between devices: 430 us -> none  [shards(): lax.psum_scatter(value, 'seq', scatter_dimension=axis, tiled=True)]
    ppermute x0 -> x64, waiting for transfers between devices: none -> 288 us  [the longest x37 155 us: swap(): lax.ppermute(value, axis, [(s, s ^ bit) for s in range(lax.axis_size(axis...]
    psum x5 -> x0, waiting for transfers between devices: 279 us -> none  [shards(): head_sum = lambda value: lax.psum(value.astype(BF), 'head').astype(F32)]
    all_gather x6 -> x0, waiting for transfers between devices: 203 us -> none  [shards(): lax.all_gather(value.astype(BF), 'seq', axis=axis, tiled=True)]
    ppermute x0 -> x64, starting transfers between devices: none -> 136 us  [the longest x27 108 us: hop(): lax.ppermute(value, 'seq', [(s, (s + 2 * steps) % count) for s in range(c...]
    all_gather x4 -> x0, blocking collectives: 109 us -> none  [shards(): lax.all_gather(value.astype(BF), 'seq', axis=axis, tiled=True)]
    unnamed x26 -> x2, waiting for transfers between devices: 108 us -> 0.03 us
    unnamed x2 -> x0, blocking collectives: 74.1 us -> none
  transfers between devices with their start and end apart: 26 -> 69, of which waited for: 22 -> 25; matrix products, arithmetic and copies ran while one was open for 10% -> 19% of each run, Pallas kernels for 3% -> 7%
where the time goes in v2:
time: 1110 us
  waiting for transfers between devices  293 us (26%)
  Pallas kernels  261 us (24%)
  starting transfers between devices  147 us (13%)
  matrix products  116 us (10%)
  other arithmetic  103 us (9%)
  local copies, waits for them, and re-layouts  85.3 us (8%)
  blocking collectives  83.5 us (8%)
  between operations  16.8 us (2%)
    pallas_call x4, Pallas kernels, state_call(): pl.pallas_call(functools.partial(body, seqs, tokens, states), grid=(chann...  219 us
    ppermute x37, waiting for transfers between devices, swap(): lax.ppermute(value, axis, [(s, s ^ bit) for s in range(lax.axis_size(axis...  155 us
    ppermute x27, waiting for transfers between devices, hop(): lax.ppermute(value, 'seq', [(s, (s + 2 * steps) % count) for s in range(c...  133 us
    ppermute x27, starting transfers between devices, hop(): lax.ppermute(value, 'seq', [(s, (s + 2 * steps) % count) for s in range(c...  108 us
    all_gather x1, blocking collectives, shards(): all_sums = lax.all_gather(step_sum, 'seq')  83.5 us
    pallas_call x1, Pallas kernels, first_gather(): pl.pallas_call(functools.partial(first_kernel, count), out_shape=tuple((j...  41.5 us
    unnamed x242, local copies, waits for them, and re-layouts  29.2 us
    ppermute x37, starting transfers between devices, swap(): lax.ppermute(value, axis, [(s, s ^ bit) for s in range(lax.axis_size(axis...  27.2 us
  transfers between devices with their start and end apart: 69, of which 25 were waited for; matrix products, arithmetic and copies ran while one was open for 19% of the time, Pallas kernels for 7%

profile of v2, /device:TPU:0, one launch (start us, length us, event | category | flops | bytes accessed | tf_op | source)
XLA Modules:
  0.0 1106.4 jit_solution(18113125717673108763)
XLA Ops:
  36.5 41.5 %shard_map.322 = (bf16[8,192,768]{2,1,0:T(8,128)(2,1)}, bf16[8,112,256]{2,1,0:T(8,128)(2,1)}) custom-call(bf16[192,768]{1,0:T(8,128)(2,1)} %convert_element_type.552.refs_0_, bf16[112,256]{1,0:T(8,128)(2,1)} %maximum_bitcast_fusion.3.refs_1_), custom_call_target="tpu_custom_call" | custom-call | tf_op jit(solution)/shard_map/pallas_call | solution.py:428
  121.5 34.7 %shard_map.323 = (bf16[128,768]{1,0:T(8,128)(2,1)}, f32[8,768]{1,0:T(8,128)}) custom-call(f32[1024,128]{1,0:T(8,128)} %maximum_maximum_fusion.bc_ref, f32[1024,768]{1,0:T(8,128)} %get-tuple-element.267.step_ref, bf16[1024,768]{1,0:T(8,128)(2,1)} %copy-done.4, f32[128,768]{1,0:T(8,128)} %broadcast_bitcast_fusion.rate_ref), custom_call_target="tpu_custom_call" | custom-call | flops 75497472 | bytes 16777216 | tf_op jit(solution)/shard_map/pallas_call | solution.py:270
  158.2 7.3 collective-permute-start.7
  171.8 83.5 %all-gather = f32[64,768]{1,0:T(8,128)S(1)} all-gather(f32[8,768]{1,0:T(8,128)S(1)} %copy-done.70), channel_id=2, replica_groups=mesh['seq'=8,'head'=4] {'seq'}, dimensions={0}, use_global_device_ids=true | all-gather | bytes 221184 | tf_op jit(solution)/shard_map/all_gather | solution.py:565
  260.0 11.6 %collective-permute-done.6 = bf16[192,1536]{1,0:T(8,128)(2,1)S(1)} collective-permute-done((bf16[192,1536]{1,0:T(8,128)(2,1)S(1)}, bf16[192,1536]{1,0:T(8,128)(2,1)S(1)}, u32[]{:S(2)}, u32[]{:S(2)}) %collective-permute-start.6) | collective-permute-done | bytes 589856 | tf_op jit(solution)/shard_map/ppermute | solution.py:292
  273.3 9.0 collective-permute-done.8
  292.5 52.1 %shard_map.324 = f32[1024,768]{1,0:T(8,128)} custom-call(f32[1024,128]{1,0:T(8,128)} %maximum_maximum_fusion.bc_ref, f32[1024,768]{1,0:T(8,128)} %get-tuple-element.267.step_ref, bf16[1024,768]{1,0:T(8,128)(2,1)} %copy-done.4, f32[128,768]{1,0:T(8,128)} %broadcast_bitcast_fusion.rate_ref, f32[128,768]{1,0:T(8,128)} %fusion.83.start_ref), custom_call_target="tpu_custom_call" | custom-call | flops 100663296 | bytes 16777216 | tf_op jit(solution)/shard_map/pallas_call | solution.py:270
  344.6 9.4 multiply_convert_fusion.3
  384.5 9.2 collective-permute-done.16
  400.9 42.6 %collective-permute-done.18 = bf16[192,3072]{1,0:T(8,128)(2,1)} collective-permute-done((bf16[192,3072]{1,0:T(8,128)(2,1)}, bf16[192,3072]{1,0:T(8,128)(2,1)}, u32[]{:S(2)}, u32[]{:S(2)}) %collective-permute-start.18) | collective-permute-done | bytes 1179680 | tf_op jit(solution)/shard_map/ppermute | solution.py:288
  447.7 24.9 %collective-permute-done.19 = bf16[192,3072]{1,0:T(8,128)(2,1)S(1)} collective-permute-done((bf16[192,3072]{1,0:T(8,128)(2,1)}, bf16[192,3072]{1,0:T(8,128)(2,1)S(1)}, u32[]{:S(2)}, u32[]{:S(2)}) %collective-permute-start.19) | collective-permute-done | bytes 1179680 | tf_op jit(solution)/shard_map/ppermute | solution.py:292
  474.1 22.5 %collective-permute-done.21 = bf16[192,3072]{1,0:T(8,128)(2,1)S(1)} collective-permute-done((bf16[192,3072]{1,0:T(8,128)(2,1)}, bf16[192,3072]{1,0:T(8,128)(2,1)S(1)}, u32[]{:S(2)}, u32[]{:S(2)}) %collective-permute-start.21) | collective-permute-done | bytes 1179680 | tf_op jit(solution)/shard_map/ppermute | solution.py:292
  508.0 9.5 fusion.2
  551.2 9.3 collective-permute-done.27
  561.2 15.2 %collective-permute-done.23 = bf16[256,1536]{1,0:T(8,128)(2,1)S(1)} collective-permute-done((bf16[256,1536]{1,0:T(8,128)(2,1)S(1)}, bf16[256,1536]{1,0:T(8,128)(2,1)S(1)}, u32[]{:S(2)}, u32[]{:S(2)}) %collective-permute-start.23) | collective-permute-done | bytes 786464 | tf_op jit(solution)/shard_map/ppermute | solution.py:292
  606.7 24.8 %collective-permute-start.58 = (bf16[192,1024]{1,0:T(8,128)(2,1)}, bf16[192,1024]{1,0:T(8,128)(2,1)}, u32[]{:S(2)}, u32[]{:S(2)}) collective-permute-start(bf16[192,1024]{1,0:T(8,128)(2,1)} %get-tuple-element.224), channel_id=1, source_target_pairs={{0,24},{4,28},{8,0},{12,4},{16,8},{20,12},{24,16},{28,20},{1,25},{... | collective-permute-start | bytes 1179656 | tf_op jit(solution)/shard_map/ppermute | solution.py:288
  635.8 13.1 %collective-permute-start.56 = (bf16[192,1024]{1,0:T(8,128)(2,1)S(1)}, bf16[192,1024]{1,0:T(8,128)(2,1)}, u32[]{:S(2)}, u32[]{:S(2)}) collective-permute-start(bf16[192,1024]{1,0:T(8,128)(2,1)S(1)} %get-tuple-element.223), channel_id=1, source_target_pairs={{0,8},{4,12},{8,16},{12,20},{16,24},{20,28},{24,0},{28,4},{1,9},{5... | collective-permute-start | bytes 1179656 | tf_op jit(solution)/shard_map/ppermute | solution.py:288
  655.1 8.8 fusion.7
  663.9 35.3 %shard_map.325 = bf16[128,768]{1,0:T(8,128)(2,1)} custom-call(f32[1024,128]{1,0:T(8,128)} %maximum_maximum_fusion.bc_ref, f32[1024,768]{1,0:T(8,128)} %get-tuple-element.267.step_ref, f32[1024,768]{1,0:T(8,128)} %get-tuple-element.190.dy_ref, f32[128,768]{1,0:T(8,128)} %broadcast_bitcast_fusion.rate_ref), custom_call_target="tpu_custom_call" | custom-call | flops 75497472 | bytes 16777216 | tf_op jit(solution)/shard_map/pallas_call | solution.py:270
  708.3 10.0 collective-permute-done.62
  718.3 16.0 %collective-permute-start.65 = (bf16[192,1024]{1,0:T(8,128)(2,1)S(1)}, bf16[192,1024]{1,0:T(8,128)(2,1)S(1)}, u32[]{:S(2)}, u32[]{:S(2)}) collective-permute-start(bf16[192,1024]{1,0:T(8,128)(2,1)S(1)} %get-tuple-element.219), channel_id=1, source_target_pairs={{0,16},{4,20},{8,24},{12,28},{16,0},{20,4},{24,8},{28,12},{1,17},{... | collective-permute-start | bytes 1179656 | tf_op jit(solution)/shard_map/ppermute | solution.py:288
  734.3 32.8 %collective-permute-done.61 = bf16[192,1024]{1,0:T(8,128)(2,1)S(1)} collective-permute-done((bf16[192,1024]{1,0:T(8,128)(2,1)S(1)}, bf16[192,1024]{1,0:T(8,128)(2,1)S(1)}, u32[]{:S(2)}, u32[]{:S(2)}) %collective-permute-start.61) | collective-permute-done | bytes 393248 | tf_op jit(solution)/shard_map/ppermute | solution.py:288
  772.1 15.3 %collective-permute-done.65 = bf16[192,1024]{1,0:T(8,128)(2,1)S(1)} collective-permute-done((bf16[192,1024]{1,0:T(8,128)(2,1)S(1)}, bf16[192,1024]{1,0:T(8,128)(2,1)S(1)}, u32[]{:S(2)}, u32[]{:S(2)}) %collective-permute-start.65) | collective-permute-done | bytes 393248 | tf_op jit(solution)/shard_map/ppermute | solution.py:288
  800.6 97.3 %shard_map.326 = (f32[1024,768]{1,0:T(8,128)}, f32[1024,768]{1,0:T(8,128)}, f32[1024,128]{1,0:T(8,128)}, f32[16,768]{1,0:T(8,128)}) custom-call(f32[1024,128]{1,0:T(8,128)} %maximum_maximum_fusion.bc_ref, f32[1024,768]{1,0:T(8,128)} %get-tuple-element.267.step_ref, bf16[1024,768]{1,0:T(8,128)(2,1)} %copy-done.4, f32[1024,768]{1,0:T(8,128)} %get-tuple-element.190.dy_ref, ...), custom_call_target="tpu_custom_call" | custom-call | flops 301989888 | bytes 16777216 | tf_op jit(solution)/shard_map/pallas_call | solution.py:270
  927.4 7.8 multiply_reduce_fusion.3
  961.9 11.4 %collective-permute-done.51 = bf16[4,192,768]{2,1,0:T(8,128)(2,1)S(1)} collective-permute-done((bf16[4,192,768]{2,1,0:T(8,128)(2,1)S(1)}, bf16[4,192,768]{2,1,0:T(8,128)(2,1)S(1)}, u32[]{:S(2)}, u32[]{:S(2)}) %collective-permute-start.51) | collective-permute-done | bytes 1179680 | tf_op jit(solution)/shard_map/ppermute | solution.py:292
  977.8 8.9 collective-permute-done.49
  998.5 11.1 %collective-permute-done.34 = bf16[256,1536]{1,0:T(8,128)(2,1)} collective-permute-done((bf16[256,1536]{1,0:T(8,128)(2,1)}, bf16[256,1536]{1,0:T(8,128)(2,1)}, u32[]{:S(2)}, u32[]{:S(2)}) %collective-permute-start.34) | collective-permute-done | bytes 786464 | tf_op jit(solution)/shard_map/ppermute | solution.py:292
  1012.3 13.4 %collective-permute-done.43 = bf16[4,192,768]{2,1,0:T(8,128)(2,1)} collective-permute-done((bf16[4,192,768]{2,1,0:T(8,128)(2,1)}, bf16[4,192,768]{2,1,0:T(8,128)(2,1)}, u32[]{:S(2)}, u32[]{:S(2)}) %collective-permute-start.43) | collective-permute-done | bytes 1179680 | tf_op jit(solution)/shard_map/ppermute | solution.py:292
  1037.8 10.2 collective-permute-start.39
  1059.6 9.6 collective-permute-start.45
  1071.9 11.1 %collective-permute-done.45 = bf16[192,768]{1,0:T(8,128)(2,1)S(1)} collective-permute-done((bf16[192,768]{1,0:T(8,128)(2,1)S(1)}, bf16[192,768]{1,0:T(8,128)(2,1)S(1)}, u32[]{:S(2)}, u32[]{:S(2)}) %collective-permute-start.45) | collective-permute-done | bytes 294944 | tf_op jit(solution)/shard_map/ppermute | solution.py:288
  (581 shorter events, 370.5 us)
Async XLA Ops:
  7.2 282.2 %all-gather.6.cloned.1.call-start = ((), (), s32[]{:S(2)}) async-start(), calls=%async_computation | async-start | bytes 1769472 | tf_op jit(solution)/shard_map/all_gather | solution.py:564
  8.8 89.0 %collective-permute-start.1 = (s32[24]{0:T(128)}, s32[24]{0:T(128)}, u32[]{:S(2)}, u32[]{:S(2)}) collective-permute-start(s32[24]{0:T(128)} %slice.279), channel_id=1, source_target_pairs={{0,4},{4,8},{8,12},{12,16},{16,20},{20,24},{24,28},{1,5},{5,9},{9,... | collective-permute-start | bytes 296 | tf_op jit(solution)/shard_map/ppermute | solution.py:22
  156.2 641.5 %all-gather.8.cloned.1.call-start = ((), (), s32[]{:S(2)}) async-start(), calls=%async_computation.1 | async-start | bytes 1769472 | tf_op jit(solution)/shard_map/all_gather | solution.py:626
  156.2 99.1 %collective-permute-start.5 = (bf16[192,1536]{1,0:T(8,128)(2,1)S(1)}, bf16[192,1536]{1,0:T(8,128)(2,1)S(1)}, u32[]{:S(2)}, u32[]{:S(2)}) collective-permute-start(bf16[192,1536]{1,0:T(8,128)(2,1)S(1)} %copy-done.32), channel_id=1, source_target_pairs={{0,8},{4,12},{8,16},{12,20},{16,24},{20,28},{24,0},{28,4},{1,9},{5... | collective-permute-start | bytes 1769480 | tf_op jit(solution)/shard_map/ppermute | solution.py:288
  158.2 97.8 %collective-permute-start.7 = (bf16[192,1536]{1,0:T(8,128)(2,1)S(1)}, bf16[192,1536]{1,0:T(8,128)(2,1)S(1)}, u32[]{:S(2)}, u32[]{:S(2)}) collective-permute-start(bf16[192,1536]{1,0:T(8,128)(2,1)S(1)} %copy-done.32), channel_id=1, source_target_pairs={{0,16},{4,20},{8,24},{12,28},{16,0},{20,4},{24,8},{28,12},{1,17},{... | collective-permute-start | bytes 1769480 | tf_op jit(solution)/shard_map/ppermute | solution.py:288
  165.6 92.6 %collective-permute-start.9 = (bf16[192,1536]{1,0:T(8,128)(2,1)S(1)}, bf16[192,1536]{1,0:T(8,128)(2,1)S(1)}, u32[]{:S(2)}, u32[]{:S(2)}) collective-permute-start(bf16[192,1536]{1,0:T(8,128)(2,1)S(1)} %copy-done.32), channel_id=1, source_target_pairs={{0,24},{4,28},{8,0},{12,4},{16,8},{20,12},{24,16},{28,20},{1,25},{... | collective-permute-start | bytes 1769480 | tf_op jit(solution)/shard_map/ppermute | solution.py:288
  165.6 92.7 %collective-permute-start.4 = (bf16[192,1536]{1,0:T(8,128)(2,1)S(1)}, bf16[192,1536]{1,0:T(8,128)(2,1)S(1)}, u32[]{:S(2)}, u32[]{:S(2)}) collective-permute-start(bf16[192,1536]{1,0:T(8,128)(2,1)S(1)} %copy-done.32), channel_id=1, source_target_pairs={{0,4},{4,0},{8,12},{12,8},{16,20},{20,16},{24,28},{28,24},{1,5},{5... | collective-permute-start | bytes 1769480 | tf_op jit(solution)/shard_map/ppermute | solution.py:292
  361.0 33.2 %collective-permute-start.15 = (bf16[192,3072]{1,0:T(8,128)(2,1)}, bf16[192,3072]{1,0:T(8,128)(2,1)}, u32[]{:S(2)}, u32[]{:S(2)}) collective-permute-start(bf16[192,3072]{1,0:T(8,128)(2,1)} %pad_maximum_fusion.8), channel_id=1, source_target_pairs={{0,4},{4,0},{8,12},{12,8},{16,20},{20,16},{24,28},{28,24},{1,5},{5... | collective-permute-start | bytes 3538952 | tf_op jit(solution)/shard_map/ppermute | solution.py:292
  363.3 80.3 %collective-permute-start.18 = (bf16[192,3072]{1,0:T(8,128)(2,1)}, bf16[192,3072]{1,0:T(8,128)(2,1)}, u32[]{:S(2)}, u32[]{:S(2)}) collective-permute-start(bf16[192,3072]{1,0:T(8,128)(2,1)} %pad_maximum_fusion.8), channel_id=1, source_target_pairs={{0,16},{4,20},{8,24},{12,28},{16,0},{20,4},{24,8},{28,12},{1,17},{... | collective-permute-start | bytes 3538952 | tf_op jit(solution)/shard_map/ppermute | solution.py:288
  366.4 77.5 %collective-permute-start.20 = (bf16[192,3072]{1,0:T(8,128)(2,1)}, bf16[192,3072]{1,0:T(8,128)(2,1)}, u32[]{:S(2)}, u32[]{:S(2)}) collective-permute-start(bf16[192,3072]{1,0:T(8,128)(2,1)} %pad_maximum_fusion.8), channel_id=1, source_target_pairs={{0,24},{4,28},{8,0},{12,4},{16,8},{20,12},{24,16},{28,20},{1,25},{... | collective-permute-start | bytes 3538952 | tf_op jit(solution)/shard_map/ppermute | solution.py:288
  393.7 51.8 %collective-permute-start.17 = (bf16[192,3072]{1,0:T(8,128)(2,1)}, bf16[192,3072]{1,0:T(8,128)(2,1)S(1)}, u32[]{:S(2)}, u32[]{:S(2)}) collective-permute-start(bf16[192,3072]{1,0:T(8,128)(2,1)} %collective-permute-done.16), channel_id=1, source_target_pairs={{0,4},{4,0},{8,12},{12,8},{16,20},{20,16},{24,28},{28,24},{1,5},{5... | collective-permute-start | bytes 3538952 | tf_op jit(solution)/shard_map/ppermute | solution.py:292
  398.0 49.2 %collective-permute-start.13 = (bf16[256,1536]{1,0:T(8,128)(2,1)S(1)}, bf16[256,1536]{1,0:T(8,128)(2,1)S(1)}, u32[]{:S(2)}, u32[]{:S(2)}) collective-permute-start(bf16[256,1536]{1,0:T(8,128)(2,1)S(1)} %multiply_convert_fusion.5), channel_id=1, source_target_pairs={{0,2},{1,3},{2,0},{3,1},{4,6},{5,7},{6,4},{7,5},{8,10},{9,11},{10,... | collective-permute-start | bytes 2359304 | tf_op jit(solution)/shard_map/ppermute | solution.py:292
  443.9 52.7 %collective-permute-start.21 = (bf16[192,3072]{1,0:T(8,128)(2,1)}, bf16[192,3072]{1,0:T(8,128)(2,1)S(1)}, u32[]{:S(2)}, u32[]{:S(2)}) collective-permute-start(bf16[192,3072]{1,0:T(8,128)(2,1)} %collective-permute-done.20), channel_id=1, source_target_pairs={{0,4},{4,0},{8,12},{12,8},{16,20},{20,16},{24,28},{28,24},{1,5},{5... | collective-permute-start | bytes 3538952 | tf_op jit(solution)/shard_map/ppermute | solution.py:292
  447.6 54.7 %collective-permute-start.14 = (bf16[512,1536]{1,0:T(8,128)(2,1)S(1)}, bf16[512,1536]{1,0:T(8,128)(2,1)S(1)}, u32[]{:S(2)}, u32[]{:S(2)}) collective-permute-start(bf16[512,1536]{1,0:T(8,128)(2,1)S(1)} %pad_maximum_fusion.4), channel_id=1, source_target_pairs={{0,1},{1,0},{2,3},{3,2},{4,5},{5,4},{6,7},{7,6},{8,9},{9,8},{10,11... | collective-permute-start | bytes 4718600 | tf_op jit(solution)/shard_map/ppermute | solution.py:292
  542.1 34.2 %collective-permute-start.23 = (bf16[256,1536]{1,0:T(8,128)(2,1)S(1)}, bf16[256,1536]{1,0:T(8,128)(2,1)S(1)}, u32[]{:S(2)}, u32[]{:S(2)}) collective-permute-start(bf16[256,1536]{1,0:T(8,128)(2,1)S(1)} %dynamic-slice_bitcast_fusion.12), channel_id=1, source_target_pairs={{0,2},{1,3},{2,0},{3,1},{4,6},{5,7},{6,4},{7,5},{8,10},{9,11},{10,... | collective-permute-start | bytes 2359304 | tf_op jit(solution)/shard_map/ppermute | solution.py:292
  547.9 53.9 %collective-permute-start.55 = (bf16[4,192,1024]{2,1,0:T(8,128)(2,1)}, bf16[4,192,1024]{2,1,0:T(8,128)(2,1)}, u32[]{:S(2)}, u32[]{:S(2)}) collective-permute-start(bf16[4,192,1024]{2,1,0:T(8,128)(2,1)} %dynamic-slice_bitcast_fusion.2), channel_id=1, source_target_pairs={{0,4},{4,0},{8,12},{12,8},{16,20},{20,16},{24,28},{28,24},{1,5},{5... | collective-permute-start | bytes 4718600 | tf_op jit(solution)/shard_map/ppermute | solution.py:292
  549.6 81.9 %collective-permute-start.59 = (bf16[4,192,1024]{2,1,0:T(8,128)(2,1)}, bf16[4,192,1024]{2,1,0:T(8,128)(2,1)}, u32[]{:S(2)}, u32[]{:S(2)}) collective-permute-start(bf16[4,192,1024]{2,1,0:T(8,128)(2,1)} %dynamic-slice_bitcast_fusion.1), channel_id=1, source_target_pairs={{0,4},{4,0},{8,12},{12,8},{16,20},{20,16},{24,28},{28,24},{1,5},{5... | collective-permute-start | bytes 4718600 | tf_op jit(solution)/shard_map/ppermute | solution.py:292
  594.3 106.2 %collective-permute-start.63 = (bf16[4,192,1024]{2,1,0:T(8,128)(2,1)}, bf16[4,192,1024]{2,1,0:T(8,128)(2,1)}, u32[]{:S(2)}, u32[]{:S(2)}) collective-permute-start(bf16[4,192,1024]{2,1,0:T(8,128)(2,1)} %dynamic-slice_bitcast_fusion), channel_id=1, source_target_pairs={{0,4},{4,0},{8,12},{12,8},{16,20},{20,16},{24,28},{28,24},{1,5},{5... | collective-permute-start | bytes 4718600 | tf_op jit(solution)/shard_map/ppermute | solution.py:292
  594.7 41.1 %collective-permute-start.24 = (bf16[256,1536]{1,0:T(8,128)(2,1)S(1)}, bf16[256,1536]{1,0:T(8,128)(2,1)S(1)}, u32[]{:S(2)}, u32[]{:S(2)}) collective-permute-start(bf16[256,1536]{1,0:T(8,128)(2,1)S(1)} %get-tuple-element.230), channel_id=1, source_target_pairs={{0,2},{1,3},{2,0},{3,1},{4,6},{5,7},{6,4},{7,5},{8,10},{9,11},{10,... | collective-permute-start | bytes 2359304 | tf_op jit(solution)/shard_map/ppermute | solution.py:292
  601.7 49.5 %collective-permute-start.29 = (bf16[512,1536]{1,0:T(8,128)(2,1)S(1)}, bf16[512,1536]{1,0:T(8,128)(2,1)S(1)}, u32[]{:S(2)}, u32[]{:S(2)}) collective-permute-start(bf16[512,1536]{1,0:T(8,128)(2,1)S(1)} %pad_maximum_fusion.6), channel_id=1, source_target_pairs={{0,1},{1,0},{2,3},{3,2},{4,5},{5,4},{6,7},{7,6},{8,9},{9,8},{10,11... | collective-permute-start | bytes 4718600 | tf_op jit(solution)/shard_map/ppermute | solution.py:292
  606.7 93.9 %collective-permute-start.58 = (bf16[192,1024]{1,0:T(8,128)(2,1)}, bf16[192,1024]{1,0:T(8,128)(2,1)}, u32[]{:S(2)}, u32[]{:S(2)}) collective-permute-start(bf16[192,1024]{1,0:T(8,128)(2,1)} %get-tuple-element.224), channel_id=1, source_target_pairs={{0,24},{4,28},{8,0},{12,4},{16,8},{20,12},{24,16},{28,20},{1,25},{... | collective-permute-start | bytes 1179656 | tf_op jit(solution)/shard_map/ppermute | solution.py:288
  631.5 72.8 %collective-permute-start.57 = (bf16[192,1024]{1,0:T(8,128)(2,1)}, bf16[192,1024]{1,0:T(8,128)(2,1)}, u32[]{:S(2)}, u32[]{:S(2)}) collective-permute-start(bf16[192,1024]{1,0:T(8,128)(2,1)} %get-tuple-element.225), channel_id=1, source_target_pairs={{0,16},{4,20},{8,24},{12,28},{16,0},{20,4},{24,8},{28,12},{1,17},{... | collective-permute-start | bytes 1179656 | tf_op jit(solution)/shard_map/ppermute | solution.py:288
  635.8 69.2 %collective-permute-start.56 = (bf16[192,1024]{1,0:T(8,128)(2,1)S(1)}, bf16[192,1024]{1,0:T(8,128)(2,1)}, u32[]{:S(2)}, u32[]{:S(2)}) collective-permute-start(bf16[192,1024]{1,0:T(8,128)(2,1)S(1)} %get-tuple-element.223), channel_id=1, source_target_pairs={{0,8},{4,12},{8,16},{12,20},{16,24},{20,28},{24,0},{28,4},{1,9},{5... | collective-permute-start | bytes 1179656 | tf_op jit(solution)/shard_map/ppermute | solution.py:288
  651.2 138.0 %collective-permute-start.25 = (bf16[512,1536]{1,0:T(8,128)(2,1)}, bf16[512,1536]{1,0:T(8,128)(2,1)}, u32[]{:S(2)}, u32[]{:S(2)}) collective-permute-start(bf16[512,1536]{1,0:T(8,128)(2,1)} %pad_maximum_fusion.5), channel_id=1, source_target_pairs={{0,1},{1,0},{2,3},{3,2},{4,5},{5,4},{6,7},{7,6},{8,9},{9,8},{10,11... | collective-permute-start | bytes 4718600 | tf_op jit(solution)/shard_map/ppermute | solution.py:292
  700.6 66.4 %collective-permute-start.61 = (bf16[192,1024]{1,0:T(8,128)(2,1)S(1)}, bf16[192,1024]{1,0:T(8,128)(2,1)S(1)}, u32[]{:S(2)}, u32[]{:S(2)}) collective-permute-start(bf16[192,1024]{1,0:T(8,128)(2,1)S(1)} %get-tuple-element.222), channel_id=1, source_target_pairs={{0,16},{4,20},{8,24},{12,28},{16,0},{20,4},{24,8},{28,12},{1,17},{... | collective-permute-start | bytes 1179656 | tf_op jit(solution)/shard_map/ppermute | solution.py:288
  704.3 65.4 %collective-permute-start.60 = (bf16[192,1024]{1,0:T(8,128)(2,1)S(1)}, bf16[192,1024]{1,0:T(8,128)(2,1)S(1)}, u32[]{:S(2)}, u32[]{:S(2)}) collective-permute-start(bf16[192,1024]{1,0:T(8,128)(2,1)S(1)} %get-tuple-element.220), channel_id=1, source_target_pairs={{0,8},{4,12},{8,16},{12,20},{16,24},{20,28},{24,0},{28,4},{1,9},{5... | collective-permute-start | bytes 1179656 | tf_op jit(solution)/shard_map/ppermute | solution.py:288
  705.0 67.1 %collective-permute-start.66 = (bf16[192,1024]{1,0:T(8,128)(2,1)S(1)}, bf16[192,1024]{1,0:T(8,128)(2,1)S(1)}, u32[]{:S(2)}, u32[]{:S(2)}) collective-permute-start(bf16[192,1024]{1,0:T(8,128)(2,1)S(1)} %get-tuple-element.218), channel_id=1, source_target_pairs={{0,24},{4,28},{8,0},{12,4},{16,8},{20,12},{24,16},{28,20},{1,25},{... | collective-permute-start | bytes 1179656 | tf_op jit(solution)/shard_map/ppermute | solution.py:288
  718.3 69.1 %collective-permute-start.65 = (bf16[192,1024]{1,0:T(8,128)(2,1)S(1)}, bf16[192,1024]{1,0:T(8,128)(2,1)S(1)}, u32[]{:S(2)}, u32[]{:S(2)}) collective-permute-start(bf16[192,1024]{1,0:T(8,128)(2,1)S(1)} %get-tuple-element.219), channel_id=1, source_target_pairs={{0,16},{4,20},{8,24},{12,28},{16,0},{20,4},{24,8},{28,12},{1,17},{... | collective-permute-start | bytes 1179656 | tf_op jit(solution)/shard_map/ppermute | solution.py:288
  919.2 37.1 %collective-permute-start.47 = (bf16[4,192,768]{2,1,0:T(8,128)(2,1)S(1)}, bf16[4,192,768]{2,1,0:T(8,128)(2,1)}, u32[]{:S(2)}, u32[]{:S(2)}) collective-permute-start(bf16[4,192,768]{2,1,0:T(8,128)(2,1)S(1)} %dynamic-slice_bitcast_fusion.8), channel_id=1, source_target_pairs={{0,4},{4,0},{8,12},{12,8},{16,20},{20,16},{24,28},{28,24},{1,5},{5... | collective-permute-start | bytes 3538952 | tf_op jit(solution)/shard_map/ppermute | solution.py:292
  975.9 83.6 %collective-permute-start.54 = (bf16[192,768]{1,0:T(8,128)(2,1)}, bf16[192,768]{1,0:T(8,128)(2,1)}, u32[]{:S(2)}, u32[]{:S(2)}) collective-permute-start(bf16[192,768]{1,0:T(8,128)(2,1)} %get-tuple-element.236), channel_id=1, source_target_pairs={{0,24},{4,28},{8,0},{12,4},{16,8},{20,12},{24,16},{28,20},{1,25},{... | collective-permute-start | bytes 884744 | tf_op jit(solution)/shard_map/ppermute | solution.py:288
  976.0 93.2 %collective-permute-start.53 = (bf16[192,768]{1,0:T(8,128)(2,1)}, bf16[192,768]{1,0:T(8,128)(2,1)}, u32[]{:S(2)}, u32[]{:S(2)}) collective-permute-start(bf16[192,768]{1,0:T(8,128)(2,1)} %get-tuple-element.237), channel_id=1, source_target_pairs={{0,16},{4,20},{8,24},{12,28},{16,0},{20,4},{24,8},{28,12},{1,17},{... | collective-permute-start | bytes 884744 | tf_op jit(solution)/shard_map/ppermute | solution.py:288
  986.7 82.8 %collective-permute-start.52 = (bf16[192,768]{1,0:T(8,128)(2,1)}, bf16[192,768]{1,0:T(8,128)(2,1)}, u32[]{:S(2)}, u32[]{:S(2)}) collective-permute-start(bf16[192,768]{1,0:T(8,128)(2,1)} %get-tuple-element.235), channel_id=1, source_target_pairs={{0,8},{4,12},{8,16},{12,20},{16,24},{20,28},{24,0},{28,4},{1,9},{5... | collective-permute-start | bytes 884744 | tf_op jit(solution)/shard_map/ppermute | solution.py:288
  (152 other events, 2216.7 us)
Sparse Core Ops, SparseCore 0:
  156.3 78.2 all-gather.5
  699.4 71.7 all-gather.7

commit v3 on v2

v3 whole, which is shorter than its diff:
```python
import functools

import jax
import jax.numpy as jnp
from jax import lax
from jax.experimental import pallas as pl
from jax.experimental.pallas import tpu as pltpu
from jax.sharding import PartitionSpec as P

EPS = 1e-06
LOG2E = 1.4426950408889634
LN2 = 0.6931471805599453
STOP = 1e30
LANES = 128
BF = jnp.bfloat16
F32 = jnp.float32


def shifted(value, axis, steps):
    count = lax.axis_size(axis)
    initial, last = (max(0, -steps), min(count, count - steps))
    return lax.ppermute(value, axis, [(source, source + steps) for source in range(initial, last)])


def norm_rows(values, gain_vec):
    inv_rms = lax.rsqrt(jnp.mean(values * values, axis=-1, keepdims=True) + EPS)
    return (values * inv_rms * gain_vec, inv_rms)


def norm_back(values, inv_rms, gain_vec, grad_rows):
    normed = values * inv_rms
    gain_grad = jnp.sum(grad_rows * normed, axis=0)
    scaled = grad_rows * gain_vec
    value_grad = inv_rms * (scaled - normed * jnp.mean(scaled * normed, axis=-1, keepdims=True))
    return (value_grad, gain_grad)


def silu_slope(values):
    logistic = jax.nn.sigmoid(values)
    return logistic * (1.0 + values * (1.0 - logistic))


GROUP = 4


def at_rows(index, size):
    return pl.ds(pl.multiple_of(index * size, size), size)


def spread(parts_ref, states, target):
    rows = parts_ref.shape[0]
    wide = 2 * LANES
    chunk = 256 if rows % 256 == 0 else rows
    source = lax.broadcasted_iota(jnp.int32, (LANES, wide), 0)
    half = lax.broadcasted_iota(jnp.int32, (LANES, wide), 1) // LANES
    columns = 2 * states

    def one(pair, carry):
        column = pair * 2 + half
        third = source % columns == column
        hot = jnp.where((source < 3 * columns) & third, 1.0, 0.0)
        stop = (column == columns) & (source == 3 * columns)
        hot = jnp.where(stop, 1.0, hot).astype(BF)
        for k in range(rows // chunk):
            target[pl.ds(k * chunk, chunk), at_rows(pair, wide)] = jnp.dot(
                parts_ref[pl.ds(k * chunk, chunk), :], hot, preferred_element_type=F32
            )
        return carry

    lax.fori_loop(0, states + 1, one, 0)


def group_tokens(ref, group, lanes, seqs):
    both = ref[at_rows(group, GROUP * seqs), lanes].astype(F32)
    return [both[k * seqs : (k + 1) * seqs] for k in range(GROUP)]


class Exchange:
    def __init__(self, count, forward, arrays, sems):
        place = lax.axis_index("seq")
        self.around = count // 2
        self.low, self.high = lax.rem(place, 2), place // 2
        self.place = place
        self.forward = forward
        self.arrays = arrays
        self.sems = sems
        self.mate = self.high * 2 + 1 - self.low

    def copies(self, steps, tile, source, device, kind):
        send, recv = self.sems[2 * kind], self.sems[2 * kind + 1]
        lanes = at_rows(tile, LANES)
        return [
            pltpu.make_async_remote_copy(
                src_ref=array.at[source, :, lanes],
                dst_ref=array.at[source, :, lanes],
                send_sem=send.at[k, steps, tile],
                recv_sem=recv.at[k, steps, tile],
                device_id={"seq": device},
                device_id_type=pl.DeviceIdType.MESH,
            )
            for k, array in enumerate(self.arrays)
        ]

    def away(self, steps):
        return self.high + steps if self.forward else self.high - steps

    def inside(self, pair):
        return pair < self.around if self.forward else pair >= 0

    def behind(self, steps):
        return self.high - steps if self.forward else self.high + steps

    def has_behind(self, steps):
        pair = self.behind(steps)
        return pair >= 0 if self.forward else pair < self.around

    def gives(self):
        return self.low == (0 if self.forward else 1)

    def hop(self, steps, tile):
        pair = jnp.clip(self.away(steps), 0, self.around - 1)
        return self.copies(steps, tile, self.place, pair * 2 + self.low, 0)

    def relay(self, steps, tile):
        pair = jnp.clip(self.behind(steps), 0, self.around - 1)
        return self.copies(steps, tile, pair * 2 + self.low, self.mate, 1)

    def start(self, tile):
        for steps in range(1, self.around):

            @pl.when(self.inside(self.away(steps)))
            def _():
                for copy in self.hop(steps, tile):
                    copy.start()

        @pl.when(self.gives())
        def _():
            for copy in self.relay(0, tile):
                copy.start()

    def pass_on(self, tile):
        for steps in range(1, self.around):

            @pl.when(self.has_behind(steps))
            def _():
                for copy in self.hop(steps, tile):
                    copy.wait_recv()
                for copy in self.relay(steps, tile):
                    copy.start()

    def arrive(self, tile):
        @pl.when(jnp.logical_not(self.gives()))
        def _():
            for copy in self.relay(0, tile):
                copy.wait_recv()

        for steps in range(1, self.around):

            @pl.when(self.has_behind(steps))
            def _():
                for copy in self.relay(steps, tile):
                    copy.wait_recv()

    def finish(self, tile):
        @pl.when(self.gives())
        def _():
            for copy in self.relay(0, tile):
                copy.wait_send()

        for steps in range(1, self.around):

            @pl.when(self.inside(self.away(steps)))
            def _():
                for copy in self.hop(steps, tile):
                    copy.wait_send()

            @pl.when(self.has_behind(steps))
            def _():
                for copy in self.relay(steps, tile):
                    copy.wait_send()


def chained(state, block_ref, sums_ref, rate_ref, source, lanes, seqs):
    total = sums_ref[source, :, lanes]
    block = block_ref[source, :, lanes].astype(F32)
    after = []
    for n in range(len(state)):
        decay = jnp.exp2(total * rate_ref[pl.ds(n * seqs, seqs), lanes])
        after.append(decay * state[n] + block[n * seqs : (n + 1) * seqs])
    return tuple(after)


def state_blocks(ref, lanes, seqs, states):
    return tuple(ref[pl.ds(n * seqs, seqs), lanes] for n in range(states))


def put_blocks(ref, lead, lanes, blocks):
    stacked = jnp.concatenate(blocks, axis=0)
    if lead is None:
        ref[:, lanes] = stacked.astype(ref.dtype)
    else:
        ref[lead, :, lanes] = stacked.astype(ref.dtype)


def entry_kernel(
    count, seqs, states, parts_ref, step_ref, u_ref, rate_ref, start_ref, sum_ref, *scratch
):
    spread_ref, ends, sums, *sems = scratch
    rows, channels = step_ref.shape
    tokens, tiles = rows // seqs, channels // LANES
    stop_lanes = pl.ds(2 * states * LANES, LANES)
    exchange = Exchange(count, True, (ends, sums), sems)
    place = exchange.place
    zero = jnp.zeros((seqs, LANES), F32)
    greet_pairs(count)
    spread(parts_ref, states, spread_ref)

    def local(tile, carry):
        lanes = at_rows(tile, LANES)

        def one(group, carry):
            state, total = carry
            us = group_tokens(u_ref, group, lanes, seqs)
            for k in range(GROUP):
                here = at_rows(group * GROUP + k, seqs)
                step = step_ref[here, lanes]
                drive = step * us[k]
                stop = step + spread_ref[here, stop_lanes]
                total = total + stop
                fresh = []
                for n in range(states):
                    decay = jnp.exp2(stop * rate_ref[pl.ds(n * seqs, seqs), lanes])
                    b_one = spread_ref[here, pl.ds(n * LANES, LANES)]
                    fresh.append(decay * state[n] + drive * b_one)
                state = tuple(fresh)
            return state, total

        state, total = lax.fori_loop(0, tokens // GROUP, one, ((zero,) * states, zero))
        put_blocks(ends, place, lanes, state)
        sums[place, :, lanes] = total
        exchange.start(tile)
        return carry

    lax.fori_loop(0, tiles, local, 0)
    finish_exchange(exchange, tiles, lambda first, lanes: lax.fori_loop(
        0,
        place,
        lambda source, state: chained(state, ends, sums, rate_ref, source, lanes, seqs),
        first,
    ), start_ref, states, zero)
    sum_ref[...] = sums[place]


def finish_exchange(exchange, tiles, chain, target_ref, states, zero):
    def pass_on(tile, carry):
        exchange.pass_on(tile)
        return carry

    lax.fori_loop(0, tiles, pass_on, 0)

    def take(tile, carry):
        lanes = at_rows(tile, LANES)
        exchange.arrive(tile)
        put_blocks(target_ref, None, lanes, chain((zero,) * states, lanes))
        return carry

    lax.fori_loop(0, tiles, take, 0)

    def finish(tile, carry):
        exchange.finish(tile)
        return carry

    lax.fori_loop(0, tiles, finish, 0)


def forward_kernel(
    count,
    seqs,
    states,
    parts_ref,
    step_ref,
    u_ref,
    rate_ref,
    start_ref,
    block_ref,
    y_ref,
    gathered_ref,
    *scratch,
):
    spread_ref, *sems = scratch
    gather = BlockGather(count, block_ref, gathered_ref, sems)
    rows, channels = step_ref.shape
    tokens, tiles = rows // seqs, channels // LANES
    stop_lanes = pl.ds(2 * states * LANES, LANES)
    zero = jnp.zeros((seqs, LANES), F32)
    greet_pairs(count)
    gather.start()
    spread(parts_ref, states, spread_ref)

    def whole(tile, carry):
        lanes = at_rows(tile, LANES)

        def one(group, state):
            us = group_tokens(u_ref, group, lanes, seqs)
            for k in range(GROUP):
                here = at_rows(group * GROUP + k, seqs)
                step = step_ref[here, lanes]
                drive = step * us[k]
                stop = step + spread_ref[here, stop_lanes]
                fresh = []
                out = zero
                for n in range(states):
                    decay = jnp.exp2(stop * rate_ref[pl.ds(n * seqs, seqs), lanes])
                    b_one = spread_ref[here, pl.ds(n * LANES, LANES)]
                    value = decay * state[n] + drive * b_one
                    out = out + value * spread_ref[here, pl.ds((states + n) * LANES, LANES)]
                    fresh.append(value)
                y_ref[here, lanes] = out
                state = tuple(fresh)
            return state

        lax.fori_loop(0, tokens // GROUP, one, state_blocks(start_ref, lanes, seqs, states))
        for piece in range(gather.pieces):
            if 3 * piece + 2 < tiles:

                @pl.when(tile == 3 * piece + 2)
                def _():
                    gather.relay(piece)

        return carry

    lax.fori_loop(0, tiles, whole, 0)
    for piece in range(gather.pieces):
        if 3 * piece + 2 >= tiles:
            gather.relay(piece)
    gather.finish()


def adjoint_kernel(
    count, seqs, states, parts_ref, step_ref, dy_ref, rate_ref, sum_ref, last_ref, *scratch
):
    spread_ref, ends, sums, *sems = scratch
    rows, channels = step_ref.shape
    tokens, tiles = rows // seqs, channels // LANES
    groups = tokens // GROUP
    stop_lanes = pl.ds(2 * states * LANES, LANES)
    exchange = Exchange(count, False, (ends, sums), sems)
    place = exchange.place
    zero = jnp.zeros((seqs, LANES), F32)
    greet_pairs(count)
    spread(parts_ref, states, spread_ref)

    def own(tile, carry):
        lanes = at_rows(tile, LANES)

        def one(back, grads):
            group = groups - 1 - back
            for k in reversed(range(GROUP)):
                here = at_rows(group * GROUP + k, seqs)
                stop = step_ref[here, lanes] + spread_ref[here, stop_lanes]
                dy = dy_ref[here, lanes]
                fresh = []
                for n in range(states):
                    decay = jnp.exp2(stop * rate_ref[pl.ds(n * seqs, seqs), lanes])
                    c_one = spread_ref[here, pl.ds((states + n) * LANES, LANES)]
                    fresh.append(decay * (grads[n] + dy * c_one))
                grads = tuple(fresh)
            return grads

        put_blocks(ends, place, lanes, lax.fori_loop(0, groups, one, (zero,) * states))
        sums[place, :, lanes] = sum_ref[:, lanes]
        exchange.start(tile)
        return carry

    lax.fori_loop(0, tiles, own, 0)
    finish_exchange(exchange, tiles, lambda first, lanes: lax.fori_loop(
        0,
        count - 1 - place,
        lambda hop, state: chained(state, ends, sums, rate_ref, count - 1 - hop, lanes, seqs),
        first,
    ), last_ref, states, zero)


def backward_kernel(
    count,
    seqs,
    states,
    parts_ref,
    step_ref,
    u_ref,
    dy_ref,
    rate_ref,
    start_ref,
    last_ref,
    *refs,
):
    kinds = (len(refs) - 16) // 3
    grad_refs, refs = refs[:kinds], refs[kinds:]
    du_ref, dpre_ref, dbc_ref, dlog_ref, dbias_ref, *refs = refs
    given_refs, came_refs, scratch = refs[:kinds], refs[kinds : 2 * kinds], refs[2 * kinds :]
    spread_ref, held, acc, *scratch = scratch
    rows, channels = step_ref.shape
    tokens, tiles = rows // seqs, channels // LANES
    groups = tokens // GROUP
    stop_lanes = pl.ds(2 * states * LANES, LANES)
    place = lax.axis_index("seq")
    low, high = lax.rem(place, 2), place // 2
    zero = jnp.zeros((seqs, LANES), F32)
    greet_pairs(count)

    scatter = PairScatter(count, grad_refs, given_refs, came_refs, scratch)
    scatter.start()
    spread(parts_ref, states, spread_ref)

    def clear(row, carry):
        acc[at_rows(row, seqs), :] = jnp.zeros((seqs, acc.shape[1]), F32)
        return carry

    lax.fori_loop(0, tokens, clear, 0)

    def whole(tile, carry):
        lanes = at_rows(tile, LANES)

        def again(group, state):
            us = group_tokens(u_ref, group, lanes, seqs)
            for k in range(GROUP):
                token = group * GROUP + k
                here = at_rows(token, seqs)
                step = step_ref[here, lanes]
                drive = step * us[k]
                stop = step + spread_ref[here, stop_lanes]
                fresh = []
                for n in range(states):
                    held[token * states + n] = state[n]
                    decay = jnp.exp2(stop * rate_ref[pl.ds(n * seqs, seqs), lanes])
                    b_one = spread_ref[here, pl.ds(n * LANES, LANES)]
                    fresh.append(decay * state[n] + drive * b_one)
                state = tuple(fresh)
            return state

        state = lax.fori_loop(0, groups, again, state_blocks(start_ref, lanes, seqs, states))
        for n in range(states):
            held[tokens * states + n] = state[n]
        for k in range(tiles):

            @pl.when(tile == k)
            def _():
                scatter.advance(2 * k)

        grads = state_blocks(last_ref, lanes, seqs, states)

        def one(back, carry):
            grads, logs, bias = carry
            group = groups - 1 - back
            us = group_tokens(u_ref, group, lanes, seqs)
            pres = [None] * GROUP
            for k in reversed(range(GROUP)):
                token = group * GROUP + k
                here = at_rows(token, seqs)
                step = step_ref[here, lanes]
                dy = dy_ref[here, lanes]
                drive = step * us[k]
                stop = step + spread_ref[here, stop_lanes]
                fresh, fresh_logs = [], []
                on_b, on_rate = zero, zero
                for n in range(states):
                    at = token * states + n
                    on_lanes = pl.ds(n * LANES, LANES)
                    other_lanes = pl.ds((states + n) * LANES, LANES)
                    rate = rate_ref[pl.ds(n * seqs, seqs), lanes]
                    decay = jnp.exp2(stop * rate)
                    lam = grads[n] + dy * spread_ref[here, other_lanes]
                    carried = lam * decay
                    fresh.append(carried)
                    kept = carried * held[at]
                    on_b = on_b + lam * spread_ref[here, on_lanes]
                    on_rate = on_rate + kept * rate
                    fresh_logs.append(logs[n] + kept * step)
                    acc[here, on_lanes] = acc[here, on_lanes] + lam * drive
                    acc[here, other_lanes] = acc[here, other_lanes] + dy * held[at + states]
                du_ref[here, lanes] = step * on_b
                series = step * (1.0 - step * (0.5 - step * (1.0 / 6.0 - step * (1.0 / 24.0))))
                slope = jnp.where(step < 0.05, series, 1.0 - jnp.exp2(step * (-LOG2E)))
                pres[k] = (on_rate * LN2 + us[k] * on_b) * slope
                bias = bias + pres[k]
                grads, logs = tuple(fresh), tuple(fresh_logs)
            dpre_ref[at_rows(group, GROUP * seqs), lanes] = jnp.concatenate(pres, 0).astype(BF)
            return grads, logs, bias

        grads, logs, bias = lax.fori_loop(0, groups, one, (grads, (zero,) * states, zero))
        dlog_ref[:, lanes] = jnp.concatenate(
            [jnp.sum(log, axis=0, keepdims=True) for log in logs], axis=0
        )
        dbias_ref[:, lanes] = bias
        for k in range(tiles):

            @pl.when(tile == k)
            def _():
                scatter.advance(2 * k + 1)

        return carry

    lax.fori_loop(0, tiles, whole, 0)

    wide = 2 * LANES
    chunk = 256 if rows % 256 == 0 else rows
    target = lax.broadcasted_iota(jnp.int32, (wide, LANES), 1)
    half = lax.broadcasted_iota(jnp.int32, (wide, LANES), 0) // LANES
    dbc_ref[...] = jnp.zeros(dbc_ref.shape, F32)

    def reduce(pair, carry):
        hot = jnp.where(target == pair * 2 + half, 1.0, 0.0).astype(BF)
        for k in range(rows // chunk):
            here = pl.ds(k * chunk, chunk)
            values = acc[here, at_rows(pair, wide)]
            main = values.astype(BF)
            rest = (values - main.astype(F32)).astype(BF)
            dbc_ref[here, :] += jnp.dot(main, hot, preferred_element_type=F32) + jnp.dot(
                rest, hot, preferred_element_type=F32
            )
        return carry

    lax.fori_loop(0, states, reduce, 0)

    for turn in range(2 * tiles, scatter.turns):
        scatter.advance(turn)
    scatter.finish()


class PairScatter:
    def __init__(self, count, grads, given, came, scratch):
        place = lax.axis_index("seq")
        self.around = count // 2
        self.low, self.high = lax.rem(place, 2), place // 2
        self.grads, self.given, self.came = grads, given, came
        self.mine_buf, self.given_buf, self.sum_buf = scratch[:3]
        self.swap_send, self.swap_recv, self.hop_send, self.hop_recv, self.load_sem = scratch[3:]
        self.items = [(k, steps) for k in range(len(grads)) for steps in range(1, self.around)]
        self.turns = len(self.items) + 1

    def pair(self, steps):
        return lax.rem(self.high + steps, self.around)

    def swap(self, kind, steps):
        return pltpu.make_async_remote_copy(
            src_ref=self.grads[kind].at[self.pair(steps), 1 - self.low],
            dst_ref=self.given[kind].at[steps],
            send_sem=self.swap_send.at[kind, steps],
            recv_sem=self.swap_recv.at[kind, steps],
            device_id={"seq": self.high * 2 + 1 - self.low},
            device_id_type=pl.DeviceIdType.MESH,
        )

    def hop(self, item):
        kind, steps = self.items[item]
        wide = self.grads[kind].shape[-1]
        return pltpu.make_async_remote_copy(
            src_ref=self.sum_buf.at[item % 2, :, pl.ds(0, wide)],
            dst_ref=self.came[kind].at[steps - 1],
            send_sem=self.hop_send.at[kind, steps],
            recv_sem=self.hop_recv.at[kind, steps],
            device_id={"seq": self.pair(steps) * 2 + self.low},
            device_id_type=pl.DeviceIdType.MESH,
        )

    def loads(self, item):
        kind, steps = self.items[item]
        lanes = pl.ds(0, self.grads[kind].shape[-1])
        return [
            pltpu.make_async_copy(
                self.grads[kind].at[self.pair(steps), self.low],
                self.mine_buf.at[item % 2, :, lanes],
                self.load_sem.at[item % 2, 0],
            ),
            pltpu.make_async_copy(
                self.given[kind].at[steps],
                self.given_buf.at[item % 2, :, lanes],
                self.load_sem.at[item % 2, 1],
            ),
        ]

    def start(self):
        for kind, steps in self.items:
            self.swap(kind, steps).start()
        for kind in range(len(self.grads)):
            self.swap(kind, 0).start()

    def advance(self, turn):
        if turn < len(self.items):
            self.swap(*self.items[turn]).wait_recv()
            for load in self.loads(turn):
                load.start()
        item = turn - 1
        if 0 <= item < len(self.items):
            for load in self.loads(item):
                load.wait()
            if item >= 2:
                self.hop(item - 2).wait_send()
            wide = self.grads[self.items[item][0]].shape[-1]
            rows = self.mine_buf.shape[1]

            def add(row, carry):
                here = at_rows(row, 16)
                lanes = pl.ds(0, wide)
                total = self.mine_buf[item % 2, here, lanes].astype(F32) + self.given_buf[
                    item % 2, here, lanes
                ].astype(F32)
                self.sum_buf[item % 2, here, lanes] = total.astype(BF)
                return carry

            lax.fori_loop(0, rows // 16, add, 0)
            self.hop(item).start()

    def finish(self):
        for item in range(max(0, len(self.items) - 2), len(self.items)):
            self.hop(item).wait_send()
        for item in range(len(self.items)):
            self.hop(item).wait_recv()
            self.swap(*self.items[item]).wait_send()
        for kind in range(len(self.grads)):
            self.swap(kind, 0).wait()


def scatter_scratch(count, grads):
    rows = grads[0].shape[2]
    wide = max(grad.shape[3] for grad in grads)
    sems = pltpu.SemaphoreType.DMA((len(grads), count // 2))
    return [pltpu.VMEM((2, rows, wide), BF)] * 3 + [sems] * 4 + [pltpu.SemaphoreType.DMA((2, 2))]


def exchange_scratch(count, seqs, states, channels):
    sems = pltpu.SemaphoreType.DMA((2, count // 2, channels // LANES))
    return [
        pltpu.VMEM((count, states * seqs, channels), BF),
        pltpu.VMEM((count, seqs, channels), F32),
    ] + [sems] * 4


def state_call(body, ident, seqs, states, ins, outs, scratch, ops, hosted):
    count = lax.axis_size("seq")
    rows, channels = ins[1].shape
    in_vmem = pl.BlockSpec(memory_space=pltpu.VMEM)
    anywhere = pl.BlockSpec(memory_space=pl.ANY)
    return pl.pallas_call(
        functools.partial(body, count, seqs, states),
        in_specs=[in_vmem] * (len(ins) - hosted[0]) + [anywhere] * hosted[0],
        out_specs=tuple([in_vmem] * (len(outs) - hosted[1]) + [anywhere] * hosted[1]),
        out_shape=tuple(outs),
        scratch_shapes=[pltpu.VMEM((rows, 2 * (states + 1) * LANES), F32)] + scratch,
        compiler_params=pltpu.CompilerParams(
            collective_id=ident, has_side_effects=True, vmem_limit_bytes=62 * 1024 * 1024
        ),
        cost_estimate=pl.CostEstimate(
            flops=ops * rows * channels * states,
            bytes_accessed=16 * 1024 * 1024,
            transcendentals=0,
        ),
    )(*ins)


class BlockGather:
    def __init__(self, count, source, target, sems):
        place = lax.axis_index("seq")
        self.around = count // 2
        self.low, self.high = lax.rem(place, 2), place // 2
        self.place = place
        self.source, self.target = source, target
        self.hop_send, self.hop_recv, self.swap_send, self.swap_recv, self.local_sem = sems
        self.mate = self.high * 2 + 1 - self.low
        self.pieces = pieces_of(source.shape[-1])

    def pair(self, steps):
        return lax.rem(self.high + steps + self.around, self.around) * 2 + self.low

    def lanes(self, piece):
        size = self.source.shape[-1] // self.pieces
        return pl.ds(piece * size, size)

    def local(self):
        return pltpu.make_async_copy(self.source, self.target.at[self.place], self.local_sem.at[0])

    def hop(self, piece, steps):
        return pltpu.make_async_remote_copy(
            src_ref=self.source.at[:, self.lanes(piece)],
            dst_ref=self.target.at[self.place, :, self.lanes(piece)],
            send_sem=self.hop_send.at[piece, steps],
            recv_sem=self.hop_recv.at[piece, steps],
            device_id={"seq": self.pair(steps)},
            device_id_type=pl.DeviceIdType.MESH,
        )

    def swap(self, piece, steps):
        block = self.target.at[self.pair(-steps), :, self.lanes(piece)]
        return pltpu.make_async_remote_copy(
            src_ref=block if steps else self.source.at[:, self.lanes(piece)],
            dst_ref=block,
            send_sem=self.swap_send.at[piece, steps],
            recv_sem=self.swap_recv.at[piece, steps],
            device_id={"seq": self.mate},
            device_id_type=pl.DeviceIdType.MESH,
        )

    def start(self):
        self.local().start()
        for piece in range(self.pieces):
            for steps in range(1, self.around):
                self.hop(piece, steps).start()
        for piece in range(self.pieces):
            self.swap(piece, 0).start()

    def relay(self, piece):
        for steps in range(1, self.around):
            self.hop(piece, steps).wait_recv()
            self.swap(piece, steps).start()

    def finish(self):
        self.local().wait()
        for piece in range(self.pieces):
            for steps in range(1, self.around):
                self.hop(piece, steps).wait_send()
            for steps in range(self.around):
                self.swap(piece, steps).wait()


def pieces_of(width):
    for size in (384, 256):
        if width % size == 0:
            return width // size
    return 1


def gather_sems(around, width):
    pieces = pieces_of(width)
    return [pltpu.SemaphoreType.DMA((pieces, around))] * 4 + [pltpu.SemaphoreType.DMA((1,))]


def greet_pairs(count, heads=False):
    place = lax.axis_index("seq")
    around = count // 2
    low, high = lax.rem(place, 2), place // 2
    barrier = pltpu.get_barrier_semaphore()
    peers = [lax.rem(high + steps, around) * 2 + low for steps in range(1, around)]
    peers = [{"seq": device} for device in peers + [high * 2 + 1 - low]]
    if heads:
        head = lax.axis_index("head")
        low, high = lax.rem(head, 2), head // 2
        peers += [{"head": high * 2 + 1 - low}, {"head": 2 - 2 * high + low}]
    for device in peers:
        pl.semaphore_signal(barrier, inc=1, device_id=device, device_id_type=pl.DeviceIdType.MESH)
    pl.semaphore_wait(barrier, len(peers))


class HeadSum:
    def __init__(self, part, half, give, take, whole, sems):
        head = lax.axis_index("head")
        self.low, self.high = lax.rem(head, 2), head // 2
        self.near = {"head": self.high * 2 + 1 - self.low}
        self.far = {"head": 2 - 2 * self.high + self.low}
        self.part, self.half, self.give, self.take, self.whole = part, half, give, take, whole
        self.sems = sems
        self.size = half.shape[1]

    def copy(self, source, target, kind, chunk, device):
        return pltpu.make_async_remote_copy(
            src_ref=source,
            dst_ref=target,
            send_sem=self.sems.at[kind, 0, chunk],
            recv_sem=self.sems.at[kind, 1, chunk],
            device_id=device,
            device_id_type=pl.DeviceIdType.MESH,
        )

    def rows(self, chunk, bit):
        start = pl.multiple_of((chunk * 2 + bit) * self.size, self.size)
        return pl.ds(start, self.size)

    def own_rows(self, chunk):
        quarter = self.size // 2
        start = (chunk * 2 + self.low) * self.size + self.high * quarter
        return pl.ds(pl.multiple_of(start, quarter), quarter)

    def near_copy(self, chunk):
        return self.copy(
            self.part.at[self.rows(chunk, 1 - self.low)], self.half.at[chunk], 0, chunk, self.near
        )

    def far_copy(self, chunk):
        return self.copy(self.give.at[chunk], self.take.at[chunk], 1, chunk, self.far)

    def far_back(self, chunk):
        here = self.whole.at[self.own_rows(chunk)]
        return self.copy(here, here, 2, chunk, self.far)

    def near_back(self, chunk):
        here = self.whole.at[self.rows(chunk, self.low)]
        return self.copy(here, here, 3, chunk, self.near)

    def fold(self, chunk, kept):
        self.near_copy(chunk).wait_recv()
        quarter = self.size // 2
        base = (chunk * 2 + self.low) * self.size
        for mine in (False, True):
            bit = self.high if mine else 1 - self.high
            start = pl.multiple_of(bit * quarter, quarter)
            at = pl.multiple_of(base + bit * quarter, quarter)
            total = self.part[pl.ds(at, quarter), :].astype(F32)
            total = total + self.half[chunk, pl.ds(start, quarter), :].astype(F32)
            if mine:
                kept[chunk] = total
            else:
                self.give[chunk] = total.astype(BF)
                self.far_copy(chunk).start()

    def finish(self, chunk):
        for copy in (self.near_copy, self.far_copy, self.far_back, self.near_back):
            copy(chunk).wait_send()


def transposed_dot(left, right):
    return lax.dot_general(left, right, (((1,), (1,)), ((), ())), preferred_element_type=F32)


def ffn_kernel(count, chunks, hosted, *refs):
    g_ref, out_ref, x_ref, gain_ref, low_ref, dout_ref, *refs = refs
    ready, refs = refs[: 3 - hosted], refs[3 - hosted :]
    shards_in, refs = refs[:hosted], refs[hosted:]
    hidden_ref, norm_ref, act_ref, dgate_ref, dup_ref, dnorm_gain_ref, part_out_ref, *refs = refs
    dhidden_ref, dmix_ref, *refs = refs
    landed, refs = refs[:hosted], refs[hosted:]
    part_a, half_a, give_a, take_a, part_b, half_b, give_b, take_b, kept, *refs = refs
    sems_a, sems_b, *refs = refs
    gathers = [
        BlockGather(count, shards_in[k], landed[k], refs[5 * k : 5 * k + 5]) for k in range(hosted)
    ]
    gate_ref, up_ref, down_ref = list(ready) + list(landed)
    mix = HeadSum(part_a, half_a, give_a, take_a, norm_ref, sems_a)
    back = HeadSum(part_b, half_b, give_b, take_b, dmix_ref, sems_b)
    size = g_ref.shape[0] // chunks
    quarter = size // 4
    width = x_ref.shape[1]
    shard, units = gate_ref.shape[1:]
    greet_pairs(count, True)
    for gather in gathers:
        gather.start()
    relays = [(gather, piece) for gather in gathers for piece in range(gather.pieces)]
    fourth = -(-len(relays) // chunks)

    def project(chunk, carry):
        here = at_rows(chunk, size)
        part_a[here, :] = transposed_dot(g_ref[here, :], out_ref[...]).astype(BF)
        mix.near_copy(chunk).start()
        return carry

    lax.fori_loop(0, chunks, project, 0)

    def fold(chunk, carry):
        mix.fold(chunk, kept)
        return carry

    lax.fori_loop(0, chunks, fold, 0)

    def normalise(chunk, carry):
        mix.far_copy(chunk).wait_recv()
        here = at_rows(chunk, quarter)
        hidden = x_ref[here, :] + kept[chunk] + take_a[chunk].astype(F32)
        hidden_ref[here, :] = hidden
        scale = lax.rsqrt(jnp.mean(hidden * hidden, axis=1, keepdims=True) + EPS)
        norm_ref[mix.own_rows(chunk), :] = (hidden * scale * gain_ref[...]).astype(BF)
        mix.far_back(chunk).start()
        for k in range(chunks):
            if relays[k * fourth : (k + 1) * fourth]:

                @pl.when(chunk == k)
                def _():
                    for gather, piece in relays[k * fourth : (k + 1) * fourth]:
                        gather.relay(piece)

        return carry

    lax.fori_loop(0, chunks, normalise, 0)
    mix.far_back(0).wait_recv()
    mix.near_back(0).start()
    for gather in gathers:
        gather.finish()
    per_block = max(1, count // 4)
    wide = per_block * shard
    lanes_block = 256 if units % 256 == 0 else units

    def feed(chunk, carry):
        here = at_rows(chunk, size)

        @pl.when(chunk + 1 < chunks)
        def _():
            mix.far_back(chunk + 1).wait_recv()
            mix.near_back(chunk + 1).start()

        mix.near_back(chunk).wait_recv()
        rows = norm_ref[here, :]
        grads = low_ref[here, :]
        for k in range(units // lanes_block):
            lanes = pl.ds(k * lanes_block, lanes_block)
            block = lambda ref: ref[:, :, lanes].reshape(width, lanes_block)
            gate = jnp.dot(rows, block(gate_ref), preferred_element_type=F32)
            up = jnp.dot(rows, block(up_ref), preferred_element_type=F32)
            d_act = jnp.dot(grads, block(down_ref), preferred_element_type=F32)
            logistic = 1.0 / (1.0 + jnp.exp(-gate))
            silu = gate * logistic
            act_ref[here, lanes] = (silu * up).astype(BF)
            slope = logistic * (1.0 + gate * (1.0 - logistic))
            dgate_ref[here, lanes] = (d_act * up * slope).astype(BF)
            dup_ref[here, lanes] = (d_act * silu).astype(BF)
        for k in range(count // per_block):
            lanes = pl.ds(k * wide, wide)
            block = lambda ref: ref[pl.ds(k * per_block, per_block)].reshape(wide, units)
            total = transposed_dot(dgate_ref[here, :], block(gate_ref))
            total = total + transposed_dot(dup_ref[here, :], block(up_ref))
            part_b[here, lanes] = total.astype(BF)
        back.near_copy(chunk).start()
        for k in range(count // per_block):
            lanes = pl.ds(k * wide, wide)
            block = down_ref[pl.ds(k * per_block, per_block)].reshape(wide, units)
            part_out_ref[here, lanes] = transposed_dot(act_ref[here, :], block).astype(BF)

        @pl.when(chunk >= 1)
        def _():
            back.fold(chunk - 1, kept)

        return carry

    lax.fori_loop(0, chunks, feed, 0)
    back.fold(chunks - 1, kept)
    dnorm_gain_ref[...] = jnp.zeros(dnorm_gain_ref.shape, F32)

    def turn(chunk, carry):
        back.far_copy(chunk).wait_recv()
        here = at_rows(chunk, quarter)
        hidden = hidden_ref[here, :]
        scale = lax.rsqrt(jnp.mean(hidden * hidden, axis=1, keepdims=True) + EPS)
        normed = hidden * scale
        d_norm = kept[chunk] + take_b[chunk].astype(F32)
        dnorm_gain_ref[...] += jnp.sum(d_norm * normed, axis=0, keepdims=True)
        scaled = d_norm * gain_ref[...]
        shift = jnp.mean(scaled * normed, axis=1, keepdims=True)
        d_hidden = dout_ref[here, :] + scale * (scaled - normed * shift)
        dhidden_ref[here, :] = d_hidden
        dmix_ref[back.own_rows(chunk), :] = d_hidden.astype(BF)
        back.far_back(chunk).start()
        return carry

    lax.fori_loop(0, chunks, turn, 0)

    def spread_out(chunk, carry):
        back.far_back(chunk).wait_recv()
        back.near_back(chunk).start()
        return carry

    lax.fori_loop(0, chunks, spread_out, 0)

    def finish(chunk, carry):
        back.near_back(chunk).wait_recv()
        mix.finish(chunk)
        back.finish(chunk)
        return carry

    lax.fori_loop(0, chunks, finish, 0)


CHUNKS = 4


def ffn_call(g_low, out_t, x_own, gain, grad_low, dout_own, ready, waiting):
    count = lax.axis_size("seq")
    rows, width = grad_low.shape
    units = waiting[0].shape[1]
    chunk = rows // CHUNKS
    shape = jax.ShapeDtypeStruct
    in_vmem = pl.BlockSpec(memory_space=pltpu.VMEM)
    anywhere = pl.BlockSpec(memory_space=pl.ANY)
    sums = [
        pltpu.VMEM((rows, width), BF),
        pltpu.VMEM((CHUNKS, chunk // 2, width), BF),
        pltpu.VMEM((CHUNKS, chunk // 4, width), BF),
        pltpu.VMEM((CHUNKS, chunk // 4, width), BF),
    ]
    outs = [
        shape((rows // 4, width), F32),
        shape((rows, width), BF),
        shape((rows, units), BF),
        shape((rows, units), BF),
        shape((rows, units), BF),
        shape((1, width), F32),
        shape((rows, width), BF),
        shape((rows // 4, width), F32),
        shape((rows, width), BF),
    ]
    return pl.pallas_call(
        functools.partial(ffn_kernel, count, CHUNKS, len(waiting)),
        in_specs=[in_vmem] * (6 + len(ready)) + [anywhere] * len(waiting),
        out_specs=tuple([in_vmem] * len(outs)),
        out_shape=tuple(outs),
        scratch_shapes=[pltpu.VMEM((count,) + w.shape, BF) for w in waiting]
        + sums
        + sums
        + [pltpu.VMEM((CHUNKS, chunk // 4, width), F32)]
        + [pltpu.SemaphoreType.DMA((4, 2, CHUNKS))] * 2
        + [sem for w in waiting for sem in gather_sems(count // 2, w.shape[1])],
        compiler_params=pltpu.CompilerParams(
            collective_id=5, has_side_effects=True, vmem_limit_bytes=62 * 1024 * 1024
        ),
        cost_estimate=pl.CostEstimate(
            flops=14 * rows * width * units, bytes_accessed=40 * 1024 * 1024, transcendentals=0
        ),
    )(g_low, out_t, x_own, gain, grad_low, dout_own, *ready, *waiting)


def pairs_of(axis):
    return lax.axis_size(axis) // 2


def hop(value, steps):
    count = lax.axis_size("seq")
    return lax.ppermute(value, "seq", [(s, (s + 2 * steps) % count) for s in range(count)])


def swap(value, axis, bit):
    return lax.ppermute(value, axis, [(s, s ^ bit) for s in range(lax.axis_size(axis))])


def owner_blocks(value):
    return value.reshape((pairs_of("seq"), 2, -1) + value.shape[1:])


def scatter_half(blocks, theirs):
    place = lax.axis_index("seq")
    around = pairs_of("seq")
    low, high = place % 2, place // 2
    mine = lax.dynamic_index_in_dim(blocks, low, 1, False)
    half = mine.astype(F32) + theirs.astype(F32)
    total = lax.dynamic_index_in_dim(half, high, 0, False)
    half = half.astype(blocks.dtype)
    for steps in range(1, around):
        part = lax.dynamic_index_in_dim(half, (high + steps) % around, 0, False)
        total = total + hop(part, steps).astype(F32)
    return total


def scatter_rows(value, kind=BF):
    low = lax.axis_index("seq") % 2
    blocks = owner_blocks(value.astype(kind))
    theirs = lax.dynamic_index_in_dim(blocks, 1 - low, 1, False)
    return scatter_half(blocks, swap(theirs, "seq", 1))


def scatter_own(blocks, given, came):
    place = lax.axis_index("seq")
    own = blocks.reshape((-1,) + blocks.shape[2:])
    total = lax.dynamic_index_in_dim(own, place, 0, False).astype(F32) + given[0].astype(F32)
    for k in range(came.shape[0]):
        total = total + came[k].astype(F32)
    return total


def head_bits():
    return (lax.axis_size("head") - 1).bit_length()


def head_scatter(value):
    place = lax.axis_index("head")
    width = value.shape[1]
    value = value.reshape(CHUNKS, -1, width)
    for k in range(head_bits()):
        bit = place // 2**k % 2
        halves = value.astype(BF).reshape(CHUNKS, 2, -1, width)
        keep = lax.dynamic_index_in_dim(halves, bit, 1, False)
        send = lax.dynamic_index_in_dim(halves, 1 - bit, 1, False)
        value = keep.astype(F32) + swap(send, "head", 2**k).astype(F32)
    return value.reshape(-1, width)


def head_part(value):
    place = lax.axis_index("head")
    width = value.shape[1]
    value = value.reshape(CHUNKS, -1, width)
    for k in range(head_bits()):
        halves = value.reshape(CHUNKS, 2, -1, width)
        value = lax.dynamic_index_in_dim(halves, place // 2**k % 2, 1, False)
    return value.reshape(-1, width)


def head_gather(value):
    place = lax.axis_index("head")
    width = value.shape[1]
    value = value.reshape(CHUNKS, -1, width)
    for k in reversed(range(head_bits())):
        got = swap(value, "head", 2**k)
        first = place // 2**k % 2 == 0
        both = [jnp.where(first, value, got), jnp.where(first, got, value)]
        value = jnp.concatenate(both, axis=1)
    return value.reshape(-1, width)


def head_total(value, kind):
    for k in range(head_bits()):
        value = value.astype(kind)
        value = value.astype(F32) + swap(value, "head", 2**k).astype(F32)
    return value


def first_kernel(count, *refs):
    kinds = len(refs) // 7
    gathers = [
        BlockGather(count, refs[k], refs[kinds + k], refs[2 * kinds + 5 * k : 2 * kinds + 5 * k + 5])
        for k in range(kinds)
    ]
    greet_pairs(count)
    for gather in gathers:
        gather.start()
    for gather in gathers:
        for piece in range(gather.pieces):
            gather.relay(piece)
    for gather in gathers:
        gather.finish()


def first_gather(*values):
    count = lax.axis_size("seq")
    around = count // 2
    kinds = len(values)
    return pl.pallas_call(
        functools.partial(first_kernel, count),
        out_shape=tuple(jax.ShapeDtypeStruct((count,) + v.shape, v.dtype) for v in values),
        in_specs=[pl.BlockSpec(memory_space=pl.ANY)] * kinds,
        out_specs=tuple([pl.BlockSpec(memory_space=pl.ANY)] * kinds),
        scratch_shapes=[sem for v in values for sem in gather_sems(around, v.shape[-1])],
        compiler_params=pltpu.CompilerParams(collective_id=0, has_side_effects=True),
    )(*values)


def shards(
    x_in,
    seg_ids,
    norm1_gain,
    w_in_x,
    w_in_z,
    conv_w,
    conv_b,
    w_xproj,
    ssm_gain,
    w_dt,
    dt_bias,
    a_log,
    d_skip,
    w_out,
    norm2_gain,
    w_gate,
    w_up,
    w_down,
    d_out,
):
    count = lax.axis_size("seq")
    place = lax.axis_index("seq")
    seqs, tokens, width = x_in.shape
    rows = seqs * tokens
    taps = conv_w.shape[0]
    rank = w_dt.shape[0]
    states = a_log.shape[1]
    channels = w_in_x.shape[1]
    halo = (taps - 1) * seqs

    per = channels // count
    fields = [w_xproj, w_dt.T, a_log, conv_w.T, conv_b[:, None], dt_bias[:, None], d_skip[:, None]]
    starts = [0]
    for field in fields:
        starts.append(starts[-1] + field.shape[1])
    pack_width = -(-starts[-1] // LANES) * LANES
    gains = [norm1_gain, norm2_gain, ssm_gain]
    gain_starts = [0]
    for gain in gains:
        gain_starts.append(gain_starts[-1] + gain.shape[0])
    pack_rows = -(-(per + -(-gain_starts[-1] // pack_width)) // 16) * 16

    def pack(channel_fields, gain_fields):
        table = jnp.concatenate([f.astype(F32) for f in channel_fields], axis=1)
        table = jnp.pad(table, ((0, 0), (0, pack_width - table.shape[1])))
        table = table.reshape(-1, per, pack_width)
        rest = jnp.concatenate([g.astype(F32).reshape(table.shape[0], -1) for g in gain_fields], 1)
        rest = jnp.pad(rest, ((0, 0), (0, (pack_rows - per) * pack_width - rest.shape[1])))
        return jnp.concatenate([table, rest.reshape(-1, pack_rows - per, pack_width)], axis=1)

    def unpack(block):
        table = block[:, :per].reshape(-1, pack_width)
        rest = block[:, per:].reshape(block.shape[0], -1)
        return (
            [table[:, starts[k] : starts[k + 1]] for k in range(len(fields))],
            [rest[:, gain_starts[k] : gain_starts[k + 1]].reshape(-1) for k in range(len(gains))],
        )

    in_x_blocks, pack_blocks = first_gather(w_in_x.astype(BF), pack(fields, gains)[0].astype(BF))
    full_in_x = in_x_blocks.reshape(width, channels)
    fulls, full_gains = unpack(pack_blocks)
    full_xproj, w_dt_cols, full_a_log, conv_cols, conv_b_col, bias_col, skip_col = fulls
    full_w_dt = w_dt_cols.T
    full_conv_w = conv_cols.T
    full_conv_b, full_dt_bias, full_d_skip = conv_b_col[:, 0], bias_col[:, 0], skip_col[:, 0]
    full_norm1, full_norm2, full_ssm_gain = full_gains

    w_mix = jnp.concatenate([w_in_z.astype(BF), w_out.astype(BF).T], axis=1)
    w_wide = jnp.concatenate([w_gate.astype(BF), w_up.astype(BF)], axis=1)
    full_wide = lax.all_gather(w_wide, "seq", axis=0, tiled=True)
    hidden_units = w_gate.shape[1]

    norm1_vec = full_norm1.astype(F32)
    x_rows = x_in.transpose(1, 0, 2).reshape(rows, width).astype(F32)
    ids = seg_ids.T.reshape(rows)
    normed1, scale_one = norm_rows(x_rows, norm1_vec)
    x_norm = normed1.astype(BF)
    x_inner = jnp.dot(x_norm, full_in_x, preferred_element_type=F32).astype(BF)
    prev_tail, prev_ids = shifted((x_inner[rows - halo :], ids[rows - halo :]), "seq", 1)
    extended = jnp.concatenate([prev_tail, x_inner], axis=0).astype(F32)
    ext_ids = jnp.concatenate([prev_ids, ids])
    conv_weight = full_conv_w.astype(F32)
    x_conv = full_conv_b.astype(F32)[None, :]
    same_docs = []
    for offset in range(taps):
        first = (taps - 1 - offset) * seqs
        same = (ext_ids[first : first + rows] == ids).astype(F32)[:, None]
        same_docs.append(same)
        x_conv = x_conv + conv_weight[offset] * extended[first : first + rows] * same
    u_low = jax.nn.silu(x_conv).astype(BF)
    projected = head_total(jnp.dot(u_low, full_xproj, preferred_element_type=F32), BF)
    ssm_vec = full_ssm_gain.astype(F32)
    b_end = rank + states
    dt_normed, dt_scale = norm_rows(projected[:, :rank], ssm_vec[:rank])
    b_normed, b_scale = norm_rows(projected[:, rank:b_end], ssm_vec[rank:b_end])
    c_normed, c_scale = norm_rows(projected[:, b_end:], ssm_vec[b_end:])
    dt_low = dt_normed.astype(BF)
    dt_pre = jnp.dot(dt_low, full_w_dt, preferred_element_type=F32) + full_dt_bias.astype(F32)
    step = jax.nn.softplus(dt_pre)
    rates = -jnp.exp(full_a_log.astype(F32))
    rate_rows = jnp.repeat((rates * LOG2E).T, seqs, axis=0)
    bc = jnp.concatenate([b_normed, c_normed], axis=1)
    part_one = bc.astype(BF)
    part_two = (bc - part_one.astype(F32)).astype(BF)
    part_three = (bc - part_one.astype(F32) - part_two.astype(F32)).astype(BF)
    stops = ((1.0 - same_docs[1]) * STOP).astype(BF)
    spare = jnp.zeros((rows, LANES - 6 * states - 1), BF)
    parts = jnp.concatenate([part_one, part_two, part_three, stops, spare], axis=1)
    shape = jax.ShapeDtypeStruct
    state_rows = states * seqs
    step, full_wide = lax.optimization_barrier((step, full_wide))
    full_gate, full_up = full_wide[:, :hidden_units], full_wide[:, hidden_units:]
    start, step_sum = state_call(
        entry_kernel,
        1,
        seqs,
        states,
        [parts, step, u_low, rate_rows],
        [shape((state_rows, channels), F32), shape((seqs, channels), F32)],
        exchange_scratch(count, seqs, states, channels),
        6,
        (0, 0),
    )
    y_state, mix_blocks = state_call(
        forward_kernel,
        2,
        seqs,
        states,
        [parts, step, u_low, rate_rows, start, w_mix],
        [shape((rows, channels), F32), shape((count,) + w_mix.shape, BF)],
        gather_sems(count // 2, w_mix.shape[1]),
        8,
        (1, 1),
    )
    full_mix = mix_blocks.reshape(width, 2 * channels)
    full_in_z, full_out_t = full_mix[:, :channels], full_mix[:, channels:]
    z_gate = jnp.dot(x_norm, full_in_z, preferred_element_type=F32)
    skip_vec = full_d_skip.astype(F32)
    u_rows = u_low.astype(F32)
    y_full = y_state + skip_vec * u_rows
    silu_z = jax.nn.silu(z_gate)
    g_low = (y_full * silu_z).astype(BF)
    grad_low = d_out.transpose(1, 0, 2).reshape(rows, width)
    blocks = lambda full: full.reshape(count, -1, full.shape[1])
    hidden, x_norm2, act_low, d_gate, d_up, norm2_sums, ffn_part, d_hidden, d_mix = ffn_call(
        g_low,
        full_out_t,
        head_part(x_rows),
        full_norm2.astype(F32)[None, :],
        grad_low,
        head_part(grad_low).astype(F32),
        [blocks(full_gate), blocks(full_up)],
        [w_down.astype(BF).T],
    )
    grad_norm2 = norm2_sums[0]
    grad_down = jnp.einsum("rd,rf->df", grad_low, act_low, preferred_element_type=F32)
    grad_gate = jnp.einsum("rd,rf->df", x_norm2, d_gate, preferred_element_type=F32)
    grad_up = jnp.einsum("rd,rf->df", x_norm2, d_up, preferred_element_type=F32)
    ffn_own = head_scatter(ffn_part)
    grad_out_w = jnp.einsum("rd,re->de", d_mix, g_low, preferred_element_type=F32)
    d_g = jnp.dot(d_mix, full_out_t, preferred_element_type=F32)
    d_y = d_g * silu_z
    d_z = (d_g * y_full * silu_slope(z_gate)).astype(BF)
    grad_skip = jnp.sum(d_y * u_rows, axis=0)
    grad_in_z = jnp.einsum("rd,re->de", x_norm, d_z, preferred_element_type=F32)
    big_grads = [
        owner_blocks(grad.astype(BF))
        for grad in (grad_down, grad_gate, grad_up, grad_out_w, grad_in_z)
    ]
    (last,) = state_call(
        adjoint_kernel,
        3,
        seqs,
        states,
        [parts, step, d_y, rate_rows, step_sum],
        [shape((state_rows, channels), F32)],
        exchange_scratch(count, seqs, states, channels),
        6,
        (0, 0),
    )
    last, ffn_own = lax.optimization_barrier((last, ffn_own))
    block_rows = head_gather((hidden + ffn_own).astype(BF))
    d_u_state, d_pre_low, d_bc, d_log, d_bias, *moved = state_call(
        backward_kernel,
        4,
        seqs,
        states,
        [parts, step, u_low, d_y, rate_rows, start, last] + big_grads,
        [
            shape((rows, channels), F32),
            shape((rows, channels), BF),
            shape((rows, LANES), F32),
            shape((states, channels), F32),
            shape((seqs, channels), F32),
        ]
        + [shape((count // 2,) + grad.shape[2:], BF) for grad in big_grads]
        + [shape((count // 2 - 1,) + grad.shape[2:], BF) for grad in big_grads],
        [
            pltpu.VMEM(((tokens + 1) * states, seqs, LANES), F32),
            pltpu.VMEM((rows, 2 * states * LANES), F32),
        ]
        + scatter_scratch(count, big_grads),
        30,
        (len(big_grads), 2 * len(big_grads)),
    )
    d_bc, block_rows = lax.optimization_barrier((d_bc, block_rows))
    block_out = block_rows.reshape(tokens, seqs, width).transpose(1, 0, 2)
    own_down, own_gate, own_up, own_out, own_in_z = (
        scatter_own(grad, given, came)
        for grad, given, came in zip(big_grads, moved[: len(big_grads)], moved[len(big_grads) :])
    )
    grad_alog = d_log.T * rates
    grad_bias = jnp.sum(d_bias, axis=0)
    grad_step_w = jnp.einsum("rk,re->ke", dt_low, d_pre_low, preferred_element_type=F32)
    d_dt_part = jnp.einsum("re,ke->rk", d_pre_low, full_w_dt, preferred_element_type=F32)
    d_stats = head_total(jnp.concatenate([d_dt_part, d_bc[:, : 2 * states]], axis=1), BF)
    d_dt_raw, grad_dt_gain = norm_back(
        projected[:, :rank], dt_scale, ssm_vec[:rank], d_stats[:, :rank]
    )
    d_b_raw, grad_b_gain = norm_back(
        projected[:, rank:b_end], b_scale, ssm_vec[rank:b_end], d_stats[:, rank:b_end]
    )
    d_c_raw, grad_c_gain = norm_back(
        projected[:, b_end:], c_scale, ssm_vec[b_end:], d_stats[:, b_end:]
    )
    d_proj = jnp.concatenate([d_dt_raw, d_b_raw, d_c_raw], axis=1)
    grad_ssm = jnp.concatenate([grad_dt_gain, grad_b_gain, grad_c_gain])
    grad_xproj = jnp.einsum("re,rk->ek", u_low, d_proj, preferred_element_type=F32)
    d_u = (
        d_y * skip_vec
        + d_u_state
        + jnp.einsum("rk,ek->re", d_proj, full_xproj, preferred_element_type=F32)
    )
    d_conv = d_u * silu_slope(x_conv)
    grad_conv_b = jnp.sum(d_conv, axis=0)
    d_extended = jnp.zeros((rows + halo, channels), F32)
    conv_grads = []
    for offset in range(taps):
        first = (taps - 1 - offset) * seqs
        masked = d_conv * same_docs[offset]
        conv_grads.append(jnp.sum(masked * extended[first : first + rows], axis=0))
        d_extended = d_extended + jnp.pad(
            conv_weight[offset] * masked, ((first, halo - first), (0, 0))
        )
    grad_conv_w = jnp.stack(conv_grads)
    from_next = shifted(d_extended[:halo].astype(BF), "seq", -1).astype(F32)
    d_inner = d_extended[halo:] + jnp.pad(from_next, ((rows - halo, 0), (0, 0)))
    d_inner_low = d_inner.astype(BF)
    grad_in_x = jnp.einsum("rd,re->de", x_norm, d_inner_low, preferred_element_type=F32)
    d_norm1 = head_scatter(
        jnp.einsum("re,de->rd", d_inner_low, full_in_x, preferred_element_type=F32)
        + jnp.einsum("re,de->rd", d_z, full_in_z, preferred_element_type=F32)
    )
    d_input_part, grad_norm1 = norm_back(head_part(x_rows), head_part(scale_one), norm1_vec, d_norm1)
    input_rows = head_gather((d_hidden + d_input_part).astype(BF)).astype(F32)
    grad_input = input_rows.reshape(tokens, seqs, width).transpose(1, 0, 2)

    grad_ssm = grad_ssm * (lax.axis_index("head") == 0).astype(F32)
    small = pack(
        [
            grad_xproj,
            grad_step_w.T,
            grad_alog,
            grad_conv_w.T,
            grad_conv_b[:, None],
            grad_bias[:, None],
            grad_skip[:, None],
        ],
        [grad_norm1, grad_norm2, grad_ssm],
    )
    small = scatter_rows(small.reshape(-1, pack_width), F32)
    small = jnp.concatenate([small[:per], head_total(small[per:], F32)])[None]
    small_fields, small_gains = unpack(small)
    own_in_x = scatter_rows(grad_in_x)
    return (
        block_out,
        grad_input,
        small_gains[0],
        own_in_x,
        own_in_z,
        small_fields[3].T,
        small_fields[4][:, 0],
        small_fields[0],
        small_gains[2],
        small_fields[1].T,
        small_fields[5][:, 0],
        small_fields[2],
        small_fields[6][:, 0],
        own_out.T,
        small_gains[1],
        own_gate,
        own_up,
        own_down.T,
    )


def solution(mesh):
    placed = (
        P(None, "seq", None),
        P(None, "seq"),
        P("seq"),
        P("seq", "head"),
        P("seq", "head"),
        P(None, ("head", "seq")),
        P(("head", "seq")),
        P(("head", "seq"), None),
        P("seq"),
        P(None, ("head", "seq")),
        P(("head", "seq")),
        P(("head", "seq"), None),
        P(("head", "seq")),
        P("head", "seq"),
        P("seq"),
        P("seq", "head"),
        P("seq", "head"),
        P("head", "seq"),
        P(None, "seq", None),
    )
    return jax.shard_map(
        shards,
        mesh=mesh,
        in_specs=placed,
        out_specs=(
            P(None, "seq", None),
            P(None, "seq", None),
            P("seq"),
            P("seq", "head"),
            P("seq", "head"),
            P(None, ("head", "seq")),
            P(("head", "seq")),
            P(("head", "seq"), None),
            P("seq"),
            P(None, ("head", "seq")),
            P(("head", "seq")),
            P(("head", "seq"), None),
            P(("head", "seq")),
            P("head", "seq"),
            P("seq"),
            P("seq", "head"),
            P("seq", "head"),
            P("head", "seq"),
        ),
        check_vma=False,
    )
```

time: 1110 us -> 853 us (0.77)
  Pallas kernels: 261 us -> 513 us
  waiting for transfers between devices: 293 us -> 41.2 us
  starting transfers between devices: 147 us -> 40.9 us
  blocking collectives: 83.5 us -> 0 us
  matrix products: 116 us -> 82.6 us
  other arithmetic: 103 us -> 74.7 us
    pallas_call x4 -> x5, Pallas kernels: 219 us -> 450 us  [the longest x4 341 us: state_call(): pl.pallas_call(functools.partial(body, count, seqs, states), in_specs=[in...]
    ppermute x37 -> x16, waiting for transfers between devices: 155 us -> 30.5 us  [swap(): lax.ppermute(value, axis, [(s, s ^ bit) for s in range(lax.axis_size(axis...]
    ppermute x27 -> x6, waiting for transfers between devices: 133 us -> 10.6 us  [hop(): lax.ppermute(value, 'seq', [(s, (s + 2 * steps) % count) for s in range(c...]
    ppermute x27 -> x6, starting transfers between devices: 108 us -> 17.4 us  [hop(): lax.ppermute(value, 'seq', [(s, (s + 2 * steps) % count) for s in range(c...]
    all_gather x1 -> x0, blocking collectives: 83.5 us -> none  [shards(): all_sums = lax.all_gather(step_sum, 'seq')]
    dot_general x7 -> x0, matrix products: 40 us -> none  [the longest x1 9.54 us: shards(): up_proj = jnp.dot(x_norm2, full_up, preferred_element_type=F32)]
    pallas_call x1, Pallas kernels: 41.5 us -> 63 us  [first_gather(): pl.pallas_call(functools.partial(first_kernel, count), out_shape=tuple((j...]
    ppermute x37 -> x16, starting transfers between devices: 27.2 us -> 12.2 us  [swap(): lax.ppermute(value, axis, [(s, s ^ bit) for s in range(lax.axis_size(axis...]
  transfers between devices with their start and end apart: 69 -> 26, of which waited for: 25 -> 11; matrix products, arithmetic and copies ran while one was open for 19% -> 18% of each run, Pallas kernels for 7% -> 35%
where the time goes in v3:
time: 853 us; the launch traced here: 846 us
  Pallas kernels  513 us (60%)
  matrix products  82.6 us (10%)
  local copies, waits for them, and re-layouts  78.1 us (9%)
  other arithmetic  74.7 us (9%)
  waiting for transfers between devices  41.2 us (5%)
  starting transfers between devices  40.9 us (5%)
  between operations  16.3 us (2%)
    pallas_call x4, Pallas kernels, state_call(): pl.pallas_call(functools.partial(body, count, seqs, states), in_specs=[in...  341 us
    pallas_call x1, Pallas kernels, ffn_call(): pl.pallas_call(functools.partial(ffn_kernel, count, CHUNKS, len(waiting))...  109 us
    pallas_call x1, Pallas kernels, first_gather(): pl.pallas_call(functools.partial(first_kernel, count), out_shape=tuple((j...  63 us
    ppermute x16, waiting for transfers between devices, swap(): lax.ppermute(value, axis, [(s, s ^ bit) for s in range(lax.axis_size(axis...  30.5 us
    unnamed x260, local copies, waits for them, and re-layouts  27 us
    ppermute x6, starting transfers between devices, hop(): lax.ppermute(value, 'seq', [(s, (s + 2 * steps) % count) for s in range(c...  17.4 us
  transfers between devices with their start and end apart: 26, of which 11 were waited for; matrix products, arithmetic and copies ran while one was open for 18% of the time, Pallas kernels for 35%

profile of v3, /device:TPU:0, one launch (start us, length us, event | category | flops | bytes accessed | tf_op | source)
XLA Modules:
  0.0 846.3 jit_solution(6046332934940232088)
XLA Ops:
  8.8 5.4 collective-permute-start.1
  21.3 63.0 %shard_map.322 = (bf16[8,192,768]{2,1,0:T(8,128)(2,1)}, bf16[8,112,256]{2,1,0:T(8,128)(2,1)}) custom-call(bf16[192,768]{1,0:T(8,128)(2,1)} %convert_element_type.445.refs_0_, bf16[112,256]{1,0:T(8,128)(2,1)} %maximum_bitcast_fusion.1.refs_1_), custom_call_target="tpu_custom_call" | custom-call | tf_op jit(solution)/shard_map/pallas_call | solution.py:1129
  88.3 3.8 fusion.22
  93.9 4.4 collective-permute-start
  104.6 5.3 copy.202
  125.2 3.6 multiply_convert_fusion.2
  134.8 5.1 collective-permute-done.3
  143.0 3.7 compare_select_fusion.step_ref
  146.7 6.3 fusion.76
  152.9 28.9 %shard_map.323 = (f32[128,768]{1,0:T(8,128)}, f32[8,768]{1,0:T(8,128)}) custom-call(bf16[1024,128]{1,0:T(8,128)(2,1)} %concatenate.75.parts_ref, f32[1024,768]{1,0:T(8,128)} %compare_select_fusion.step_ref, bf16[1024,768]{1,0:T(8,128)(2,1)} %copy-done.2, f32[128,768]{1,0:T(8,128)} %broadcast_bitcast_fusion.rate_ref), custom_call_target="tpu_custom_call" | custom-call | flops 75497472 | bytes 16777216 | tf_op jit(solution)/shard_map/pallas_call | solution.py:644
  181.8 77.8 %shard_map.324 = (f32[1024,768]{1,0:T(8,128)}, bf16[8,192,1536]{2,1,0:T(8,128)(2,1)}) custom-call(bf16[1024,128]{1,0:T(8,128)(2,1)} %concatenate.75.parts_ref, f32[1024,768]{1,0:T(8,128)} %compare_select_fusion.step_ref, bf16[1024,768]{1,0:T(8,128)(2,1)} %copy-done.2, f32[128,768]{1,0:T(8,128)} %broadcast_bitcast_fusion.rate_ref, ...), custom_call_target="tpu_custom_call" | custom-call | flops 100663296 | bytes 16777216 | tf_op jit(solution)/shard_map/pallas_call | solution.py:644
  263.1 10.3 %multiply_convert_fusion.1 = (bf16[1024,768]{1,0:T(8,128)(2,1)}, f32[1024,768]{1,0:T(8,128)}) fusion(f32[1024,768]{1,0:T(8,128)} %get-tuple-element.58, bf16[1024,768]{1,0:T(8,128)(2,1)S(1)} %copy-done.3, f32[768]{0:T(1024)S(1)} %copy-done.89, bf16[1536,1536]{1,0:T(8,128)(2,1)} %bitcast.290, f32[1536]{0:T(1024)S(1)} %reshape.461, f32[1024]{0:T(1024)S(1)} %rsqrt.50, ...), kind=kOutput, calls=%fused_computation.39 | convolution fusion | flops 2429288448 | bytes 14955520 | tf_op jit(solution)/shard_map/dot_general | solution.py:1276
  273.4 109.0 %shard_map.325 = (f32[256,1536]{1,0:T(8,128)}, bf16[1024,1536]{1,0:T(8,128)(2,1)}, bf16[1024,1024]{1,0:T(8,128)(2,1)}, bf16[1024,1024]{1,0:T(8,128)(2,1)}, bf16[...) custom-call(bf16[1024,768]{1,0:T(8,128)(2,1)} %get-tuple-element.273, ...), custom_call_target="tpu_custom_call" | custom-call | flops 22548578304 | bytes 41943040 | tf_op jit(solution)/shard_map/pallas_call | solution.py:996
  393.8 8.1 fusion.7
  401.8 46.7 %shard_map.326.last_ref = f32[128,768]{1,0:T(8,128)} custom-call(bf16[1024,128]{1,0:T(8,128)(2,1)} %concatenate.75.parts_ref, f32[1024,768]{1,0:T(8,128)} %compare_select_fusion.step_ref, f32[1024,768]{1,0:T(8,128)} %get-tuple-element.228.dy_ref, f32[128,768]{1,0:T(8,128)} %broadcast_bitcast_fusion.rate_ref, f32[8,768]{1,0:T(8,128)} %get-tuple-element.62.sum_ref), custom_call_target="tpu_custom_call" | custom-call | flops 75497472 | bytes 16777216 | tf_op jit(solution)/shard_map/pallas_call | solution.py:644
  448.6 6.4 fusion.5
  458.9 5.1 convolution_convert_fusion.4
  466.8 7.7 convolution_convert_fusion.1
  478.8 4.0 convolution_convert_fusion.5
  482.8 5.0 convolution_convert_fusion
  487.9 187.2 %shard_map.327 = (f32[1024,768]{1,0:T(8,128)}, bf16[1024,768]{1,0:T(8,128)(2,1)}, f32[1024,128]{1,0:T(8,128)}, f32[16,768]{1,0:T(8,128)}, f32[8,768]{1,0:T(8,128...) custom-call(bf16[1024,128]{1,0:T(8,128)(2,1)} %concatenate.75.parts_, ...), custom_call_target="tpu_custom_call" | custom-call | flops 377487360 | bytes 16777216 | tf_op jit(solution)/shard_map/pallas_call | solution.py:644
  690.3 4.7 collective-permute-done.9
  701.9 7.2 multiply_reduce_fusion.3
  711.5 6.4 fusion.17
  719.2 5.7 add_convert_fusion
  741.4 4.3 convolution_convert_fusion.3
  752.8 4.6 concatenate.84
  766.5 11.5 %collective-permute-done.21 = bf16[4,192,768]{2,1,0:T(8,128)(2,1)} collective-permute-done((bf16[4,192,768]{2,1,0:T(8,128)(2,1)}, bf16[4,192,768]{2,1,0:T(8,128)(2,1)}, u32[]{:S(2)}, u32[]{:S(2)}) %collective-permute-start.21) | collective-permute-done | bytes 1179680 | tf_op jit(solution)/shard_map/ppermute | solution.py:1026
  782.3 3.5 collective-permute-start.22
  793.5 9.7 %collective-permute-done.16 = f32[112,256]{1,0:T(8,128)S(1)} collective-permute-done((f32[112,256]{1,0:T(8,128)S(1)}, f32[112,256]{1,0:T(8,128)S(1)}, u32[]{:S(2)}, u32[]{:S(2)}) %collective-permute-start.16) | collective-permute-done | bytes 114720 | tf_op jit(solution)/shard_map/ppermute | solution.py:1022
  803.2 8.6 %collective-permute-start.23 = (bf16[192,768]{1,0:T(8,128)(2,1)S(1)}, bf16[192,768]{1,0:T(8,128)(2,1)S(1)}, u32[]{:S(2)}, u32[]{:S(2)}) collective-permute-start(bf16[192,768]{1,0:T(8,128)(2,1)S(1)} %copy-done.41), channel_id=1, source_target_pairs={{0,16},{4,20},{8,24},{12,28},{16,0},{20,4},{24,8},{28,12},{1,17},{... | collective-permute-start | bytes 884744 | tf_op jit(solution)/shard_map/ppermute | solution.py:1022
  832.8 6.4 copy.171
  (469 shorter events, 160.8 us)
Async XLA Ops:
  7.3 139.4 %all-gather.2.cloned.1.call-start = ((), (), s32[]{:S(2)}) async-start(), calls=%async_computation | async-start | bytes 7077888 | tf_op jit(solution)/shard_map/all_gather | solution.py:1209
  8.8 113.7 %collective-permute-start.1 = (s32[24]{0:T(128)}, s32[24]{0:T(128)}, u32[]{:S(2)}, u32[]{:S(2)}) collective-permute-start(s32[24]{0:T(128)} %slice.264), channel_id=1, source_target_pairs={{0,4},{4,8},{8,12},{12,16},{16,20},{20,24},{24,28},{1,5},{5,9},{9,... | collective-permute-start | bytes 296 | tf_op jit(solution)/shard_map/ppermute | solution.py:22
  15.4 71.2 %copy-start.8 = (bf16[8,128,1536]{2,1,0:T(8,128)(2,1)S(1)}, bf16[8,128,1536]{2,1,0:T(8,128)(2,1)}, u32[]{:S(2)}) copy-start(bf16[8,128,1536]{2,1,0:T(8,128)(2,1)} %param.19) | copy-start | bytes 9437188
  93.9 30.2 %collective-permute-start = (bf16[24,768]{1,0:T(8,128)(2,1)}, bf16[24,768]{1,0:T(8,128)(2,1)}, u32[]{:S(2)}, u32[]{:S(2)}) collective-permute-start(bf16[24,768]{1,0:T(8,128)(2,1)} %slice.336), channel_id=1, source_target_pairs={{0,4},{4,8},{8,12},{12,16},{16,20},{20,24},{24,28},{1,5},{5,9},{9,... | collective-permute-start | bytes 110600 | tf_op jit(solution)/shard_map/ppermute | solution.py:22
  100.2 575.0 %copy-start.14 = (bf16[8,96,256]{2,1,0:T(8,128)(2,1)}, bf16[8,96,256]{2,1,0:T(8,128)(2,1)S(1)}, u32[]{:S(2)}) copy-start(bf16[8,96,256]{2,1,0:T(8,128)(2,1)S(1)} %slice.253) | copy-start | bytes 1179652
  129.6 1.6 collective-permute-start.2
  131.3 8.6 %collective-permute-start.3 = (bf16[1024,128]{0,1:T(8,128)(2,1)S(1)}, bf16[1024,128]{0,1:T(8,128)(2,1)}, u32[]{:S(2)}, u32[]{:S(2)}) collective-permute-start(bf16[1024,128]{0,1:T(8,128)(2,1)S(1)} %add_convert_fusion.3), channel_id=1, source_target_pairs={{0,2},{1,3},{2,0},{3,1},{4,6},{5,7},{6,4},{7,5},{8,10},{9,11},{10,... | collective-permute-start | bytes 786440 | tf_op jit(solution)/shard_map/ppermute | solution.py:1026
  133.0 130.1 %copy-start.93 = (f32[1024]{0:T(1024)}, f32[1024]{0:T(1024)S(1)}, u32[]{:S(2)}) copy-start(f32[1024]{0:T(1024)S(1)} %rsqrt.50) | copy-start | bytes 12292
  385.0 3.8 collective-permute-start.4
  393.2 61.8 %collective-permute-start.5 = (bf16[4,64,1536]{2,1,0:T(8,128)(2,1)}, bf16[4,64,1536]{2,1,0:T(8,128)(2,1)}, u32[]{:S(2)}, u32[]{:S(2)}) collective-permute-start(bf16[4,64,1536]{2,1,0:T(8,128)(2,1)} %dynamic-slice_bitcast_fusion.4), channel_id=1, source_target_pairs={{0,2},{1,3},{2,0},{3,1},{4,6},{5,7},{6,4},{7,5},{8,10},{9,11},{10,... | collective-permute-start | bytes 2359304 | tf_op jit(solution)/shard_map/ppermute | solution.py:1026
  457.6 18.5 %collective-permute-start.6 = (bf16[4,64,1536]{2,1,0:T(8,128)(2,1)}, bf16[4,64,1536]{2,1,0:T(8,128)(2,1)}, u32[]{:S(2)}, u32[]{:S(2)}) collective-permute-start(bf16[4,64,1536]{2,1,0:T(8,128)(2,1)} %bitcast.46), channel_id=1, source_target_pairs={{0,2},{1,3},{2,0},{3,1},{4,6},{5,7},{6,4},{7,5},{8,10},{9,11},{10,... | collective-permute-start | bytes 2359304 | tf_op jit(solution)/shard_map/ppermute | solution.py:1026
  478.8 199.0 %collective-permute-start.7 = (bf16[4,128,1536]{2,1,0:T(8,128)(2,1)}, bf16[4,128,1536]{2,1,0:T(8,128)(2,1)}, u32[]{:S(2)}, u32[]{:S(2)}) collective-permute-start(bf16[4,128,1536]{2,1,0:T(8,128)(2,1)} %pad_maximum_fusion.2), channel_id=1, source_target_pairs={{0,1},{1,0},{2,3},{3,2},{4,5},{5,4},{6,7},{7,6},{8,9},{9,8},{10,11... | collective-permute-start | bytes 4718600 | tf_op jit(solution)/shard_map/ppermute | solution.py:1026
  683.8 1.6 collective-permute-start.8
  686.3 8.7 %collective-permute-start.9 = (bf16[1024,128]{0,1:T(8,128)(2,1)}, bf16[1024,128]{0,1:T(8,128)(2,1)}, u32[]{:S(2)}, u32[]{:S(2)}) collective-permute-start(bf16[1024,128]{0,1:T(8,128)(2,1)} %add_convert_fusion.2), channel_id=1, source_target_pairs={{0,2},{1,3},{2,0},{3,1},{4,6},{5,7},{6,4},{7,5},{8,10},{9,11},{10,... | collective-permute-start | bytes 786440 | tf_op jit(solution)/shard_map/ppermute | solution.py:1026
  710.0 9.2 %collective-permute-start.10 = (bf16[24,768]{1,0:T(8,128)(2,1)S(1)}, bf16[24,768]{1,0:T(8,128)(2,1)S(1)}, u32[]{:S(2)}, u32[]{:S(2)}) collective-permute-start(bf16[24,768]{1,0:T(8,128)(2,1)S(1)} %slice.527), channel_id=1, source_target_pairs={{4,0},{8,4},{12,8},{16,12},{20,16},{24,20},{28,24},{5,1},{9,5},{13... | collective-permute-start | bytes 110600 | tf_op jit(solution)/shard_map/ppermute | solution.py:22
  725.1 10.9 %collective-permute-start.11 = (bf16[4,128,1536]{2,1,0:T(8,128)(2,1)S(1)}, bf16[4,128,1536]{2,1,0:T(8,128)(2,1)S(1)}, u32[]{:S(2)}, u32[]{:S(2)}) collective-permute-start(bf16[4,128,1536]{2,1,0:T(8,128)(2,1)S(1)} %dynamic-slice_bitcast_fusion), channel_id=1, source_target_pairs={{0,1},{1,0},{2,3},{3,2},{4,5},{5,4},{6,7},{7,6},{8,9},{9,8},{10,11... | collective-permute-start | bytes 4718600 | tf_op jit(solution)/shard_map/ppermute | solution.py:1026
  740.0 21.7 %collective-permute-start.12 = (bf16[4,64,1536]{2,1,0:T(8,128)(2,1)}, bf16[4,64,1536]{2,1,0:T(8,128)(2,1)}, u32[]{:S(2)}, u32[]{:S(2)}) collective-permute-start(bf16[4,64,1536]{2,1,0:T(8,128)(2,1)} %dynamic-slice_bitcast_fusion.3), channel_id=1, source_target_pairs={{0,2},{1,3},{2,0},{3,1},{4,6},{5,7},{6,4},{7,5},{8,10},{9,11},{10,... | collective-permute-start | bytes 2359304 | tf_op jit(solution)/shard_map/ppermute | solution.py:1026
  748.2 29.8 %collective-permute-start.21 = (bf16[4,192,768]{2,1,0:T(8,128)(2,1)}, bf16[4,192,768]{2,1,0:T(8,128)(2,1)}, u32[]{:S(2)}, u32[]{:S(2)}) collective-permute-start(bf16[4,192,768]{2,1,0:T(8,128)(2,1)} %dynamic-slice_bitcast_fusion.2), channel_id=1, source_target_pairs={{0,4},{4,0},{8,12},{12,8},{16,20},{20,16},{24,28},{28,24},{1,5},{5... | collective-permute-start | bytes 3538952 | tf_op jit(solution)/shard_map/ppermute | solution.py:1026
  766.0 20.4 %copy-start.16 = (f32[768,256]{1,0:T(8,128)S(1)}, f32[768,256]{1,0:T(8,128)}, u32[]{:S(2)}) copy-start(f32[768,256]{1,0:T(8,128)} %pad.49.clone) | copy-start | bytes 2359300
  766.0 20.4 %collective-permute-start.15 = (f32[4,112,256]{2,1,0:T(8,128)S(1)}, f32[4,112,256]{2,1,0:T(8,128)S(1)}, u32[]{:S(2)}, u32[]{:S(2)}) collective-permute-start(f32[4,112,256]{2,1,0:T(8,128)S(1)} %fusion.33), channel_id=1, source_target_pairs={{0,4},{4,0},{8,12},{12,8},{16,20},{20,16},{24,28},{28,24},{1,5},{5... | collective-permute-start | bytes 1376264 | tf_op jit(solution)/shard_map/ppermute | solution.py:1026
  782.3 36.3 %collective-permute-start.22 = (bf16[192,768]{1,0:T(8,128)(2,1)}, bf16[192,768]{1,0:T(8,128)(2,1)}, u32[]{:S(2)}, u32[]{:S(2)}) collective-permute-start(bf16[192,768]{1,0:T(8,128)(2,1)} %get-tuple-element.253), channel_id=1, source_target_pairs={{0,8},{4,12},{8,16},{12,20},{16,24},{20,28},{24,0},{28,4},{1,9},{5... | collective-permute-start | bytes 884744 | tf_op jit(solution)/shard_map/ppermute | solution.py:1022
  785.8 32.9 %collective-permute-start.24 = (bf16[192,768]{1,0:T(8,128)(2,1)}, bf16[192,768]{1,0:T(8,128)(2,1)}, u32[]{:S(2)}, u32[]{:S(2)}) collective-permute-start(bf16[192,768]{1,0:T(8,128)(2,1)} %get-tuple-element.254), channel_id=1, source_target_pairs={{0,24},{4,28},{8,0},{12,4},{16,8},{20,12},{24,16},{28,20},{1,25},{... | collective-permute-start | bytes 884744 | tf_op jit(solution)/shard_map/ppermute | solution.py:1022
  786.5 26.3 %copy-start.34 = (bf16[3,192,768]{2,1,0:T(8,128)(2,1)S(1)}, bf16[3,192,768]{2,1,0:T(8,128)(2,1)}, u32[]{:S(2)}) copy-start(bf16[3,192,768]{2,1,0:T(8,128)(2,1)} %get-tuple-element.81) | copy-start | bytes 2654212
  786.5 16.7 %collective-permute-start.16 = (f32[112,256]{1,0:T(8,128)S(1)}, f32[112,256]{1,0:T(8,128)S(1)}, u32[]{:S(2)}, u32[]{:S(2)}) collective-permute-start(f32[112,256]{1,0:T(8,128)S(1)} %get-tuple-element.262), channel_id=1, source_target_pairs={{0,8},{4,12},{8,16},{12,20},{16,24},{20,28},{24,0},{28,4},{1,9},{5... | collective-permute-start | bytes 344072 | tf_op jit(solution)/shard_map/ppermute | solution.py:1022
  789.7 22.1 %collective-permute-start.18 = (f32[112,256]{1,0:T(8,128)S(1)}, f32[112,256]{1,0:T(8,128)S(1)}, u32[]{:S(2)}, u32[]{:S(2)}) collective-permute-start(f32[112,256]{1,0:T(8,128)S(1)} %get-tuple-element.263), channel_id=1, source_target_pairs={{0,24},{4,28},{8,0},{12,4},{16,8},{20,12},{24,16},{28,20},{1,25},{... | collective-permute-start | bytes 344072 | tf_op jit(solution)/shard_map/ppermute | solution.py:1022
  790.6 22.0 %collective-permute-start.17 = (f32[112,256]{1,0:T(8,128)S(1)}, f32[112,256]{1,0:T(8,128)S(1)}, u32[]{:S(2)}, u32[]{:S(2)}) collective-permute-start(f32[112,256]{1,0:T(8,128)S(1)} %get-tuple-element.264), channel_id=1, source_target_pairs={{0,16},{4,20},{8,24},{12,28},{16,0},{20,4},{24,8},{28,12},{1,17},{... | collective-permute-start | bytes 344072 | tf_op jit(solution)/shard_map/ppermute | solution.py:1022
  791.5 23.3 %copy-start.7 = (bf16[4,256,1536]{2,1,0:T(8,128)(2,1)S(1)}, bf16[4,256,1536]{2,1,0:T(8,128)(2,1)}, u32[]{:S(2)}) copy-start(bf16[4,256,1536]{2,1,0:T(8,128)(2,1)} %pad_maximum_fusion) | copy-start | bytes 9437188
  803.2 16.4 %collective-permute-start.23 = (bf16[192,768]{1,0:T(8,128)(2,1)S(1)}, bf16[192,768]{1,0:T(8,128)(2,1)S(1)}, u32[]{:S(2)}, u32[]{:S(2)}) collective-permute-start(bf16[192,768]{1,0:T(8,128)(2,1)S(1)} %copy-done.41), channel_id=1, source_target_pairs={{0,16},{4,20},{8,24},{12,28},{16,0},{20,4},{24,8},{28,12},{1,17},{... | collective-permute-start | bytes 884744 | tf_op jit(solution)/shard_map/ppermute | solution.py:1022
  811.8 12.4 %collective-permute-start.13 = (bf16[4,64,1536]{2,1,0:T(8,128)(2,1)S(1)}, bf16[4,64,1536]{2,1,0:T(8,128)(2,1)S(1)}, u32[]{:S(2)}, u32[]{:S(2)}) collective-permute-start(bf16[4,64,1536]{2,1,0:T(8,128)(2,1)S(1)} %bitcast.281), channel_id=1, source_target_pairs={{0,2},{1,3},{2,0},{3,1},{4,6},{5,7},{6,4},{7,5},{8,10},{9,11},{10,... | collective-permute-start | bytes 2359304 | tf_op jit(solution)/shard_map/ppermute | solution.py:1026
  812.6 4.7 collective-permute-start.19
  817.4 6.7 collective-permute-start.20
  824.4 5.4 collective-permute-start.14
  (118 other events, 873.5 us)
Sparse Core Ops, SparseCore 0:
  17.8 125.1 all-gather.1

commit v4 on v3

--- a/solution.py
+++ b/solution.py
@@ -47,7 +47,7 @@
     return pl.ds(pl.multiple_of(index * size, size), size)
 
 
-def spread(parts_ref, states, target):
+def spread(parts_ref, states, target, first=0):
     rows = parts_ref.shape[0]
     wide = 2 * LANES
     chunk = 256 if rows % 256 == 0 else rows
@@ -62,12 +62,12 @@
         stop = (column == columns) & (source == 3 * columns)
         hot = jnp.where(stop, 1.0, hot).astype(BF)
         for k in range(rows // chunk):
-            target[pl.ds(k * chunk, chunk), at_rows(pair, wide)] = jnp.dot(
+            target[pl.ds(k * chunk, chunk), at_rows(pair - first, wide)] = jnp.dot(
                 parts_ref[pl.ds(k * chunk, chunk), :], hot, preferred_element_type=F32
             )
         return carry
 
-    lax.fori_loop(0, states + 1, one, 0)
+    lax.fori_loop(first, states + 1, one, 0)
 
 
 def group_tokens(ref, group, lanes, seqs):
@@ -251,12 +251,13 @@
     sum_ref[...] = sums[place]
 
 
-def finish_exchange(exchange, tiles, chain, target_ref, states, zero):
+def finish_exchange(exchange, tiles, chain, target_ref, states, zero, relay=True):
     def pass_on(tile, carry):
         exchange.pass_on(tile)
         return carry
 
-    lax.fori_loop(0, tiles, pass_on, 0)
+    if relay:
+        lax.fori_loop(0, tiles, pass_on, 0)
 
     def take(tile, carry):
         lanes = at_rows(tile, LANES)
@@ -337,18 +338,44 @@
 
 
 def adjoint_kernel(
-    count, seqs, states, parts_ref, step_ref, dy_ref, rate_ref, sum_ref, last_ref, *scratch
+    count,
+    seqs,
+    states,
+    parts_ref,
+    step_ref,
+    dy_ref,
+    rate_ref,
+    sum_ref,
+    norm_ref,
+    low_ref,
+    act_ref,
+    dgate_ref,
+    dup_ref,
+    part_ref,
+    hidden_ref,
+    last_ref,
+    gdown_ref,
+    ggate_ref,
+    gup_ref,
+    out_ref,
+    *scratch,
 ):
-    spread_ref, ends, sums, *sems = scratch
+    spread_ref, ends, sums, *scratch = scratch
+    sems, (half, give, take, kept, block_ref, buffer, sum_sems) = scratch[:4], scratch[4:]
+    total = HeadSum(part_ref, half, give, take, block_ref, sum_sems)
+    chunks = kept.shape[0]
+    quarter = kept.shape[1]
     rows, channels = step_ref.shape
     tokens, tiles = rows // seqs, channels // LANES
     groups = tokens // GROUP
-    stop_lanes = pl.ds(2 * states * LANES, LANES)
+    stop_lanes = pl.ds(states * LANES, LANES)
     exchange = Exchange(count, False, (ends, sums), sems)
     place = exchange.place
     zero = jnp.zeros((seqs, LANES), F32)
-    greet_pairs(count)
-    spread(parts_ref, states, spread_ref)
+    greet_pairs(count, True)
+    for chunk in range(chunks):
+        total.near_copy(chunk).start()
+    spread(parts_ref, states, spread_ref, states // 2)
 
     def own(tile, carry):
         lanes = at_rows(tile, LANES)
@@ -362,7 +389,7 @@
                 fresh = []
                 for n in range(states):
                     decay = jnp.exp2(stop * rate_ref[pl.ds(n * seqs, seqs), lanes])
-                    c_one = spread_ref[here, pl.ds((states + n) * LANES, LANES)]
+                    c_one = spread_ref[here, pl.ds(n * LANES, LANES)]
                     fresh.append(decay * (grads[n] + dy * c_one))
                 grads = tuple(fresh)
             return grads
@@ -373,12 +400,64 @@
         return carry
 
     lax.fori_loop(0, tiles, own, 0)
+    for chunk in range(chunks):
+        total.fold(chunk, kept)
+    around, _, shard, units = gdown_ref.shape
+    together = max(1, 384 // (2 * shard))
+    wide = together * 2 * shard
+
+    def multiply(block):
+        lanes = pl.ds(block * wide, wide)
+        pairs = pl.ds(block * together, together)
+        mine = norm_ref[:, lanes].T
+        for d_ref, grad_ref in ((dgate_ref, ggate_ref), (dup_ref, gup_ref)):
+            grad = jnp.dot(mine, d_ref[...], preferred_element_type=F32).astype(BF)
+            grad_ref[pairs] = grad.reshape(together, 2, shard, units)
+        grad = jnp.dot(low_ref[:, lanes].T, act_ref[...], preferred_element_type=F32).astype(BF)
+        gdown_ref[pairs] = grad.reshape(together, 2, shard, units)
+
+    blocks = list(range(around // together))
+    for block in blocks[:2]:
+        multiply(block)
+
+    def pass_on(tile, carry):
+        exchange.pass_on(tile)
+        return carry
+
+    lax.fori_loop(0, tiles, pass_on, 0)
+
+    def bring(chunk, carry):
+        total.far_copy(chunk).wait_recv()
+        here = at_rows(chunk, quarter)
+        rows_out = hidden_ref[here, :] + kept[chunk] + take[chunk].astype(F32)
+        block_ref[total.own_rows(chunk), :] = rows_out.astype(BF)
+        total.far_back(chunk).start()
+        return carry
+
+    lax.fori_loop(0, chunks, bring, 0)
+    for block in blocks[2:]:
+        multiply(block)
     finish_exchange(exchange, tiles, lambda first, lanes: lax.fori_loop(
         0,
         count - 1 - place,
         lambda hop, state: chained(state, ends, sums, rate_ref, count - 1 - hop, lanes, seqs),
         first,
-    ), last_ref, states, zero)
+    ), last_ref, states, zero, False)
+
+    def spread_out(chunk, carry):
+        total.far_back(chunk).wait_recv()
+        total.near_back(chunk).start()
+        return carry
+
+    lax.fori_loop(0, chunks, spread_out, 0)
+
+    def finish(chunk, carry):
+        total.near_back(chunk).wait_recv()
+        put_sequences(out_ref, block_ref, chunk, 4 * quarter, buffer)
+        total.finish(chunk)
+        return carry
+
+    lax.fori_loop(0, chunks, finish, 0)
 
 
 def backward_kernel(
@@ -394,11 +473,14 @@
     last_ref,
     *refs,
 ):
-    kinds = (len(refs) - 16) // 3
+    kinds = (len(refs) - 35) // 3
+    dtlow_ref, wdt_ref, xproj_ref, gain_ref, taps_ref, *refs = refs
+    xconv_ref, ext_ref, proj_ref, *refs = refs
     grad_refs, refs = refs[:kinds], refs[kinds:]
-    du_ref, dpre_ref, dbc_ref, dlog_ref, dbias_ref, *refs = refs
+    inner_ref, ssm_ref, gx_ref, gw_ref, dlog_ref, sums_ref, *refs = refs
     given_refs, came_refs, scratch = refs[:kinds], refs[kinds : 2 * kinds], refs[2 * kinds :]
-    spread_ref, held, acc, *scratch = scratch
+    spread_ref, held, acc, du_ref, dpre_ref, *scratch = scratch
+    sent, got, tail, edge, from_next, head_sems, edge_sems, load_sems, *scratch = scratch
     rows, channels = step_ref.shape
     tokens, tiles = rows // seqs, channels // LANES
     groups = tokens // GROUP
@@ -406,8 +488,7 @@
     place = lax.axis_index("seq")
     low, high = lax.rem(place, 2), place // 2
     zero = jnp.zeros((seqs, LANES), F32)
-    greet_pairs(count)
-
+    greet_pairs(count, True, True)
     scatter = PairScatter(count, grad_refs, given_refs, came_refs, scratch)
     scatter.start()
     spread(parts_ref, states, spread_ref)
@@ -441,12 +522,6 @@
         state = lax.fori_loop(0, groups, again, state_blocks(start_ref, lanes, seqs, states))
         for n in range(states):
             held[tokens * states + n] = state[n]
-        for k in range(tiles):
-
-            @pl.when(tile == k)
-            def _():
-                scatter.advance(2 * k)
-
         grads = state_blocks(last_ref, lanes, seqs, states)
 
         def one(back, carry):
@@ -491,12 +566,12 @@
         dlog_ref[:, lanes] = jnp.concatenate(
             [jnp.sum(log, axis=0, keepdims=True) for log in logs], axis=0
         )
-        dbias_ref[:, lanes] = bias
+        sums_ref[pl.ds(5 * seqs, seqs), lanes] = bias
         for k in range(tiles):
 
             @pl.when(tile == k)
             def _():
-                scatter.advance(2 * k + 1)
+                scatter.advance(k)
 
         return carry
 
@@ -506,10 +581,12 @@
     chunk = 256 if rows % 256 == 0 else rows
     target = lax.broadcasted_iota(jnp.int32, (wide, LANES), 1)
     half = lax.broadcasted_iota(jnp.int32, (wide, LANES), 0) // LANES
-    dbc_ref[...] = jnp.zeros(dbc_ref.shape, F32)
+    past = taps_ref.shape[0] // 2 - 1
+    dbc_ref = spread_ref.at[:, pl.ds((past + 2) * LANES, LANES)]
+    dbc_ref[...] = jnp.zeros((rows, LANES), F32)
 
     def reduce(pair, carry):
-        hot = jnp.where(target == pair * 2 + half, 1.0, 0.0).astype(BF)
+        hot = jnp.where(target == LANES - 2 * states + pair * 2 + half, 1.0, 0.0).astype(BF)
         for k in range(rows // chunk):
             here = pl.ds(k * chunk, chunk)
             values = acc[here, at_rows(pair, wide)]
@@ -522,9 +599,197 @@
 
     lax.fori_loop(0, states, reduce, 0)
 
-    for turn in range(2 * tiles, scatter.turns):
+    scatter.advance(tiles)
+
+    span = tokens + past
+    value_at = tiles * span
+    tap_at = [value_at + k * span for k in range(past + 1)]
+    proj_lanes = pl.ds((past + 1) * LANES, LANES)
+    loads = [
+        pltpu.make_async_copy(xconv_ref, acc.at[:, pl.ds(0, channels)], load_sems.at[tiles]),
+        pltpu.make_async_copy(proj_ref, spread_ref.at[:, proj_lanes], load_sems.at[tiles + 1]),
+    ]
+    for tile in range(tiles):
+        source = ext_ref.at[:, :, pl.ds(tile * LANES, LANES)]
+        target_tiles = held.at[pl.ds(tile * span, span)]
+        loads.append(pltpu.make_async_copy(source, target_tiles, load_sems.at[tile]))
+    for load in loads:
+        load.start()
+    head = lax.axis_index("head")
+    near = {"head": head // 2 * 2 + 1 - lax.rem(head, 2)}
+    far = {"head": lax.rem(head + 2, 4)}
+    trade = [
+        pltpu.make_async_remote_copy(
+            src_ref=sent.at[k],
+            dst_ref=got.at[k],
+            send_sem=head_sems.at[0, k],
+            recv_sem=head_sems.at[1, k],
+            device_id=device,
+            device_id_type=pl.DeviceIdType.MESH,
+        )
+        for k, device in enumerate((near, far))
+    ]
+    for k in range(rows // chunk):
+        here = pl.ds(k * chunk, chunk)
+        stats = jnp.dot(dpre_ref[here, :], wdt_ref[...], preferred_element_type=F32)
+        sent[0, here, :] = (dbc_ref[here, :] + stats).astype(BF)
+    trade[0].start()
+
+    source = lax.broadcasted_iota(jnp.int32, (LANES, LANES), 0)
+    for k in range(1, past + 1):
+        hot = jnp.where(source == 6 * states + k, 1.0, 0.0).astype(BF)
+        for m in range(rows // chunk):
+            here = pl.ds(m * chunk, chunk)
+            spread_ref[here, pl.ds(k * LANES, LANES)] = jnp.dot(
+                parts_ref[here, :], hot, preferred_element_type=F32
+            )
+    scatter.advance(tiles + 1)
+    trade[0].wait_recv()
+    for k in range(rows // chunk):
+        here = pl.ds(k * chunk, chunk)
+        sent[1, here, :] = (sent[0, here, :].astype(F32) + got[0, here, :].astype(F32)).astype(BF)
+    trade[1].start()
+
+    def step_weights(tile, carry):
+        lanes = at_rows(tile, LANES)
+        gw_ref[lanes, :] = jnp.dot(
+            dpre_ref[:, lanes].T, dtlow_ref[...], preferred_element_type=F32
+        )
+        return carry
+
+    lax.fori_loop(0, tiles, step_weights, 0)
+    scatter.advance(tiles + 2)
+    trade[0].wait_send()
+    for load in loads:
+        load.wait()
+    trade[1].wait_recv()
+    ssm_ref[...] = jnp.zeros(ssm_ref.shape, F32)
+    for k in range(rows // chunk):
+        here = pl.ds(k * chunk, chunk)
+        stats = sent[1, here, :].astype(F32) + got[1, here, :].astype(F32)
+        d_proj, gain_rows = stats_back(stats, spread_ref[here, proj_lanes], gain_ref[...], states)
+        sent[0, here, :] = d_proj.astype(BF)
+        share = jnp.sum(gain_rows, axis=0, keepdims=True)
+        ssm_ref[...] += jnp.broadcast_to(share, ssm_ref.shape)
+    block = 16
+    size = block * seqs
+    edge[...] = jnp.zeros(edge.shape, BF)
+
+    def convolve(tile, carry):
+        lanes = at_rows(tile, LANES)
+        gx_ref[lanes, :] = jnp.dot(u_ref[:, lanes].T, sent[0], preferred_element_type=F32)
+        weights = xproj_ref[lanes, :]
+        skip = taps_ref[pl.ds(past + 1, 1), lanes]
+        ext_at = tile * span
+
+        def one(part, sums):
+            here = at_rows(part, size)
+            token = part * block
+            d_u = du_ref[here, lanes] + dy_ref[here, lanes] * skip
+            d_u = d_u + transposed_dot(sent[0, here, :], weights)
+            conv = acc[here, lanes]
+            logistic = 1.0 / (1.0 + jnp.exp(-conv))
+            d_conv = d_u * logistic * (1.0 + conv * (1.0 - logistic))
+            fresh = []
+            for k in range(past + 1):
+                masked = d_conv
+                if k:
+                    masked = d_conv * spread_ref[here, pl.ds(k * LANES, LANES)]
+                before = held[pl.ds(ext_at + token + past - k, block)]
+                blocks = masked.reshape(block, seqs, LANES)
+                fresh.append(sums[k] + jnp.sum(blocks * before, axis=0))
+                tap = taps_ref[pl.ds(k, 1), lanes]
+                held[pl.ds(tap_at[k] + token, block)] = blocks * tap[None]
+            fresh.append(sums[past + 1] + jnp.sum(d_conv.reshape(block, seqs, LANES), axis=0))
+            return tuple(fresh)
+
+        sums = lax.fori_loop(0, rows // size, one, (zero,) * (past + 2))
+        for k in range(past + 2):
+            sums_ref[pl.ds(k * seqs, seqs), lanes] = sums[k]
+        for k in range(1, past + 1):
+            for later in range(past):
+                held[tap_at[k] + tokens + later] = zero
+
+        def gather(part, carry):
+            token = part * block
+            total = held[pl.ds(tap_at[0] + token, block)]
+            for k in range(1, past + 1):
+                total = total + held[pl.ds(tap_at[k] + token + k, block)]
+            total = total.reshape(size, LANES)
+            inner_ref[at_rows(part, size), lanes] = total.astype(BF)
+
+            @pl.when(part == rows // size - 1)
+            def _():
+                tail[:, lanes] = total[size - tail.shape[0] :]
+
+            return carry
+
+        lax.fori_loop(0, rows // size, gather, 0)
+        first = [zero] * (tail.shape[0] // seqs - past)
+        for token in range(past):
+            total = zero
+            for k in range(past - token, past + 1):
+                total = total + held[tap_at[k] + token - past + k]
+            first.append(total)
+        edge[:, lanes] = jnp.concatenate(first, axis=0).astype(BF)
+        for k in range(tiles):
+
+            @pl.when(tile == k)
+            def _():
+                scatter.advance(tiles + 3 + k)
+
+        return carry
+
+    lax.fori_loop(0, tiles, convolve, 0)
+    hand = pltpu.make_async_remote_copy(
+        src_ref=edge,
+        dst_ref=from_next,
+        send_sem=edge_sems.at[0],
+        recv_sem=edge_sems.at[1],
+        device_id={"seq": lax.rem(place + count - 1, count)},
+        device_id_type=pl.DeviceIdType.MESH,
+    )
+
+    @pl.when(place > 0)
+    def _():
+        hand.start()
+
+    @pl.when(place < count - 1)
+    def _():
+        hand.wait_recv()
+        last_rows = pl.ds(rows - tail.shape[0], tail.shape[0])
+        inner_ref[last_rows, :] = (tail[...] + from_next[...].astype(F32)).astype(BF)
+
+    @pl.when(place > 0)
+    def _():
+        hand.wait_send()
+
+    trade[1].wait_send()
+    for turn in range(2 * tiles + 3, scatter.turns):
         scatter.advance(turn)
     scatter.finish()
+
+
+def stats_back(stats, projected, gains, states):
+    rank = LANES - 2 * states
+    lane = lax.broadcasted_iota(jnp.int32, stats.shape, 1)
+    parts = [
+        (lane < rank, rank),
+        ((lane >= rank) & (lane < rank + states), states),
+        (lane >= rank + states, states),
+    ]
+
+    def means(values):
+        total = jnp.zeros_like(values)
+        for inside, size in parts:
+            mean = jnp.sum(jnp.where(inside, values, 0.0), axis=1, keepdims=True) / size
+            total = jnp.where(inside, mean, total)
+        return total
+
+    scale = lax.rsqrt(means(projected * projected) + EPS)
+    normed = projected * scale
+    scaled = stats * gains
+    return scale * (scaled - normed * means(scaled * normed)), stats * normed
 
 
 class PairScatter:
@@ -605,7 +870,7 @@
                 total = self.mine_buf[item % 2, here, lanes].astype(F32) + self.given_buf[
                     item % 2, here, lanes
                 ].astype(F32)
-                self.sum_buf[item % 2, here, lanes] = total.astype(BF)
+                self.sum_buf[item % 2, here, lanes] = total.astype(self.sum_buf.dtype)
                 return carry
 
             lax.fori_loop(0, rows // 16, add, 0)
@@ -625,7 +890,8 @@
     rows = grads[0].shape[2]
     wide = max(grad.shape[3] for grad in grads)
     sems = pltpu.SemaphoreType.DMA((len(grads), count // 2))
-    return [pltpu.VMEM((2, rows, wide), BF)] * 3 + [sems] * 4 + [pltpu.SemaphoreType.DMA((2, 2))]
+    buffer = pltpu.VMEM((2, rows, wide), grads[0].dtype)
+    return [buffer] * 3 + [sems] * 4 + [pltpu.SemaphoreType.DMA((2, 2))]
 
 
 def exchange_scratch(count, seqs, states, channels):
@@ -636,7 +902,7 @@
     ] + [sems] * 4
 
 
-def state_call(body, ident, seqs, states, ins, outs, scratch, ops, hosted):
+def state_call(body, ident, seqs, states, columns, ins, outs, scratch, ops, hosted):
     count = lax.axis_size("seq")
     rows, channels = ins[1].shape
     in_vmem = pl.BlockSpec(memory_space=pltpu.VMEM)
@@ -646,7 +912,7 @@
         in_specs=[in_vmem] * (len(ins) - hosted[0]) + [anywhere] * hosted[0],
         out_specs=tuple([in_vmem] * (len(outs) - hosted[1]) + [anywhere] * hosted[1]),
         out_shape=tuple(outs),
-        scratch_shapes=[pltpu.VMEM((rows, 2 * (states + 1) * LANES), F32)] + scratch,
+        scratch_shapes=[pltpu.VMEM((rows, columns * LANES), F32)] + scratch,
         compiler_params=pltpu.CompilerParams(
             collective_id=ident, has_side_effects=True, vmem_limit_bytes=62 * 1024 * 1024
         ),
@@ -734,7 +1000,7 @@
     return [pltpu.SemaphoreType.DMA((pieces, around))] * 4 + [pltpu.SemaphoreType.DMA((1,))]
 
 
-def greet_pairs(count, heads=False):
+def greet_pairs(count, heads=False, ring=False):
     place = lax.axis_index("seq")
     around = count // 2
     low, high = lax.rem(place, 2), place // 2
@@ -745,6 +1011,8 @@
         head = lax.axis_index("head")
         low, high = lax.rem(head, 2), head // 2
         peers += [{"head": high * 2 + 1 - low}, {"head": 2 - 2 * high + low}]
+    if ring:
+        peers += [{"seq": lax.rem(place + 1, count)}, {"seq": lax.rem(place + count - 1, count)}]
     for device in peers:
         pl.semaphore_signal(barrier, inc=1, device_id=device, device_id_type=pl.DeviceIdType.MESH)
     pl.semaphore_wait(barrier, len(peers))
@@ -816,29 +1084,39 @@
             copy(chunk).wait_send()
 
 
+def put_sequences(target, rows_ref, chunk, size, buffer):
+    seqs = target.shape[0]
+    span = size // seqs
+    for m in range(buffer.shape[0]):
+        lanes = pl.ds(m * LANES, LANES)
+        buffer[m] = rows_ref[at_rows(chunk, size), lanes].astype(F32)
+        for k in range(seqs):
+            rows = buffer[m, pl.ds(k, span, stride=seqs), :]
+            target[k, at_rows(chunk, span), lanes] = rows.astype(target.dtype)
+
+
 def transposed_dot(left, right):
     return lax.dot_general(left, right, (((1,), (1,)), ((), ())), preferred_element_type=F32)
 
 
-def ffn_kernel(count, chunks, hosted, *refs):
-    g_ref, out_ref, x_ref, gain_ref, low_ref, dout_ref, *refs = refs
-    ready, refs = refs[: 3 - hosted], refs[3 - hosted :]
-    shards_in, refs = refs[:hosted], refs[hosted:]
+def ffn_kernel(count, chunks, *refs):
+    g_ref, out_ref, x_ref, gain_ref, low_ref, gate_ref, up_shard, down_shard, *refs = refs
     hidden_ref, norm_ref, act_ref, dgate_ref, dup_ref, dnorm_gain_ref, part_out_ref, *refs = refs
     dhidden_ref, dmix_ref, *refs = refs
-    landed, refs = refs[:hosted], refs[hosted:]
+    up_ref, down_ref, *refs = refs
     part_a, half_a, give_a, take_a, part_b, half_b, give_b, take_b, kept, *refs = refs
     sems_a, sems_b, *refs = refs
     gathers = [
-        BlockGather(count, shards_in[k], landed[k], refs[5 * k : 5 * k + 5]) for k in range(hosted)
+        BlockGather(count, up_shard, up_ref, refs[:5]),
+        BlockGather(count, down_shard, down_ref, refs[5:]),
     ]
-    gate_ref, up_ref, down_ref = list(ready) + list(landed)
     mix = HeadSum(part_a, half_a, give_a, take_a, norm_ref, sems_a)
     back = HeadSum(part_b, half_b, give_b, take_b, dmix_ref, sems_b)
     size = g_ref.shape[0] // chunks
     quarter = size // 4
     width = x_ref.shape[1]
-    shard, units = gate_ref.shape[1:]
+    shard, units = down_ref.shape[1:]
+    channels = g_ref.shape[1]
     greet_pairs(count, True)
     for gather in gathers:
         gather.start()
@@ -847,7 +1125,8 @@
 
     def project(chunk, carry):
         here = at_rows(chunk, size)
-        part_a[here, :] = transposed_dot(g_ref[here, :], out_ref[...]).astype(BF)
+        weights = out_ref[:, :, pl.ds(channels, channels)].reshape(width, channels)
+        part_a[here, :] = transposed_dot(g_ref[here, :], weights).astype(BF)
         mix.near_copy(chunk).start()
         return carry
 
@@ -862,7 +1141,8 @@
     def normalise(chunk, carry):
         mix.far_copy(chunk).wait_recv()
         here = at_rows(chunk, quarter)
-        hidden = x_ref[here, :] + kept[chunk] + take_a[chunk].astype(F32)
+        own = x_ref[mix.own_rows(chunk), :].astype(F32)
+        hidden = own + kept[chunk] + take_a[chunk].astype(F32)
         hidden_ref[here, :] = hidden
         scale = lax.rsqrt(jnp.mean(hidden * hidden, axis=1, keepdims=True) + EPS)
         norm_ref[mix.own_rows(chunk), :] = (hidden * scale * gain_ref[...]).astype(BF)
@@ -941,7 +1221,8 @@
         dnorm_gain_ref[...] += jnp.sum(d_norm * normed, axis=0, keepdims=True)
         scaled = d_norm * gain_ref[...]
         shift = jnp.mean(scaled * normed, axis=1, keepdims=True)
-        d_hidden = dout_ref[here, :] + scale * (scaled - normed * shift)
+        own = low_ref[back.own_rows(chunk), :].astype(F32)
+        d_hidden = own + scale * (scaled - normed * shift)
         dhidden_ref[here, :] = d_hidden
         dmix_ref[back.own_rows(chunk), :] = d_hidden.astype(BF)
         back.far_back(chunk).start()
@@ -968,20 +1249,30 @@
 CHUNKS = 4
 
 
-def ffn_call(g_low, out_t, x_own, gain, grad_low, dout_own, ready, waiting):
-    count = lax.axis_size("seq")
-    rows, width = grad_low.shape
-    units = waiting[0].shape[1]
+def sum_scratch(rows, width, part=True):
     chunk = rows // CHUNKS
-    shape = jax.ShapeDtypeStruct
-    in_vmem = pl.BlockSpec(memory_space=pltpu.VMEM)
-    anywhere = pl.BlockSpec(memory_space=pl.ANY)
-    sums = [
-        pltpu.VMEM((rows, width), BF),
+    parts = [pltpu.VMEM((rows, width), BF)] if part else []
+    return parts + [
         pltpu.VMEM((CHUNKS, chunk // 2, width), BF),
         pltpu.VMEM((CHUNKS, chunk // 4, width), BF),
         pltpu.VMEM((CHUNKS, chunk // 4, width), BF),
     ]
+
+
+def kept_scratch(rows, width):
+    return pltpu.VMEM((CHUNKS, rows // CHUNKS // 4, width), F32)
+
+
+SUM_SEMS = pltpu.SemaphoreType.DMA((4, 2, CHUNKS))
+
+
+def ffn_call(g_low, mix_blocks, x_low, gain, grad_low, gate_blocks, w_up, w_down_t):
+    count = lax.axis_size("seq")
+    rows, width = grad_low.shape
+    units = w_down_t.shape[1]
+    shape = jax.ShapeDtypeStruct
+    in_vmem = pl.BlockSpec(memory_space=pltpu.VMEM)
+    anywhere = pl.BlockSpec(memory_space=pl.ANY)
     outs = [
         shape((rows // 4, width), F32),
         shape((rows, width), BF),
@@ -994,23 +1285,308 @@
         shape((rows, width), BF),
     ]
     return pl.pallas_call(
-        functools.partial(ffn_kernel, count, CHUNKS, len(waiting)),
-        in_specs=[in_vmem] * (6 + len(ready)) + [anywhere] * len(waiting),
+        functools.partial(ffn_kernel, count, CHUNKS),
+        in_specs=[in_vmem] * 6 + [anywhere] * 2,
         out_specs=tuple([in_vmem] * len(outs)),
         out_shape=tuple(outs),
-        scratch_shapes=[pltpu.VMEM((count,) + w.shape, BF) for w in waiting]
-        + sums
-        + sums
-        + [pltpu.VMEM((CHUNKS, chunk // 4, width), F32)]
-        + [pltpu.SemaphoreType.DMA((4, 2, CHUNKS))] * 2
-        + [sem for w in waiting for sem in gather_sems(count // 2, w.shape[1])],
+        scratch_shapes=[pltpu.VMEM((count,) + w_down_t.shape, BF)] * 2
+        + sum_scratch(rows, width)
+        + sum_scratch(rows, width)
+        + [kept_scratch(rows, width)]
+        + [SUM_SEMS] * 2
+        + gather_sems(count // 2, units) * 2,
         compiler_params=pltpu.CompilerParams(
             collective_id=5, has_side_effects=True, vmem_limit_bytes=62 * 1024 * 1024
         ),
         cost_estimate=pl.CostEstimate(
             flops=14 * rows * width * units, bytes_accessed=40 * 1024 * 1024, transcendentals=0
         ),
-    )(g_low, out_t, x_own, gain, grad_low, dout_own, *ready, *waiting)
+    )(g_low, mix_blocks, x_low, gain, grad_low, gate_blocks, w_up, w_down_t)
+
+
+def input_kernel(count, chunks, kinds, *refs):
+    inner_ref, z_ref, in_x_ref, mix_ref, x_ref, norm_ref, gain_ref, dhidden_ref, *refs = refs
+    pack_ref, refs = refs[0], refs[1:]
+    olds, refs = [refs[k * kinds : (k + 1) * kinds] for k in range(3)], refs[3 * kinds :]
+    out_ref, gain_out_ref, *refs = refs
+    own_refs, refs = refs[: kinds + 1], refs[kinds + 1 :]
+    pack_given, pack_came, *refs = refs
+    part, half, give, take, kept, rows_ref, buffer, sems, *refs = refs
+    sent, got, vector_sems, grad_ref, given, came, *refs = refs
+    owned = OwnSum(count, olds, own_refs, refs[:3])
+    refs = refs[3:]
+    scatter = PairScatter(count, [grad_ref], [given], [came], refs[:8])
+    pack = PairScatter(count, [pack_ref], [pack_given], [pack_came], refs[8:])
+    back = HeadSum(part, half, give, take, rows_ref, sems)
+    size = inner_ref.shape[0] // chunks
+    quarter = size // 4
+    shard, channels = in_x_ref.shape[1:]
+    per_block = max(1, count // 4)
+    wide = per_block * shard
+    greet_pairs(count, True)
+    pack.start()
+    owned.load(0)
+    around, _, shard_rows, _ = grad_ref.shape
+    together = max(1, 384 // (2 * shard_rows))
+    for block in range(around // together):
+        lanes = pl.ds(block * together * 2 * shard_rows, together * 2 * shard_rows)
+        grad = jnp.dot(norm_ref[:, lanes].T, inner_ref[...], preferred_element_type=F32)
+        grad = grad.astype(BF).reshape(together, 2, shard_rows, channels)
+        grad_ref[pl.ds(block * together, together)] = grad
+    scatter.start()
+    turns = [(scatter, turn) for turn in range(scatter.turns)]
+    turns += [(pack, turn) for turn in range(pack.turns)]
+    share = -(-len(turns) // (3 * chunks))
+    early = 2 * chunks * share
+
+    def move(chunk, stage):
+        for k in range(chunks):
+            todo = turns[(stage * chunks + k) * share :][:share]
+            if todo:
+
+                @pl.when(chunk == k)
+                def _():
+                    for moving, turn in todo:
+                        moving.advance(turn)
+
+    def own_step(chunk, first):
+        for k in range(chunks):
+            if first + k < kinds:
+
+                @pl.when(chunk == k)
+                def _():
+                    owned.add(first + k)
+
+    def project(chunk, carry):
+        here = at_rows(chunk, size)
+        for k in range(count // per_block):
+            blocks = pl.ds(k * per_block, per_block)
+            total = transposed_dot(inner_ref[here, :], in_x_ref[blocks].reshape(wide, channels))
+            in_z = mix_ref[blocks, :, pl.ds(0, channels)].reshape(wide, channels)
+            total = total + transposed_dot(z_ref[here, :], in_z)
+            part[here, pl.ds(k * wide, wide)] = total.astype(BF)
+        back.near_copy(chunk).start()
+        return carry
+
+    lax.fori_loop(0, chunks, project, 0)
+
+    def fold(chunk, carry):
+        back.fold(chunk, kept)
+        own_step(chunk, 0)
+        return carry
+
+    lax.fori_loop(0, chunks, fold, 0)
+    gain_out_ref[...] = jnp.zeros(gain_out_ref.shape, F32)
+    around = scatter.around
+
+    def vector(stage, slot, device):
+        return pltpu.make_async_remote_copy(
+            src_ref=sent.at[stage],
+            dst_ref=got.at[slot],
+            send_sem=vector_sems.at[0, slot],
+            recv_sem=vector_sems.at[1, slot],
+            device_id=device,
+            device_id_type=pl.DeviceIdType.MESH,
+        )
+
+    stages = [
+        [vector(0, 0, {"seq": scatter.high * 2 + 1 - scatter.low})],
+        [
+            vector(1, steps, {"seq": scatter.pair(steps) * 2 + scatter.low})
+            for steps in range(1, around)
+        ],
+        [vector(2, around, back.near)],
+        [vector(3, around + 1, back.far)],
+    ]
+
+    def pass_sum(stage):
+        value = gain_out_ref[...]
+        if stage > 0:
+            for copy in stages[stage - 1]:
+                copy.wait_recv()
+            slots = [[0], list(range(1, around)), [around], [around + 1]][stage - 1]
+            for slot in slots:
+                value = value + got[slot]
+            gain_out_ref[...] = value
+        if stage < len(stages):
+            sent[stage] = value
+            for copy in stages[stage]:
+                copy.start()
+
+    def turn(chunk, carry):
+        back.far_copy(chunk).wait_recv()
+        here = at_rows(chunk, quarter)
+        values = x_ref[back.own_rows(chunk), :].astype(F32)
+        scale = lax.rsqrt(jnp.mean(values * values, axis=1, keepdims=True) + EPS)
+        normed = values * scale
+        d_norm = kept[chunk] + take[chunk].astype(F32)
+        share_of_sum = jnp.sum(d_norm * normed, axis=0, keepdims=True)
+        gain_out_ref[...] += jnp.broadcast_to(share_of_sum, gain_out_ref.shape)
+        scaled = d_norm * gain_ref[...]
+        shift = jnp.mean(scaled * normed, axis=1, keepdims=True)
+        total = dhidden_ref[here, :] + scale * (scaled - normed * shift)
+        rows_ref[back.own_rows(chunk), :] = total.astype(BF)
+        back.far_back(chunk).start()
+        move(chunk, 0)
+        return carry
+
+    lax.fori_loop(0, chunks, turn, 0)
+    pass_sum(0)
+
+    def spread_out(chunk, carry):
+        back.far_back(chunk).wait_recv()
+        back.near_back(chunk).start()
+        move(chunk, 1)
+        own_step(chunk, chunks)
+        return carry
+
+    lax.fori_loop(0, chunks, spread_out, 0)
+    for stage in range(1, len(stages) + 1):
+        pass_sum(stage)
+    for old in range(2 * chunks, kinds):
+        owned.add(old)
+    for moving, turn in turns[early:]:
+        moving.advance(turn)
+    for copies in stages:
+        for copy in copies:
+            copy.wait_send()
+
+    def finish(chunk, carry):
+        back.near_back(chunk).wait_recv()
+        put_sequences(out_ref, rows_ref, chunk, size, buffer)
+        back.finish(chunk)
+        return carry
+
+    lax.fori_loop(0, chunks, finish, 0)
+    scatter.finish()
+    pack.finish()
+    place = lax.axis_index("seq")
+    total = grad_ref[place // 2, lax.rem(place, 2)].astype(F32) + given[0].astype(F32)
+    for k in range(around - 1):
+        total = total + came[k].astype(F32)
+    own_refs[kinds][...] = total
+    owned.finish()
+
+
+class OwnSum:
+    def __init__(self, count, olds, targets, scratch):
+        self.place = lax.axis_index("seq")
+        self.around = count // 2
+        self.grads, self.given, self.came = olds
+        self.targets = targets
+        self.parts, self.total, self.sems = scratch
+
+    def sources(self, kind):
+        own = self.grads[kind].at[self.place // 2, lax.rem(self.place, 2)]
+        came = [self.came[kind].at[k] for k in range(self.around - 1)]
+        return [own, self.given[kind].at[0]] + came
+
+    def loads(self, kind):
+        lanes = pl.ds(0, self.targets[kind].shape[1])
+        return [
+            pltpu.make_async_copy(source, self.parts.at[k, :, lanes], self.sems.at[k])
+            for k, source in enumerate(self.sources(kind))
+        ]
+
+    def store(self, kind):
+        lanes = pl.ds(0, self.targets[kind].shape[1])
+        return pltpu.make_async_copy(
+            self.total.at[:, lanes], self.targets[kind], self.sems.at[self.around + 1]
+        )
+
+    def load(self, kind):
+        for load in self.loads(kind):
+            load.start()
+
+    def add(self, kind):
+        for load in self.loads(kind):
+            load.wait()
+        if kind:
+            self.store(kind - 1).wait()
+        lanes = pl.ds(0, self.targets[kind].shape[1])
+
+        def one(row, carry):
+            here = at_rows(row, 16)
+            total = self.parts[0, here, lanes].astype(F32)
+            for k in range(1, self.around + 1):
+                total = total + self.parts[k, here, lanes].astype(F32)
+            self.total[here, lanes] = total
+            return carry
+
+        lax.fori_loop(0, self.total.shape[0] // 16, one, 0)
+        self.store(kind).start()
+        if kind + 1 < len(self.grads):
+            self.load(kind + 1)
+
+    def finish(self):
+        self.store(len(self.grads) - 1).wait()
+
+
+def moved_shapes(grads):
+    shape = jax.ShapeDtypeStruct
+    around = grads[0].shape[0]
+    given = [shape((around,) + grad.shape[2:], grad.dtype) for grad in grads]
+    return given + [shape((around - 1,) + grad.shape[2:], grad.dtype) for grad in grads]
+
+
+def input_call(d_inner, d_z, in_x_blocks, mix_blocks, x_low, x_norm, gain, d_hidden, pack, olds, dims):
+    count = lax.axis_size("seq")
+    around = count // 2
+    rows, channels = d_inner.shape
+    width = x_low.shape[1]
+    shape = jax.ShapeDtypeStruct
+    in_vmem = pl.BlockSpec(memory_space=pltpu.VMEM)
+    anywhere = pl.BlockSpec(memory_space=pl.ANY)
+    grads, given, came = olds
+    shard = grads[0].shape[2]
+    widest = max(grad.shape[3] for grad in grads)
+    moved = moved_shapes([pack])
+    late = shape((around, 2, shard, channels), BF)
+    return pl.pallas_call(
+        functools.partial(input_kernel, count, CHUNKS, len(grads)),
+        in_specs=[in_vmem] * 8 + [anywhere] * (3 * len(grads) + 1),
+        out_specs=tuple(
+            [in_vmem] * 2 + [anywhere] * len(grads) + [in_vmem] + [anywhere] * len(moved)
+        ),
+        out_shape=tuple(
+            [shape(dims, F32), shape((8, width), F32)]
+            + [shape((shard, grad.shape[3]), F32) for grad in grads]
+            + [shape((shard, channels), F32)]
+            + moved
+        ),
+        scratch_shapes=sum_scratch(rows, width)
+        + [kept_scratch(rows, width), pltpu.VMEM((rows, width), BF)]
+        + [pltpu.VMEM((width // LANES, rows // CHUNKS, LANES), F32), SUM_SEMS]
+        + [pltpu.VMEM((4, 8, width), F32), pltpu.VMEM((around + 2, 8, width), F32)]
+        + [pltpu.SemaphoreType.DMA((2, around + 2))]
+        + [pltpu.VMEM(late.shape, BF), pltpu.VMEM((around, shard, channels), BF)]
+        + [pltpu.VMEM((around - 1, shard, channels), BF)]
+        + [pltpu.VMEM((around + 1, shard, widest), BF), pltpu.VMEM((shard, widest), F32)]
+        + [pltpu.SemaphoreType.DMA((around + 2,))]
+        + scatter_scratch(count, [late])
+        + scatter_scratch(count, [pack]),
+        compiler_params=pltpu.CompilerParams(
+            collective_id=6, has_side_effects=True, vmem_limit_bytes=62 * 1024 * 1024
+        ),
+        cost_estimate=pl.CostEstimate(
+            flops=4 * rows * width * d_inner.shape[1],
+            bytes_accessed=40 * 1024 * 1024,
+            transcendentals=0,
+        ),
+    )(
+        d_inner,
+        d_z,
+        in_x_blocks,
+        mix_blocks,
+        x_low,
+        x_norm,
+        gain,
+        d_hidden,
+        pack,
+        *grads,
+        *given,
+        *came,
+    )
 
 
 def pairs_of(axis):
@@ -1106,15 +1682,35 @@
     return value
 
 
-def first_kernel(count, *refs):
-    kinds = len(refs) // 7
+def first_kernel(count, kinds, turned, *refs):
+    sources, plain, refs = refs[:kinds], refs[kinds : kinds + turned], refs[kinds + turned :]
+    targets, outs, refs = refs[:kinds], refs[kinds : kinds + turned], refs[kinds + turned :]
+    buffer, *refs = refs
     gathers = [
-        BlockGather(count, refs[k], refs[kinds + k], refs[2 * kinds + 5 * k : 2 * kinds + 5 * k + 5])
-        for k in range(kinds)
+        BlockGather(count, sources[k], targets[k], refs[5 * k : 5 * k + 5]) for k in range(kinds)
     ]
     greet_pairs(count)
     for gather in gathers:
         gather.start()
+    for source, target in zip(plain, outs):
+        seqs, tokens, _ = source.shape
+
+        def widen(k, carry):
+            for m in range(buffer.shape[0]):
+                lanes = pl.ds(m * LANES, LANES)
+                buffer[m, at_rows(k, tokens), :] = source[k, :, lanes].astype(F32)
+            return carry
+
+        lax.fori_loop(0, seqs, widen, 0)
+
+        def turn(pair, carry):
+            for m in range(buffer.shape[0]):
+                both = [buffer[m, pl.ds(2 * pair + k, seqs, stride=tokens), :] for k in range(2)]
+                both = jnp.concatenate(both, axis=0).astype(BF)
+                target[at_rows(pair, 2 * seqs), pl.ds(m * LANES, LANES)] = both
+            return carry
+
+        lax.fori_loop(0, tokens // 2, turn, 0)
     for gather in gathers:
         for piece in range(gather.pieces):
             gather.relay(piece)
@@ -1122,18 +1718,27 @@
         gather.finish()
 
 
-def first_gather(*values):
+def first_gather(values, plain):
     count = lax.axis_size("seq")
     around = count // 2
-    kinds = len(values)
+    seqs, tokens, width = plain[0].shape
+    shape = jax.ShapeDtypeStruct
+    in_vmem = pl.BlockSpec(memory_space=pltpu.VMEM)
+    anywhere = pl.BlockSpec(memory_space=pl.ANY)
     return pl.pallas_call(
-        functools.partial(first_kernel, count),
-        out_shape=tuple(jax.ShapeDtypeStruct((count,) + v.shape, v.dtype) for v in values),
-        in_specs=[pl.BlockSpec(memory_space=pl.ANY)] * kinds,
-        out_specs=tuple([pl.BlockSpec(memory_space=pl.ANY)] * kinds),
-        scratch_shapes=[sem for v in values for sem in gather_sems(around, v.shape[-1])],
-        compiler_params=pltpu.CompilerParams(collective_id=0, has_side_effects=True),
-    )(*values)
+        functools.partial(first_kernel, count, len(values), len(plain)),
+        out_shape=tuple(
+            [shape((count,) + v.shape, v.dtype) for v in values]
+            + [shape((seqs * tokens, width), BF) for _ in plain]
+        ),
+        in_specs=[anywhere] * len(values) + [in_vmem] * len(plain),
+        out_specs=tuple([anywhere] * len(values) + [in_vmem] * len(plain)),
+        scratch_shapes=[pltpu.VMEM((width // LANES, seqs * tokens, LANES), F32)]
+        + [sem for v in values for sem in gather_sems(around, v.shape[-1])],
+        compiler_params=pltpu.CompilerParams(
+            collective_id=0, has_side_effects=True, vmem_limit_bytes=40 * 1024 * 1024
+        ),
+    )(*values, *plain)
 
 
 def shards(
@@ -1195,8 +1800,9 @@
             [rest[:, gain_starts[k] : gain_starts[k + 1]].reshape(-1) for k in range(len(gains))],
         )
 
-    in_x_blocks, pack_blocks = first_gather(w_in_x.astype(BF), pack(fields, gains)[0].astype(BF))
-    full_in_x = in_x_blocks.reshape(width, channels)
+    in_x_blocks, pack_blocks, x_low, grad_low = first_gather(
+        [w_in_x.astype(BF), pack(fields, gains)[0].astype(BF)], [x_in, d_out]
+    )
     fulls, full_gains = unpack(pack_blocks)
     full_xproj, w_dt_cols, full_a_log, conv_cols, conv_b_col, bias_col, skip_col = fulls
     full_w_dt = w_dt_cols.T
@@ -1205,12 +1811,12 @@
     full_norm1, full_norm2, full_ssm_gain = full_gains
 
     w_mix = jnp.concatenate([w_in_z.astype(BF), w_out.astype(BF).T], axis=1)
-    w_wide = jnp.concatenate([w_gate.astype(BF), w_up.astype(BF)], axis=1)
-    full_wide = lax.all_gather(w_wide, "seq", axis=0, tiled=True)
-    hidden_units = w_gate.shape[1]
+    w_mix, in_x_blocks = lax.optimization_barrier((w_mix, in_x_blocks))
+    full_in_x = in_x_blocks.reshape(width, channels)
+    full_mix = lax.all_gather(w_mix, "seq", axis=0, tiled=True)
 
     norm1_vec = full_norm1.astype(F32)
-    x_rows = x_in.transpose(1, 0, 2).reshape(rows, width).astype(F32)
+    x_rows = x_low.astype(F32)
     ids = seg_ids.T.reshape(rows)
     normed1, scale_one = norm_rows(x_rows, norm1_vec)
     x_norm = normed1.astype(BF)
@@ -1243,178 +1849,164 @@
     part_two = (bc - part_one.astype(F32)).astype(BF)
     part_three = (bc - part_one.astype(F32) - part_two.astype(F32)).astype(BF)
     stops = ((1.0 - same_docs[1]) * STOP).astype(BF)
-    spare = jnp.zeros((rows, LANES - 6 * states - 1), BF)
-    parts = jnp.concatenate([part_one, part_two, part_three, stops, spare], axis=1)
+    masks = [same.astype(BF) for same in same_docs[1:]]
+    spare = jnp.zeros((rows, LANES - 6 * states - taps), BF)
+    parts = jnp.concatenate([part_one, part_two, part_three, stops] + masks + [spare], axis=1)
     shape = jax.ShapeDtypeStruct
     state_rows = states * seqs
-    step, full_wide = lax.optimization_barrier((step, full_wide))
-    full_gate, full_up = full_wide[:, :hidden_units], full_wide[:, hidden_units:]
     start, step_sum = state_call(
         entry_kernel,
         1,
         seqs,
         states,
+        2 * states + 2,
         [parts, step, u_low, rate_rows],
         [shape((state_rows, channels), F32), shape((seqs, channels), F32)],
         exchange_scratch(count, seqs, states, channels),
         6,
         (0, 0),
     )
-    y_state, mix_blocks = state_call(
+    start, full_mix = lax.optimization_barrier((start, full_mix))
+    mix_blocks = full_mix.reshape(count, -1, full_mix.shape[1])
+    w_gate_low = w_gate.astype(BF)
+    y_state, gate_blocks = state_call(
         forward_kernel,
         2,
         seqs,
         states,
-        [parts, step, u_low, rate_rows, start, w_mix],
-        [shape((rows, channels), F32), shape((count,) + w_mix.shape, BF)],
-        gather_sems(count // 2, w_mix.shape[1]),
+        2 * states + 2,
+        [parts, step, u_low, rate_rows, start, w_gate_low],
+        [shape((rows, channels), F32), shape((count,) + w_gate.shape, BF)],
+        gather_sems(count // 2, w_gate.shape[1]),
         8,
         (1, 1),
     )
-    full_mix = mix_blocks.reshape(width, 2 * channels)
-    full_in_z, full_out_t = full_mix[:, :channels], full_mix[:, channels:]
+    full_in_z = full_mix[:, :channels]
     z_gate = jnp.dot(x_norm, full_in_z, preferred_element_type=F32)
     skip_vec = full_d_skip.astype(F32)
     u_rows = u_low.astype(F32)
     y_full = y_state + skip_vec * u_rows
     silu_z = jax.nn.silu(z_gate)
     g_low = (y_full * silu_z).astype(BF)
-    grad_low = d_out.transpose(1, 0, 2).reshape(rows, width)
-    blocks = lambda full: full.reshape(count, -1, full.shape[1])
     hidden, x_norm2, act_low, d_gate, d_up, norm2_sums, ffn_part, d_hidden, d_mix = ffn_call(
         g_low,
-        full_out_t,
-        head_part(x_rows),
+        mix_blocks,
+        x_low,
         full_norm2.astype(F32)[None, :],
         grad_low,
-        head_part(grad_low).astype(F32),
-        [blocks(full_gate), blocks(full_up)],
-        [w_down.astype(BF).T],
+        gate_blocks,
+        w_up.astype(BF),
+        w_down.astype(BF).T,
     )
     grad_norm2 = norm2_sums[0]
-    grad_down = jnp.einsum("rd,rf->df", grad_low, act_low, preferred_element_type=F32)
-    grad_gate = jnp.einsum("rd,rf->df", x_norm2, d_gate, preferred_element_type=F32)
-    grad_up = jnp.einsum("rd,rf->df", x_norm2, d_up, preferred_element_type=F32)
-    ffn_own = head_scatter(ffn_part)
     grad_out_w = jnp.einsum("rd,re->de", d_mix, g_low, preferred_element_type=F32)
+    full_out_t = full_mix[:, channels:]
     d_g = jnp.dot(d_mix, full_out_t, preferred_element_type=F32)
     d_y = d_g * silu_z
     d_z = (d_g * y_full * silu_slope(z_gate)).astype(BF)
     grad_skip = jnp.sum(d_y * u_rows, axis=0)
-    grad_in_z = jnp.einsum("rd,re->de", x_norm, d_z, preferred_element_type=F32)
-    big_grads = [
-        owner_blocks(grad.astype(BF))
-        for grad in (grad_down, grad_gate, grad_up, grad_out_w, grad_in_z)
-    ]
-    (last,) = state_call(
+    grad_block = shape((count // 2, 2, width // count, w_gate.shape[1]), BF)
+    last, grad_down, grad_gate, grad_up, block_out = state_call(
         adjoint_kernel,
         3,
         seqs,
         states,
-        [parts, step, d_y, rate_rows, step_sum],
-        [shape((state_rows, channels), F32)],
-        exchange_scratch(count, seqs, states, channels),
+        states + 2,
+        [parts, step, d_y, rate_rows, step_sum, x_norm2, grad_low, act_low, d_gate, d_up]
+        + [ffn_part, hidden],
+        [shape((state_rows, channels), F32)] + [grad_block] * 3 + [shape(x_in.shape, BF)],
+        exchange_scratch(count, seqs, states, channels)
+        + sum_scratch(rows, width, False)
+        + [kept_scratch(rows, width), pltpu.VMEM((rows, width), BF)]
+        + [pltpu.VMEM((width // LANES, rows // CHUNKS, LANES), F32), SUM_SEMS],
         6,
         (0, 0),
     )
-    last, ffn_own = lax.optimization_barrier((last, ffn_own))
-    block_rows = head_gather((hidden + ffn_own).astype(BF))
-    d_u_state, d_pre_low, d_bc, d_log, d_bias, *moved = state_call(
+    grad_in_z = jnp.einsum("rd,re->de", x_norm, d_z, preferred_element_type=F32)
+    big_grads = [grad_down, grad_gate, grad_up]
+    big_grads += [owner_blocks(grad.astype(BF)) for grad in (grad_out_w, grad_in_z)]
+    padded = lambda value: jnp.pad(value, ((0, 0), (0, LANES - value.shape[1])))
+    taps_table = jnp.concatenate([conv_weight, skip_vec[None, :]], axis=0)
+    taps_table = jnp.pad(taps_table, ((0, 2 * taps - taps_table.shape[0]), (0, 0)))
+    big_ins = [x_conv, extended.reshape(-1, seqs, channels), projected] + big_grads
+    block_rows_moved = moved_shapes(big_grads)
+    bf_rows = pltpu.VMEM((4 * seqs, channels), BF)
+    d_inner_low, ssm_sums, grad_xproj, grad_step_t, d_log, column_sums, *first_moved = state_call(
         backward_kernel,
         4,
         seqs,
         states,
-        [parts, step, u_low, d_y, rate_rows, start, last] + big_grads,
+        2 * states + 2,
+        [parts, step, u_low, d_y, rate_rows, start, last, padded(dt_low)]
+        + [padded(w_dt_cols), full_xproj, ssm_vec[None, :], taps_table]
+        + big_ins,
         [
-            shape((rows, channels), F32),
             shape((rows, channels), BF),
-            shape((rows, LANES), F32),
+            shape((8, LANES), F32),
+            shape((channels, LANES), F32),
+            shape((channels, LANES), F32),
             shape((states, channels), F32),
-            shape((seqs, channels), F32),
+            shape(((taps + 2) * seqs, channels), F32),
         ]
-        + [shape((count // 2,) + grad.shape[2:], BF) for grad in big_grads]
-        + [shape((count // 2 - 1,) + grad.shape[2:], BF) for grad in big_grads],
+        + block_rows_moved,
         [
             pltpu.VMEM(((tokens + 1) * states, seqs, LANES), F32),
             pltpu.VMEM((rows, 2 * states * LANES), F32),
+            pltpu.VMEM((rows, channels), F32),
+            pltpu.VMEM((rows, channels), BF),
+            pltpu.VMEM((2, rows, LANES), BF),
+            pltpu.VMEM((2, rows, LANES), BF),
+            pltpu.VMEM((4 * seqs, channels), F32),
+            bf_rows,
+            bf_rows,
+            pltpu.SemaphoreType.DMA((2, 2)),
+            pltpu.SemaphoreType.DMA((2,)),
+            pltpu.SemaphoreType.DMA((channels // LANES + 2,)),
         ]
         + scatter_scratch(count, big_grads),
         30,
-        (len(big_grads), 2 * len(big_grads)),
-    )
-    d_bc, block_rows = lax.optimization_barrier((d_bc, block_rows))
-    block_out = block_rows.reshape(tokens, seqs, width).transpose(1, 0, 2)
-    own_down, own_gate, own_up, own_out, own_in_z = (
-        scatter_own(grad, given, came)
-        for grad, given, came in zip(big_grads, moved[: len(big_grads)], moved[len(big_grads) :])
+        (len(big_ins), len(block_rows_moved)),
     )
     grad_alog = d_log.T * rates
-    grad_bias = jnp.sum(d_bias, axis=0)
-    grad_step_w = jnp.einsum("rk,re->ke", dt_low, d_pre_low, preferred_element_type=F32)
-    d_dt_part = jnp.einsum("re,ke->rk", d_pre_low, full_w_dt, preferred_element_type=F32)
-    d_stats = head_total(jnp.concatenate([d_dt_part, d_bc[:, : 2 * states]], axis=1), BF)
-    d_dt_raw, grad_dt_gain = norm_back(
-        projected[:, :rank], dt_scale, ssm_vec[:rank], d_stats[:, :rank]
-    )
-    d_b_raw, grad_b_gain = norm_back(
-        projected[:, rank:b_end], b_scale, ssm_vec[rank:b_end], d_stats[:, rank:b_end]
-    )
-    d_c_raw, grad_c_gain = norm_back(
-        projected[:, b_end:], c_scale, ssm_vec[b_end:], d_stats[:, b_end:]
-    )
-    d_proj = jnp.concatenate([d_dt_raw, d_b_raw, d_c_raw], axis=1)
-    grad_ssm = jnp.concatenate([grad_dt_gain, grad_b_gain, grad_c_gain])
-    grad_xproj = jnp.einsum("re,rk->ek", u_low, d_proj, preferred_element_type=F32)
-    d_u = (
-        d_y * skip_vec
-        + d_u_state
-        + jnp.einsum("rk,ek->re", d_proj, full_xproj, preferred_element_type=F32)
-    )
-    d_conv = d_u * silu_slope(x_conv)
-    grad_conv_b = jnp.sum(d_conv, axis=0)
-    d_extended = jnp.zeros((rows + halo, channels), F32)
-    conv_grads = []
-    for offset in range(taps):
-        first = (taps - 1 - offset) * seqs
-        masked = d_conv * same_docs[offset]
-        conv_grads.append(jnp.sum(masked * extended[first : first + rows], axis=0))
-        d_extended = d_extended + jnp.pad(
-            conv_weight[offset] * masked, ((first, halo - first), (0, 0))
-        )
-    grad_conv_w = jnp.stack(conv_grads)
-    from_next = shifted(d_extended[:halo].astype(BF), "seq", -1).astype(F32)
-    d_inner = d_extended[halo:] + jnp.pad(from_next, ((rows - halo, 0), (0, 0)))
-    d_inner_low = d_inner.astype(BF)
-    grad_in_x = jnp.einsum("rd,re->de", x_norm, d_inner_low, preferred_element_type=F32)
-    d_norm1 = head_scatter(
-        jnp.einsum("re,de->rd", d_inner_low, full_in_x, preferred_element_type=F32)
-        + jnp.einsum("re,de->rd", d_z, full_in_z, preferred_element_type=F32)
-    )
-    d_input_part, grad_norm1 = norm_back(head_part(x_rows), head_part(scale_one), norm1_vec, d_norm1)
-    input_rows = head_gather((d_hidden + d_input_part).astype(BF)).astype(F32)
-    grad_input = input_rows.reshape(tokens, seqs, width).transpose(1, 0, 2)
-
+    columns = jnp.sum(column_sums.reshape(taps + 2, seqs, channels), axis=1)
+    grad_ssm = ssm_sums[0]
     grad_ssm = grad_ssm * (lax.axis_index("head") == 0).astype(F32)
     small = pack(
         [
             grad_xproj,
-            grad_step_w.T,
+            grad_step_t[:, :rank],
             grad_alog,
-            grad_conv_w.T,
-            grad_conv_b[:, None],
-            grad_bias[:, None],
+            columns[:taps].T,
+            columns[taps][:, None],
+            columns[taps + 1][:, None],
             grad_skip[:, None],
         ],
-        [grad_norm1, grad_norm2, grad_ssm],
+        [jnp.zeros_like(grad_norm2), grad_norm2, grad_ssm],
     )
-    small = scatter_rows(small.reshape(-1, pack_width), F32)
+    small = owner_blocks(small.reshape(-1, pack_width))
+    kinds = len(big_grads)
+    grad_input, norm1_sums, *owns, pack_given, pack_came = input_call(
+        d_inner_low,
+        d_z,
+        in_x_blocks,
+        mix_blocks,
+        x_low,
+        x_norm,
+        norm1_vec[None, :],
+        d_hidden,
+        small,
+        (big_grads, first_moved[:kinds], first_moved[kinds:]),
+        x_in.shape,
+    )
+    own_down, own_gate, own_up, own_out, own_in_z, own_in_x = owns
+    small = scatter_own(small, pack_given, pack_came)
+    own_norm1 = lax.dynamic_slice_in_dim(norm1_sums[0], place * (width // count), width // count)
     small = jnp.concatenate([small[:per], head_total(small[per:], F32)])[None]
     small_fields, small_gains = unpack(small)
-    own_in_x = scatter_rows(grad_in_x)
     return (
         block_out,
         grad_input,
-        small_gains[0],
+        own_norm1,
         own_in_x,
         own_in_z,
         small_fields[3].T,

time: 853 us -> 783 us (0.918)
  Pallas kernels: 513 us -> 642 us
  matrix products: 82.6 us -> 33.4 us
  other arithmetic: 74.7 us -> 29 us
  waiting for transfers between devices: 41.2 us -> 3.86 us
  local copies, waits for them, and re-layouts: 78.1 us -> 42.5 us
  starting transfers between devices: 40.9 us -> 11.4 us
    pallas_call x2 -> x3, Pallas kernels: 172 us -> 279 us  [the longest x1 150 us: ffn_call(): pl.pallas_call(functools.partial(ffn_kernel, count, CHUNKS), in_specs=[in...]
    dot_general x10 -> x0, matrix products: 47 us -> none  [the longest x1 7.67 us: shards(): jnp.einsum('rd,rf->df', x_norm2, d_gate, preferred_element_type=F32)]
    ppermute x16 -> x4, waiting for transfers between devices: 30.5 us -> 2.15 us  [swap(): lax.ppermute(value, axis, [(s, s ^ bit) for s in range(lax.axis_size(axis...]
    pallas_call x4, Pallas kernels: 341 us -> 362 us  [state_call(): pl.pallas_call(functools.partial(body, count, seqs, states), in_specs=[in...]
    ppermute x6 -> x0, starting transfers between devices: 17.4 us -> none  [hop(): lax.ppermute(value, 'seq', [(s, (s + 2 * steps) % count) for s in range(c...]
    convert_element_type x10 -> x5, other arithmetic: 16.8 us -> 3.81 us  [the longest x1 1.93 us: shards(): w_up.astype(BF)]
    ppermute x6 -> x0, waiting for transfers between devices: 10.6 us -> none  [hop(): lax.ppermute(value, 'seq', [(s, (s + 2 * steps) % count) for s in range(c...]
    slice x5 -> x4, local copies, waits for them, and re-layouts: 11.8 us -> 1.17 us  [the longest x1 0.8 us: shards(): norm1_sums[0]]
  transfers between devices with their start and end apart: 26 -> 7, of which waited for: 11 -> 3; matrix products, arithmetic and copies ran while one was open for 18% -> 4% of each run, Pallas kernels for 35% -> 6%
where the time goes in v4:
time: 783 us; the launch traced here: 777 us
  Pallas kernels  642 us (82%)
  local copies, waits for them, and re-layouts  42.5 us (5%)
  matrix products  33.4 us (4%)
  other arithmetic  29 us (4%)
  between operations  15.1 us (2%)
  starting transfers between devices  11.4 us (1%)
    pallas_call x4, Pallas kernels, state_call(): pl.pallas_call(functools.partial(body, count, seqs, states), in_specs=[in...  362 us
    pallas_call x1, Pallas kernels, ffn_call(): pl.pallas_call(functools.partial(ffn_kernel, count, CHUNKS), in_specs=[in...  150 us
    pallas_call x1, Pallas kernels, input_call(): pl.pallas_call(functools.partial(input_kernel, count, CHUNKS, len(grads))...  84.3 us
    pallas_call x1, Pallas kernels, first_gather(): pl.pallas_call(functools.partial(first_kernel, count, len(values), len(pl...  45.4 us
    unnamed x72, local copies, waits for them, and re-layouts  23.5 us
  transfers between devices with their start and end apart: 7, of which 3 were waited for; matrix products, arithmetic and copies ran while one was open for 4% of the time, Pallas kernels for 6%

profile of v4, /device:TPU:0, one launch (start us, length us, event | category | flops | bytes accessed | tf_op | source)
XLA Modules:
  0.0 777.1 jit_solution(2227036001978087684)
XLA Ops:
  15.2 1.1 convert_element_type.240.refs_0_
  16.3 1.1 convert_bitcast_fusion.1
  19.4 1.9 copy-done.2
  21.3 45.4 %shard_map.322 = (bf16[8,192,768]{2,1,0:T(8,128)(2,1)S(1)}, bf16[8,112,256]{2,1,0:T(8,128)(2,1)S(1)}, bf16[1024,1536]{1,0:T(8,128)(2,1)S(1)}, bf16[1024,1536]{1,0:T(8,128)(2,1)S(1)}) custom-call(bf16[192,768]{1,0:T(8,128)(2,1)S(1)} %convert_element_type.240.refs_0_, bf16[112,256]{1,0:T(8,128)(2,1)S(1)} %maximum_bitcast_fusion.1.refs_1_, ...), custom_call_target="tpu_custom_call" | custom-call | tf_op jit(solution)/shard_map/pallas_call | solution.py:1728
  66.7 1.7 copy-done.1
  68.4 1.4 copy-done.3
  74.0 2.6 convolution_convert_fusion.2
  76.7 1.5 collective-permute-start
  78.4 6.1 collective-permute-start.1
  86.7 2.1 fusion.19
  88.8 3.9 multiply_convert_fusion.2
  94.9 1.6 collective-permute-start.3
  100.7 1.9 convert_element_type.289.refs_6_
  107.2 3.9 concatenate.56.parts_ref
  111.1 3.6 compare_select_fusion.step_ref
  114.7 44.2 %shard_map.323 = (f32[128,768]{1,0:T(8,128)}, f32[8,768]{1,0:T(8,128)}) custom-call(bf16[1024,128]{1,0:T(8,128)(2,1)} %concatenate.56.parts_ref, f32[1024,768]{1,0:T(8,128)} %compare_select_fusion.step_ref, bf16[1024,768]{1,0:T(8,128)(2,1)} %copy-done.7, f32[128,768]{1,0:T(8,128)} %broadcast_bitcast_fusion.rate_ref), custom_call_target="tpu_custom_call" | custom-call | flops 75497472 | bytes 16777216 | tf_op jit(solution)/shard_map/pallas_call | solution.py:910
  158.9 1.7 all-gather.2.cloned.1.call-done
  160.6 59.4 %shard_map.324 = (f32[1024,768]{1,0:T(8,128)}, bf16[8,192,1024]{2,1,0:T(8,128)(2,1)}) custom-call(bf16[1024,128]{1,0:T(8,128)(2,1)} %concatenate.56.parts_ref, f32[1024,768]{1,0:T(8,128)} %compare_select_fusion.step_ref, bf16[1024,768]{1,0:T(8,128)(2,1)} %copy-done.7, f32[128,768]{1,0:T(8,128)} %broadcast_bitcast_fusion.rate_ref, ...), custom_call_target="tpu_custom_call" | custom-call | flops 100663296 | bytes 16777216 | tf_op jit(solution)/shard_map/pallas_call | solution.py:910
  220.0 8.6 %multiply_convert_fusion.1 = (bf16[1024,768]{1,0:T(8,128)(2,1)}, f32[1024,768]{1,0:T(8,128)}) fusion(f32[1024,768]{1,0:T(8,128)} %get-tuple-element.77, bf16[1024,768]{1,0:T(8,128)(2,1)S(1)} %copy-done.8, f32[768]{0:T(1024)S(1)} %get-tuple-element.232, bf16[1024,1536]{1,0:T(8,128)(2,1)} %copy-done.10, bf16[1536,1536]{1,0:T(8,128)(2,1)} %all-gather.2.cloned.1.call-done), kind=kOutput, calls=%fused_computation.24 | convolution fusion | flops 2422996992 | bytes 14945280 | tf_op jit(solution)/shard_map/dot_general | solution.py:1885
  228.5 149.7 %shard_map.325 = (f32[256,1536]{1,0:T(8,128)}, bf16[1024,1536]{1,0:T(8,128)(2,1)}, bf16[1024,1024]{1,0:T(8,128)(2,1)}, bf16[1024,1024]{1,0:T(8,128)(2,1)}, bf16[...) custom-call(bf16[1024,768]{1,0:T(8,128)(2,1)} %get-tuple-element.271, ...), custom_call_target="tpu_custom_call" | custom-call | flops 22548578304 | bytes 41943040 | tf_op jit(solution)/shard_map/pallas_call | solution.py:1287
  378.3 6.6 convolution_convert_fusion.1
  385.0 7.3 fusion.4
  392.3 4.2 convolution_convert_fusion
  396.4 72.7 %shard_map.326 = (f32[128,768]{1,0:T(8,128)}, bf16[4,2,192,1024]{3,2,1,0:T(8,128)(2,1)}, bf16[4,2,192,1024]{3,2,1,0:T(8,128)(2,1)}, bf16[4,2,192,1024]{3,2,1,0:T(8,128)(2,1)}, bf16[8,128,1536]{2,1,0:T(8,128)(2,1)}) custom-call(bf16[1024,128]{1,0:T(8,128)(2,1)} %concatenate.56.parts_ref, f32[1024,768]{1,0:T(8,128)} %compare_select_fusion.step_ref, ...), custom_call_target="tpu_custom_call" | custom-call | flops 75497472 | bytes 16777216 | tf_op jit(solution)/shard_map/pallas_call | solution.py:910
  469.1 186.3 %shard_map.327 = (bf16[1024,768]{1,0:T(8,128)(2,1)}, f32[8,128]{1,0:T(8,128)}, f32[768,128]{1,0:T(8,128)}, f32[768,128]{1,0:T(8,128)}, f32[16,768]{1,0:T(8,128)}...) custom-call(bf16[1024,128]{1,0:T(8,128)(2,1)} %concatenate.56.parts_, ...), custom_call_target="tpu_custom_call" | custom-call | flops 377487360 | bytes 16777216 | tf_op jit(solution)/shard_map/pallas_call | solution.py:910
  658.1 1.8 concatenate.58
  661.9 84.3 %shard_map.328 = (f32[8,128,1536]{2,1,0:T(8,128)}, f32[8,1536]{1,0:T(8,128)}, f32[192,1024]{1,0:T(8,128)}, f32[192,1024]{1,0:T(8,128)}, f32[192,1024]{1,0:T(8,12...) custom-call(bf16[1024,768]{1,0:T(8,128)(2,1)} %get-tuple-element.94., ...), custom_call_target="tpu_custom_call" | custom-call | flops 4831838208 | bytes 41943040 | tf_op jit(solution)/shard_map/pallas_call | solution.py:1545
  746.2 1.1 fusion.24
  748.6 1.7 collective-permute-start.5
  751.0 1.4 collective-permute-done.5
  757.2 3.9 copy.199
  762.0 2.7 copy.200
  (190 shorter events, 44.8 us)
Async XLA Ops:
  7.2 153.4 %all-gather.2.cloned.1.call-start = ((), (), s32[]{:S(2)}) async-start(), calls=%async_computation | async-start | bytes 5308416 | tf_op jit(solution)/shard_map/all_gather | solution.py:1816
  19.4 1.9 copy-start.2
  66.7 1.7 copy-start.1
  70.5 2.6 copy-start
  72.4 1.7 copy-start.4
  73.2 3.5 copy-start.10
  74.0 4.1 copy-start.22
  74.0 10.5 %copy-start.6 = (bf16[8,112,256]{2,1,0:T(8,128)(2,1)S(1)}, bf16[8,112,256]{2,1,0:T(8,128)(2,1)}, u32[]{:S(2)}) copy-start(bf16[8,112,256]{2,1,0:T(8,128)(2,1)} %copy-done.5) | copy-start | bytes 1376260
  76.7 10.0 %collective-permute-start = (bf16[24,768]{1,0:T(8,128)(2,1)S(1)}, bf16[24,768]{1,0:T(8,128)(2,1)S(1)}, u32[]{:S(2)}, u32[]{:S(2)}) collective-permute-start(bf16[24,768]{1,0:T(8,128)(2,1)S(1)} %slice.252), channel_id=1, source_target_pairs={{0,4},{4,8},{8,12},{12,16},{16,20},{20,24},{24,28},{1,5},{5,9},{9,... | collective-permute-start | bytes 110600 | tf_op jit(solution)/shard_map/ppermute | solution.py:22
  78.4 8.1 %collective-permute-start.1 = (s32[24]{0:T(128)S(1)}, s32[24]{0:T(128)S(1)}, u32[]{:S(2)}, u32[]{:S(2)}) collective-permute-start(s32[24]{0:T(128)S(1)} %slice.197), channel_id=1, source_target_pairs={{0,4},{4,8},{8,12},{12,16},{16,20},{20,24},{24,28},{1,5},{5,9},{9,... | collective-permute-start | bytes 296 | tf_op jit(solution)/shard_map/ppermute | solution.py:22
  88.8 4.6 copy-start.14
  92.7 9.9 %copy-start.7 = (bf16[1024,768]{1,0:T(8,128)(2,1)}, bf16[1024,768]{1,0:T(8,128)(2,1)S(1)}, u32[]{:S(2)}) copy-start(bf16[1024,768]{1,0:T(8,128)(2,1)S(1)} %get-tuple-element.250.u_ref) | copy-start | bytes 4718596
  92.7 6.5 copy-start.15
  93.3 1.6 collective-permute-start.2
  94.9 9.2 %collective-permute-start.3 = (bf16[1024,128]{1,0:T(8,128)(2,1)S(1)}, bf16[1024,128]{1,0:T(8,128)(2,1)S(1)}, u32[]{:S(2)}, u32[]{:S(2)}) collective-permute-start(bf16[1024,128]{1,0:T(8,128)(2,1)S(1)} %add_convert_fusion), channel_id=1, source_target_pairs={{0,2},{1,3},{2,0},{3,1},{4,6},{5,7},{6,4},{7,5},{8,10},{9,11},{10,... | collective-permute-start | bytes 786440 | tf_op jit(solution)/shard_map/ppermute | solution.py:1602
  104.2 2.0 copy-start.9
  158.9 61.1 %copy-start.8 = (bf16[1024,768]{1,0:T(8,128)(2,1)S(1)}, bf16[1024,768]{1,0:T(8,128)(2,1)}, u32[]{:S(2)}) copy-start(bf16[1024,768]{1,0:T(8,128)(2,1)} %copy-done.7) | copy-start | bytes 4718596
  378.3 6.7 copy-start.24
  378.3 6.6 copy-start.25
  378.3 6.6 copy-start.26
  384.9 7.3 copy-start.11
  392.2 4.2 copy-start.13
  657.5 3.2 copy-start.23
  747.3 1.3 collective-permute-start.4
  748.6 3.8 collective-permute-start.5
  757.2 4.9 copy-start.12
  762.0 2.7 copy-start.21
  762.0 3.5 copy-start.20
  762.0 4.4 copy-start.19
  764.7 2.5 copy-start.18
  764.8 3.3 copy-start.17
  764.8 4.2 copy-start.16
  (2 other events, 2.1 us)
Sparse Core Ops, SparseCore 0:
  70.7 89.8 all-gather.1

commit v5 on v4

--- a/solution.py
+++ b/solution.py
@@ -346,22 +346,18 @@
     dy_ref,
     rate_ref,
     sum_ref,
-    norm_ref,
-    low_ref,
-    act_ref,
-    dgate_ref,
-    dup_ref,
-    part_ref,
-    hidden_ref,
-    last_ref,
-    gdown_ref,
-    ggate_ref,
-    gup_ref,
-    out_ref,
-    *scratch,
+    *refs,
 ):
+    sources, refs = refs[:7], refs[7:]
+    last_ref, gdown_ref, ggate_ref, gup_ref, out_ref, given_ref, came_ref, *scratch = refs
     spread_ref, ends, sums, *scratch = scratch
-    sems, (half, give, take, kept, block_ref, buffer, sum_sems) = scratch[:4], scratch[4:]
+    sems, scratch = scratch[:4], scratch[4:]
+    half, give, take, kept, block_ref, buffer, sum_sems, *scratch = scratch
+    targets, fetch_sems, scratch = scratch[:7], scratch[7], scratch[8:]
+    fetch = Fetch(sources, targets, fetch_sems)
+    part_ref, low_ref, act_ref, norm_ref, dgate_ref, dup_ref, hidden_ref = targets
+    fetch.start()
+    scatter = PairScatter(count, [gdown_ref], [given_ref], [came_ref], scratch)
     total = HeadSum(part_ref, half, give, take, block_ref, sum_sems)
     chunks = kept.shape[0]
     quarter = kept.shape[1]
@@ -373,8 +369,6 @@
     place = exchange.place
     zero = jnp.zeros((seqs, LANES), F32)
     greet_pairs(count, True)
-    for chunk in range(chunks):
-        total.near_copy(chunk).start()
     spread(parts_ref, states, spread_ref, states // 2)
 
     def own(tile, carry):
@@ -400,31 +394,38 @@
         return carry
 
     lax.fori_loop(0, tiles, own, 0)
+    fetch.wait(0, 1, 2, 3, 4, 5, 6)
     for chunk in range(chunks):
-        total.fold(chunk, kept)
+        total.near_copy(chunk).start()
     around, _, shard, units = gdown_ref.shape
     together = max(1, 384 // (2 * shard))
     wide = together * 2 * shard
 
+    def place_of(block):
+        return pl.ds(block * wide, wide), pl.ds(block * together, together)
+
     def multiply(block):
-        lanes = pl.ds(block * wide, wide)
-        pairs = pl.ds(block * together, together)
+        lanes, pairs = place_of(block)
         mine = norm_ref[:, lanes].T
         for d_ref, grad_ref in ((dgate_ref, ggate_ref), (dup_ref, gup_ref)):
             grad = jnp.dot(mine, d_ref[...], preferred_element_type=F32).astype(BF)
             grad_ref[pairs] = grad.reshape(together, 2, shard, units)
+
+    blocks = list(range(around // together))
+    for block in blocks:
+        lanes, pairs = place_of(block)
         grad = jnp.dot(low_ref[:, lanes].T, act_ref[...], preferred_element_type=F32).astype(BF)
         gdown_ref[pairs] = grad.reshape(together, 2, shard, units)
 
-    blocks = list(range(around // together))
-    for block in blocks[:2]:
-        multiply(block)
+    for chunk in range(chunks):
+        total.fold(chunk, kept)
 
     def pass_on(tile, carry):
         exchange.pass_on(tile)
         return carry
 
     lax.fori_loop(0, tiles, pass_on, 0)
+    scatter.start()
 
     def bring(chunk, carry):
         total.far_copy(chunk).wait_recv()
@@ -435,14 +436,19 @@
         return carry
 
     lax.fori_loop(0, chunks, bring, 0)
+    for block in blocks[:2]:
+        multiply(block)
+    scatter.advance(0)
     for block in blocks[2:]:
         multiply(block)
+    scatter.advance(1)
     finish_exchange(exchange, tiles, lambda first, lanes: lax.fori_loop(
         0,
         count - 1 - place,
         lambda hop, state: chained(state, ends, sums, rate_ref, count - 1 - hop, lanes, seqs),
         first,
     ), last_ref, states, zero, False)
+    scatter.advance(2)
 
     def spread_out(chunk, carry):
         total.far_back(chunk).wait_recv()
@@ -450,6 +456,8 @@
         return carry
 
     lax.fori_loop(0, chunks, spread_out, 0)
+    for moment in range(3, scatter.turns):
+        scatter.advance(moment)
 
     def finish(chunk, carry):
         total.near_back(chunk).wait_recv()
@@ -458,6 +466,7 @@
         return carry
 
     lax.fori_loop(0, chunks, finish, 0)
+    scatter.finish()
 
 
 def backward_kernel(
@@ -1079,8 +1088,9 @@
                 self.give[chunk] = total.astype(BF)
                 self.far_copy(chunk).start()
 
-    def finish(self, chunk):
-        for copy in (self.near_copy, self.far_copy, self.far_back, self.near_back):
+    def finish(self, chunk, near=True):
+        copies = [self.far_copy, self.far_back, self.near_back]
+        for copy in copies + [self.near_copy] * near:
             copy(chunk).wait_send()
 
 
@@ -1100,18 +1110,22 @@
 
 
 def ffn_kernel(count, chunks, *refs):
-    g_ref, out_ref, x_ref, gain_ref, low_ref, gate_ref, up_shard, down_shard, *refs = refs
+    g_ref, out_ref, gain_ref, *refs = refs
+    sources, up_shard, down_shard, refs = refs[:3], refs[3], refs[4], refs[5:]
     hidden_ref, norm_ref, act_ref, dgate_ref, dup_ref, dnorm_gain_ref, part_out_ref, *refs = refs
     dhidden_ref, dmix_ref, *refs = refs
     up_ref, down_ref, *refs = refs
-    part_a, half_a, give_a, take_a, part_b, half_b, give_b, take_b, kept, *refs = refs
-    sems_a, sems_b, *refs = refs
+    part, half_a, give_a, take_a, half_b, give_b, take_b, kept, *refs = refs
+    gate_buf, up_buf, sems_a, sems_b, *refs = refs
+    x_ref, gate_ref, low_ref, fetch_sems, *refs = refs
+    fetch = Fetch(sources, (x_ref, gate_ref, low_ref), fetch_sems)
+    fetch.start()
     gathers = [
         BlockGather(count, up_shard, up_ref, refs[:5]),
         BlockGather(count, down_shard, down_ref, refs[5:]),
     ]
-    mix = HeadSum(part_a, half_a, give_a, take_a, norm_ref, sems_a)
-    back = HeadSum(part_b, half_b, give_b, take_b, dmix_ref, sems_b)
+    mix = HeadSum(part, half_a, give_a, take_a, norm_ref, sems_a)
+    back = HeadSum(part, half_b, give_b, take_b, dmix_ref, sems_b)
     size = g_ref.shape[0] // chunks
     quarter = size // 4
     width = x_ref.shape[1]
@@ -1120,13 +1134,23 @@
     greet_pairs(count, True)
     for gather in gathers:
         gather.start()
-    relays = [(gather, piece) for gather in gathers for piece in range(gather.pieces)]
-    fourth = -(-len(relays) // chunks)
+    fourth = -(-gathers[0].pieces // chunks)
+
+    def relay(gather, chunk):
+        for k in range(chunks):
+            pieces = range(gather.pieces)[k * fourth : (k + 1) * fourth]
+            if pieces:
+
+                @pl.when(chunk == k)
+                def _():
+                    for piece in pieces:
+                        gather.relay(piece)
+
 
     def project(chunk, carry):
         here = at_rows(chunk, size)
         weights = out_ref[:, :, pl.ds(channels, channels)].reshape(width, channels)
-        part_a[here, :] = transposed_dot(g_ref[here, :], weights).astype(BF)
+        part[here, :] = transposed_dot(g_ref[here, :], weights).astype(BF)
         mix.near_copy(chunk).start()
         return carry
 
@@ -1147,26 +1171,20 @@
         scale = lax.rsqrt(jnp.mean(hidden * hidden, axis=1, keepdims=True) + EPS)
         norm_ref[mix.own_rows(chunk), :] = (hidden * scale * gain_ref[...]).astype(BF)
         mix.far_back(chunk).start()
-        for k in range(chunks):
-            if relays[k * fourth : (k + 1) * fourth]:
-
-                @pl.when(chunk == k)
-                def _():
-                    for gather, piece in relays[k * fourth : (k + 1) * fourth]:
-                        gather.relay(piece)
-
-        return carry
-
+        relay(gathers[0], chunk)
+        return carry
+
+    fetch.wait(0)
     lax.fori_loop(0, chunks, normalise, 0)
+    fetch.wait(1)
     mix.far_back(0).wait_recv()
     mix.near_back(0).start()
-    for gather in gathers:
-        gather.finish()
+    gathers[0].finish()
     per_block = max(1, count // 4)
     wide = per_block * shard
     lanes_block = 256 if units % 256 == 0 else units
 
-    def feed(chunk, carry):
+    def widen(chunk, carry):
         here = at_rows(chunk, size)
 
         @pl.when(chunk + 1 < chunks)
@@ -1176,12 +1194,26 @@
 
         mix.near_back(chunk).wait_recv()
         rows = norm_ref[here, :]
+        for k in range(units // lanes_block):
+            lanes = pl.ds(k * lanes_block, lanes_block)
+            block = lambda ref: ref[:, :, lanes].reshape(width, lanes_block)
+            gate_buf[here, lanes] = jnp.dot(rows, block(gate_ref), preferred_element_type=F32)
+            up_buf[here, lanes] = jnp.dot(rows, block(up_ref), preferred_element_type=F32)
+        relay(gathers[1], chunk)
+        return carry
+
+    lax.fori_loop(0, chunks, widen, 0)
+    gathers[1].finish()
+    fetch.wait(2)
+
+    def feed(chunk, carry):
+        here = at_rows(chunk, size)
+        mix.near_copy(chunk).wait_send()
         grads = low_ref[here, :]
         for k in range(units // lanes_block):
             lanes = pl.ds(k * lanes_block, lanes_block)
             block = lambda ref: ref[:, :, lanes].reshape(width, lanes_block)
-            gate = jnp.dot(rows, block(gate_ref), preferred_element_type=F32)
-            up = jnp.dot(rows, block(up_ref), preferred_element_type=F32)
+            gate, up = gate_buf[here, lanes], up_buf[here, lanes]
             d_act = jnp.dot(grads, block(down_ref), preferred_element_type=F32)
             logistic = 1.0 / (1.0 + jnp.exp(-gate))
             silu = gate * logistic
@@ -1194,7 +1226,7 @@
             block = lambda ref: ref[pl.ds(k * per_block, per_block)].reshape(wide, units)
             total = transposed_dot(dgate_ref[here, :], block(gate_ref))
             total = total + transposed_dot(dup_ref[here, :], block(up_ref))
-            part_b[here, lanes] = total.astype(BF)
+            part[here, lanes] = total.astype(BF)
         back.near_copy(chunk).start()
         for k in range(count // per_block):
             lanes = pl.ds(k * wide, wide)
@@ -1239,7 +1271,7 @@
 
     def finish(chunk, carry):
         back.near_back(chunk).wait_recv()
-        mix.finish(chunk)
+        mix.finish(chunk, False)
         back.finish(chunk)
         return carry
 
@@ -1286,14 +1318,16 @@
     ]
     return pl.pallas_call(
         functools.partial(ffn_kernel, count, CHUNKS),
-        in_specs=[in_vmem] * 6 + [anywhere] * 2,
+        in_specs=[in_vmem] * 3 + [anywhere] * 5,
         out_specs=tuple([in_vmem] * len(outs)),
         out_shape=tuple(outs),
         scratch_shapes=[pltpu.VMEM((count,) + w_down_t.shape, BF)] * 2
         + sum_scratch(rows, width)
-        + sum_scratch(rows, width)
+        + sum_scratch(rows, width, False)
         + [kept_scratch(rows, width)]
+        + [pltpu.VMEM((rows, units), F32)] * 2
         + [SUM_SEMS] * 2
+        + fetch_scratch([x_low, gate_blocks, grad_low])
         + gather_sems(count // 2, units) * 2,
         compiler_params=pltpu.CompilerParams(
             collective_id=5, has_side_effects=True, vmem_limit_bytes=62 * 1024 * 1024
@@ -1301,18 +1335,23 @@
         cost_estimate=pl.CostEstimate(
             flops=14 * rows * width * units, bytes_accessed=40 * 1024 * 1024, transcendentals=0
         ),
-    )(g_low, mix_blocks, x_low, gain, grad_low, gate_blocks, w_up, w_down_t)
+    )(g_low, mix_blocks, gain, x_low, gate_blocks, grad_low, w_up, w_down_t)
 
 
 def input_kernel(count, chunks, kinds, *refs):
-    inner_ref, z_ref, in_x_ref, mix_ref, x_ref, norm_ref, gain_ref, dhidden_ref, *refs = refs
-    pack_ref, refs = refs[0], refs[1:]
+    inner_ref, z_ref, in_x_ref, gain_ref, dhidden_ref, *refs = refs
+    sources, pack_ref, refs = refs[:3], refs[3], refs[4:]
     olds, refs = [refs[k * kinds : (k + 1) * kinds] for k in range(3)], refs[3 * kinds :]
     out_ref, gain_out_ref, *refs = refs
     own_refs, refs = refs[: kinds + 1], refs[kinds + 1 :]
     pack_given, pack_came, *refs = refs
     part, half, give, take, kept, rows_ref, buffer, sems, *refs = refs
     sent, got, vector_sems, grad_ref, given, came, *refs = refs
+    norm_ref, mix_ref, x_ref, fetch_sems, *refs = refs
+    channels = inner_ref.shape[1]
+    sources = [sources[0], sources[1].at[:, :, pl.ds(0, channels)], sources[2]]
+    fetch = Fetch(sources, (norm_ref, mix_ref, x_ref), fetch_sems)
+    fetch.start()
     owned = OwnSum(count, olds, own_refs, refs[:3])
     refs = refs[3:]
     scatter = PairScatter(count, [grad_ref], [given], [came], refs[:8])
@@ -1328,6 +1367,7 @@
     owned.load(0)
     around, _, shard_rows, _ = grad_ref.shape
     together = max(1, 384 // (2 * shard_rows))
+    fetch.wait(0)
     for block in range(around // together):
         lanes = pl.ds(block * together * 2 * shard_rows, together * 2 * shard_rows)
         grad = jnp.dot(norm_ref[:, lanes].T, inner_ref[...], preferred_element_type=F32)
@@ -1357,12 +1397,14 @@
                 def _():
                     owned.add(first + k)
 
+    fetch.wait(1, 2)
+
     def project(chunk, carry):
         here = at_rows(chunk, size)
         for k in range(count // per_block):
             blocks = pl.ds(k * per_block, per_block)
             total = transposed_dot(inner_ref[here, :], in_x_ref[blocks].reshape(wide, channels))
-            in_z = mix_ref[blocks, :, pl.ds(0, channels)].reshape(wide, channels)
+            in_z = mix_ref[blocks].reshape(wide, channels)
             total = total + transposed_dot(z_ref[here, :], in_z)
             part[here, pl.ds(k * wide, wide)] = total.astype(BF)
         back.near_copy(chunk).start()
@@ -1544,7 +1586,7 @@
     late = shape((around, 2, shard, channels), BF)
     return pl.pallas_call(
         functools.partial(input_kernel, count, CHUNKS, len(grads)),
-        in_specs=[in_vmem] * 8 + [anywhere] * (3 * len(grads) + 1),
+        in_specs=[in_vmem] * 5 + [anywhere] * (3 * len(grads) + 4),
         out_specs=tuple(
             [in_vmem] * 2 + [anywhere] * len(grads) + [in_vmem] + [anywhere] * len(moved)
         ),
@@ -1561,6 +1603,7 @@
         + [pltpu.SemaphoreType.DMA((2, around + 2))]
         + [pltpu.VMEM(late.shape, BF), pltpu.VMEM((around, shard, channels), BF)]
         + [pltpu.VMEM((around - 1, shard, channels), BF)]
+        + fetch_scratch([x_norm, in_x_blocks, x_low])
         + [pltpu.VMEM((around + 1, shard, widest), BF), pltpu.VMEM((shard, widest), F32)]
         + [pltpu.SemaphoreType.DMA((around + 2,))]
         + scatter_scratch(count, [late])
@@ -1577,16 +1620,37 @@
         d_inner,
         d_z,
         in_x_blocks,
+        gain,
+        d_hidden,
+        x_norm,
         mix_blocks,
         x_low,
-        x_norm,
-        gain,
-        d_hidden,
         pack,
         *grads,
         *given,
         *came,
     )
+
+
+class Fetch:
+    def __init__(self, sources, targets, sems):
+        self.copies = [
+            pltpu.make_async_copy(source, target, sems.at[k])
+            for k, (source, target) in enumerate(zip(sources, targets))
+        ]
+
+    def start(self):
+        for copy in self.copies:
+            copy.start()
+
+    def wait(self, *which):
+        for k in which:
+            self.copies[k].wait()
+
+
+def fetch_scratch(values):
+    buffers = [pltpu.VMEM(value.shape, value.dtype) for value in values]
+    return buffers + [pltpu.SemaphoreType.DMA((len(values),))]
 
 
 def pairs_of(axis):
@@ -1906,24 +1970,30 @@
     d_z = (d_g * y_full * silu_slope(z_gate)).astype(BF)
     grad_skip = jnp.sum(d_y * u_rows, axis=0)
     grad_block = shape((count // 2, 2, width // count, w_gate.shape[1]), BF)
-    last, grad_down, grad_gate, grad_up, block_out = state_call(
+    down_moved = moved_shapes([grad_block])
+    fetched = [ffn_part, grad_low, act_low, x_norm2, d_gate, d_up, hidden]
+    last, grad_down, grad_gate, grad_up, block_out, *down_moved = state_call(
         adjoint_kernel,
         3,
         seqs,
         states,
         states + 2,
-        [parts, step, d_y, rate_rows, step_sum, x_norm2, grad_low, act_low, d_gate, d_up]
-        + [ffn_part, hidden],
-        [shape((state_rows, channels), F32)] + [grad_block] * 3 + [shape(x_in.shape, BF)],
+        [parts, step, d_y, rate_rows, step_sum] + fetched,
+        [shape((state_rows, channels), F32)]
+        + [grad_block] * 3
+        + [shape(x_in.shape, BF)]
+        + down_moved,
         exchange_scratch(count, seqs, states, channels)
         + sum_scratch(rows, width, False)
         + [kept_scratch(rows, width), pltpu.VMEM((rows, width), BF)]
-        + [pltpu.VMEM((width // LANES, rows // CHUNKS, LANES), F32), SUM_SEMS],
+        + [pltpu.VMEM((width // LANES, rows // CHUNKS, LANES), F32), SUM_SEMS]
+        + fetch_scratch(fetched)
+        + scatter_scratch(count, [grad_block]),
         6,
-        (0, 0),
+        (7, 2),
     )
     grad_in_z = jnp.einsum("rd,re->de", x_norm, d_z, preferred_element_type=F32)
-    big_grads = [grad_down, grad_gate, grad_up]
+    big_grads = [grad_gate, grad_up]
     big_grads += [owner_blocks(grad.astype(BF)) for grad in (grad_out_w, grad_in_z)]
     padded = lambda value: jnp.pad(value, ((0, 0), (0, LANES - value.shape[1])))
     taps_table = jnp.concatenate([conv_weight, skip_vec[None, :]], axis=0)
@@ -1995,7 +2065,11 @@
         norm1_vec[None, :],
         d_hidden,
         small,
-        (big_grads, first_moved[:kinds], first_moved[kinds:]),
+        (
+            [grad_down] + big_grads,
+            down_moved[:1] + first_moved[:kinds],
+            down_moved[1:] + first_moved[kinds:],
+        ),
         x_in.shape,
     )
     own_down, own_gate, own_up, own_out, own_in_z, own_in_x = owns

time: 783 us -> 762 us (0.973)
  Pallas kernels: 642 us -> 621 us
    pallas_call x4, Pallas kernels: 362 us -> 349 us  [state_call(): pl.pallas_call(functools.partial(body, count, seqs, states), in_specs=[in...]
  transfers between devices with their start and end apart: 7 -> 7, of which waited for: 3 -> 3; matrix products, arithmetic and copies ran while one was open for 4% -> 5% of each run, Pallas kernels for 6% -> 6%
where the time goes in v5:
time: 762 us; the launch traced here: 756 us
  Pallas kernels  621 us (81%)
  local copies, waits for them, and re-layouts  42.4 us (6%)
  matrix products  33.4 us (4%)
  other arithmetic  29 us (4%)
  between operations  15.1 us (2%)
  starting transfers between devices  9.74 us (1%)
    pallas_call x4, Pallas kernels, state_call(): pl.pallas_call(functools.partial(body, count, seqs, states), in_specs=[in...  349 us
    pallas_call x1, Pallas kernels, ffn_call(): pl.pallas_call(functools.partial(ffn_kernel, count, CHUNKS), in_specs=[in...  145 us
    pallas_call x1, Pallas kernels, input_call(): pl.pallas_call(functools.partial(input_kernel, count, CHUNKS, len(grads))...  81.8 us
    pallas_call x1, Pallas kernels, first_gather(): pl.pallas_call(functools.partial(first_kernel, count, len(values), len(pl...  45.4 us
    unnamed x72, local copies, waits for them, and re-layouts  23.5 us
  transfers between devices with their start and end apart: 7, of which 3 were waited for; matrix products, arithmetic and copies ran while one was open for 5% of the time, Pallas kernels for 6%

profile of v5, /device:TPU:0, one launch (start us, length us, event | category | flops | bytes accessed | tf_op | source)
XLA Modules:
  0.0 756.4 jit_solution(16846599515848927113)
XLA Ops:
  15.2 1.1 convert_element_type.240.refs_0_
  16.3 1.1 convert_bitcast_fusion.1
  17.4 1.1 convert_element_type.250
  19.4 1.9 copy-done.2
  21.3 45.4 %shard_map.322 = (bf16[8,192,768]{2,1,0:T(8,128)(2,1)S(1)}, bf16[8,112,256]{2,1,0:T(8,128)(2,1)S(1)}, bf16[1024,1536]{1,0:T(8,128)(2,1)S(1)}, bf16[1024,1536]{1,0:T(8,128)(2,1)S(1)}) custom-call(bf16[192,768]{1,0:T(8,128)(2,1)S(1)} %convert_element_type.240.refs_0_, bf16[112,256]{1,0:T(8,128)(2,1)S(1)} %maximum_bitcast_fusion.1.refs_1_, ...), custom_call_target="tpu_custom_call" | custom-call | tf_op jit(solution)/shard_map/pallas_call | solution.py:1792
  66.7 1.7 copy-done.1
  68.4 1.4 copy-done.3
  74.0 2.6 convolution_convert_fusion.2
  76.7 1.5 collective-permute-start
  78.4 6.1 collective-permute-start.1
  86.7 2.1 fusion.19
  88.8 3.9 multiply_convert_fusion.2
  94.9 1.6 collective-permute-start.3
  100.7 1.9 convert_element_type.289.refs_6_
  107.1 3.9 concatenate.56.parts_ref
  111.1 3.6 compare_select_fusion.step_ref
  114.6 44.2 %shard_map.323 = (f32[128,768]{1,0:T(8,128)}, f32[8,768]{1,0:T(8,128)}) custom-call(bf16[1024,128]{1,0:T(8,128)(2,1)} %concatenate.56.parts_ref, f32[1024,768]{1,0:T(8,128)} %compare_select_fusion.step_ref, bf16[1024,768]{1,0:T(8,128)(2,1)} %copy-done.7, f32[128,768]{1,0:T(8,128)} %broadcast_bitcast_fusion.rate_ref), custom_call_target="tpu_custom_call" | custom-call | flops 75497472 | bytes 16777216 | tf_op jit(solution)/shard_map/pallas_call | solution.py:919
  158.8 1.7 all-gather.2.cloned.1.call-done
  160.6 59.3 %shard_map.324 = (f32[1024,768]{1,0:T(8,128)}, bf16[8,192,1024]{2,1,0:T(8,128)(2,1)}) custom-call(bf16[1024,128]{1,0:T(8,128)(2,1)} %concatenate.56.parts_ref, f32[1024,768]{1,0:T(8,128)} %compare_select_fusion.step_ref, bf16[1024,768]{1,0:T(8,128)(2,1)} %copy-done.7, f32[128,768]{1,0:T(8,128)} %broadcast_bitcast_fusion.rate_ref, ...), custom_call_target="tpu_custom_call" | custom-call | flops 100663296 | bytes 16777216 | tf_op jit(solution)/shard_map/pallas_call | solution.py:919
  219.9 8.6 %multiply_convert_fusion.1 = (bf16[1024,768]{1,0:T(8,128)(2,1)}, f32[1024,768]{1,0:T(8,128)}) fusion(f32[1024,768]{1,0:T(8,128)} %get-tuple-element.77, bf16[1024,768]{1,0:T(8,128)(2,1)S(1)} %copy-done.8, f32[768]{0:T(1024)S(1)} %get-tuple-element.232, bf16[1024,1536]{1,0:T(8,128)(2,1)} %copy-done.10, bf16[1536,1536]{1,0:T(8,128)(2,1)} %all-gather.2.cloned.1.call-done), kind=kOutput, calls=%fused_computation.24 | convolution fusion | flops 2422996992 | bytes 14945280 | tf_op jit(solution)/shard_map/dot_general | solution.py:1949
  228.4 144.5 %shard_map.325 = (f32[256,1536]{1,0:T(8,128)}, bf16[1024,1536]{1,0:T(8,128)(2,1)}, bf16[1024,1024]{1,0:T(8,128)(2,1)}, bf16[1024,1024]{1,0:T(8,128)(2,1)}, bf16[...) custom-call(bf16[1024,768]{1,0:T(8,128)(2,1)} %get-tuple-element.271, ...), custom_call_target="tpu_custom_call" | custom-call | flops 22548578304 | bytes 41943040 | tf_op jit(solution)/shard_map/pallas_call | solution.py:1319
  373.0 6.6 convolution_convert_fusion.1
  379.7 7.3 fusion.4
  387.0 4.2 convolution_convert_fusion
  391.1 90.6 %shard_map.326 = (f32[128,768]{1,0:T(8,128)}, bf16[4,2,192,1024]{3,2,1,0:T(8,128)(2,1)}, bf16[4,2,192,1024]{3,2,1,0:T(8,128)(2,1)}, bf16[4,2,192,1024]{3,2,1,0:T...) custom-call(bf16[1024,128]{1,0:T(8,128)(2,1)} %concatenate.56.parts_ref, ...), custom_call_target="tpu_custom_call" | custom-call | flops 75497472 | bytes 16777216 | tf_op jit(solution)/shard_map/pallas_call | solution.py:919
  481.8 155.3 %shard_map.327 = (bf16[1024,768]{1,0:T(8,128)(2,1)}, f32[8,128]{1,0:T(8,128)}, f32[768,128]{1,0:T(8,128)}, f32[768,128]{1,0:T(8,128)}, f32[16,768]{1,0:T(8,128)}...) custom-call(bf16[1024,128]{1,0:T(8,128)(2,1)} %concatenate.56.parts_, ...), custom_call_target="tpu_custom_call" | custom-call | flops 377487360 | bytes 16777216 | tf_op jit(solution)/shard_map/pallas_call | solution.py:919
  639.8 1.8 concatenate.58
  643.7 81.8 %shard_map.328 = (f32[8,128,1536]{2,1,0:T(8,128)}, f32[8,1536]{1,0:T(8,128)}, f32[192,1024]{1,0:T(8,128)}, f32[192,1024]{1,0:T(8,128)}, f32[192,1024]{1,0:T(8,12...) custom-call(bf16[1024,768]{1,0:T(8,128)(2,1)} %get-tuple-element.93., ...), custom_call_target="tpu_custom_call" | custom-call | flops 4831838208 | bytes 41943040 | tf_op jit(solution)/shard_map/pallas_call | solution.py:1587
  725.5 1.1 fusion.24
  728.6 3.1 collective-permute-done.5
  736.5 3.9 copy.199
  741.3 2.7 copy.200
  (190 shorter events, 43.7 us)
Async XLA Ops:
  7.2 153.4 %all-gather.2.cloned.1.call-start = ((), (), s32[]{:S(2)}) async-start(), calls=%async_computation | async-start | bytes 5308416 | tf_op jit(solution)/shard_map/all_gather | solution.py:1880
  19.4 1.9 copy-start.2
  66.7 1.7 copy-start.1
  70.5 2.6 copy-start
  72.4 1.7 copy-start.4
  73.2 3.5 copy-start.10
  74.0 4.1 copy-start.22
  74.0 10.5 %copy-start.6 = (bf16[8,112,256]{2,1,0:T(8,128)(2,1)S(1)}, bf16[8,112,256]{2,1,0:T(8,128)(2,1)}, u32[]{:S(2)}) copy-start(bf16[8,112,256]{2,1,0:T(8,128)(2,1)} %copy-done.5) | copy-start | bytes 1376260
  76.7 10.0 %collective-permute-start = (bf16[24,768]{1,0:T(8,128)(2,1)S(1)}, bf16[24,768]{1,0:T(8,128)(2,1)S(1)}, u32[]{:S(2)}, u32[]{:S(2)}) collective-permute-start(bf16[24,768]{1,0:T(8,128)(2,1)S(1)} %slice.252), channel_id=1, source_target_pairs={{0,4},{4,8},{8,12},{12,16},{16,20},{20,24},{24,28},{1,5},{5,9},{9,... | collective-permute-start | bytes 110600 | tf_op jit(solution)/shard_map/ppermute | solution.py:22
  78.4 8.1 %collective-permute-start.1 = (s32[24]{0:T(128)S(1)}, s32[24]{0:T(128)S(1)}, u32[]{:S(2)}, u32[]{:S(2)}) collective-permute-start(s32[24]{0:T(128)S(1)} %slice.197), channel_id=1, source_target_pairs={{0,4},{4,8},{8,12},{12,16},{16,20},{20,24},{24,28},{1,5},{5,9},{9,... | collective-permute-start | bytes 296 | tf_op jit(solution)/shard_map/ppermute | solution.py:22
  88.8 4.6 copy-start.14
  92.7 9.9 %copy-start.7 = (bf16[1024,768]{1,0:T(8,128)(2,1)}, bf16[1024,768]{1,0:T(8,128)(2,1)S(1)}, u32[]{:S(2)}) copy-start(bf16[1024,768]{1,0:T(8,128)(2,1)S(1)} %get-tuple-element.250.u_ref) | copy-start | bytes 4718596
  92.7 6.5 copy-start.15
  93.3 1.6 collective-permute-start.2
  94.9 9.2 %collective-permute-start.3 = (bf16[1024,128]{1,0:T(8,128)(2,1)S(1)}, bf16[1024,128]{1,0:T(8,128)(2,1)S(1)}, u32[]{:S(2)}, u32[]{:S(2)}) collective-permute-start(bf16[1024,128]{1,0:T(8,128)(2,1)S(1)} %add_convert_fusion), channel_id=1, source_target_pairs={{0,2},{1,3},{2,0},{3,1},{4,6},{5,7},{6,4},{7,5},{8,10},{9,11},{10,... | collective-permute-start | bytes 786440 | tf_op jit(solution)/shard_map/ppermute | solution.py:1666
  104.2 2.0 copy-start.9
  158.8 61.1 %copy-start.8 = (bf16[1024,768]{1,0:T(8,128)(2,1)S(1)}, bf16[1024,768]{1,0:T(8,128)(2,1)}, u32[]{:S(2)}) copy-start(bf16[1024,768]{1,0:T(8,128)(2,1)} %copy-done.7) | copy-start | bytes 4718596
  373.0 6.6 copy-start.24
  373.0 6.6 copy-start.25
  373.0 6.6 copy-start.26
  379.7 7.3 copy-start.11
  387.0 4.2 copy-start.13
  639.3 3.2 copy-start.23
  726.6 1.3 collective-permute-start.4
  727.9 3.8 collective-permute-start.5
  736.5 4.9 copy-start.12
  741.3 2.7 copy-start.21
  741.3 3.5 copy-start.20
  741.3 4.4 copy-start.19
  744.0 2.5 copy-start.18
  744.0 3.3 copy-start.17
  744.1 4.2 copy-start.16
  (2 other events, 2.1 us)
Sparse Core Ops, SparseCore 0:
  70.7 89.8 all-gather.1

commit v6 on v5

--- a/solution.py
+++ b/solution.py
@@ -322,9 +322,9 @@
 
         lax.fori_loop(0, tokens // GROUP, one, state_blocks(start_ref, lanes, seqs, states))
         for piece in range(gather.pieces):
-            if 3 * piece + 2 < tiles:
-
-                @pl.when(tile == 3 * piece + 2)
+            if 2 * piece + 1 < tiles:
+
+                @pl.when(tile == 2 * piece + 1)
                 def _():
                     gather.relay(piece)
 
@@ -332,7 +332,7 @@
 
     lax.fori_loop(0, tiles, whole, 0)
     for piece in range(gather.pieces):
-        if 3 * piece + 2 >= tiles:
+        if 2 * piece + 1 >= tiles:
             gather.relay(piece)
     gather.finish()
 
@@ -998,7 +998,7 @@
 
 
 def pieces_of(width):
-    for size in (384, 256):
+    for size in (256, 384):
         if width % size == 0:
             return width // size
     return 1

time: 762 us -> 764 us (level)
  no operation moved by 1% of the time
where the time goes in v6:
time: 764 us; the launch traced here: 758 us
  Pallas kernels  623 us (82%)
  local copies, waits for them, and re-layouts  42.4 us (6%)
  matrix products  33.4 us (4%)
  other arithmetic  29 us (4%)
  between operations  15.1 us (2%)
  starting transfers between devices  9.44 us (1%)
    pallas_call x4, Pallas kernels, state_call(): pl.pallas_call(functools.partial(body, count, seqs, states), in_specs=[in...  355 us
    pallas_call x1, Pallas kernels, ffn_call(): pl.pallas_call(functools.partial(ffn_kernel, count, CHUNKS), in_specs=[in...  144 us
    pallas_call x1, Pallas kernels, input_call(): pl.pallas_call(functools.partial(input_kernel, count, CHUNKS, len(grads))...  78.9 us
    pallas_call x1, Pallas kernels, first_gather(): pl.pallas_call(functools.partial(first_kernel, count, len(values), len(pl...  45.1 us
    unnamed x72, local copies, waits for them, and re-layouts  23.5 us
  transfers between devices with their start and end apart: 7, of which 3 were waited for; matrix products, arithmetic and copies ran while one was open for 5% of the time, Pallas kernels for 6%

profile of v6, /device:TPU:0, one launch (start us, length us, event | category | flops | bytes accessed | tf_op | source)
XLA Modules:
  0.0 757.9 jit_solution(8327838826922737916)
XLA Ops:
  15.2 1.1 convert_element_type.240.refs_0_
  16.3 1.1 convert_bitcast_fusion.1
  17.4 1.1 convert_element_type.250
  19.4 1.9 copy-done.2
  21.3 45.1 %shard_map.322 = (bf16[8,192,768]{2,1,0:T(8,128)(2,1)S(1)}, bf16[8,112,256]{2,1,0:T(8,128)(2,1)S(1)}, bf16[1024,1536]{1,0:T(8,128)(2,1)S(1)}, bf16[1024,1536]{1,0:T(8,128)(2,1)S(1)}) custom-call(bf16[192,768]{1,0:T(8,128)(2,1)S(1)} %convert_element_type.240.refs_0_, bf16[112,256]{1,0:T(8,128)(2,1)S(1)} %maximum_bitcast_fusion.1.refs_1_, ...), custom_call_target="tpu_custom_call" | custom-call | tf_op jit(solution)/shard_map/pallas_call | solution.py:1792
  66.4 1.7 copy-done.1
  68.1 1.4 copy-done.3
  73.7 2.6 convolution_convert_fusion.2
  76.3 1.5 collective-permute-start
  78.1 5.8 collective-permute-start.1
  86.0 2.1 fusion.19
  88.2 3.9 multiply_convert_fusion.2
  94.3 1.6 collective-permute-start.3
  100.0 1.9 convert_element_type.289.refs_6_
  106.5 3.9 concatenate.56.parts_ref
  110.4 3.6 compare_select_fusion.step_ref
  114.0 44.6 %shard_map.323 = (f32[128,768]{1,0:T(8,128)}, f32[8,768]{1,0:T(8,128)}) custom-call(bf16[1024,128]{1,0:T(8,128)(2,1)} %concatenate.56.parts_ref, f32[1024,768]{1,0:T(8,128)} %compare_select_fusion.step_ref, bf16[1024,768]{1,0:T(8,128)(2,1)} %copy-done.7, f32[128,768]{1,0:T(8,128)} %broadcast_bitcast_fusion.rate_ref), custom_call_target="tpu_custom_call" | custom-call | flops 75497472 | bytes 16777216 | tf_op jit(solution)/shard_map/pallas_call | solution.py:919
  158.7 1.7 all-gather.2.cloned.1.call-done
  160.4 60.0 %shard_map.324 = (f32[1024,768]{1,0:T(8,128)}, bf16[8,192,1024]{2,1,0:T(8,128)(2,1)}) custom-call(bf16[1024,128]{1,0:T(8,128)(2,1)} %concatenate.56.parts_ref, f32[1024,768]{1,0:T(8,128)} %compare_select_fusion.step_ref, bf16[1024,768]{1,0:T(8,128)(2,1)} %copy-done.7, f32[128,768]{1,0:T(8,128)} %broadcast_bitcast_fusion.rate_ref, ...), custom_call_target="tpu_custom_call" | custom-call | flops 100663296 | bytes 16777216 | tf_op jit(solution)/shard_map/pallas_call | solution.py:919
  220.5 8.6 %multiply_convert_fusion.1 = (bf16[1024,768]{1,0:T(8,128)(2,1)}, f32[1024,768]{1,0:T(8,128)}) fusion(f32[1024,768]{1,0:T(8,128)} %get-tuple-element.77, bf16[1024,768]{1,0:T(8,128)(2,1)S(1)} %copy-done.8, f32[768]{0:T(1024)S(1)} %get-tuple-element.232, bf16[1024,1536]{1,0:T(8,128)(2,1)} %copy-done.10, bf16[1536,1536]{1,0:T(8,128)(2,1)} %all-gather.2.cloned.1.call-done), kind=kOutput, calls=%fused_computation.24 | convolution fusion | flops 2422996992 | bytes 14945280 | tf_op jit(solution)/shard_map/dot_general | solution.py:1949
  229.0 144.0 %shard_map.325 = (f32[256,1536]{1,0:T(8,128)}, bf16[1024,1536]{1,0:T(8,128)(2,1)}, bf16[1024,1024]{1,0:T(8,128)(2,1)}, bf16[1024,1024]{1,0:T(8,128)(2,1)}, bf16[...) custom-call(bf16[1024,768]{1,0:T(8,128)(2,1)} %get-tuple-element.271, ...), custom_call_target="tpu_custom_call" | custom-call | flops 22548578304 | bytes 41943040 | tf_op jit(solution)/shard_map/pallas_call | solution.py:1319
  373.0 6.6 convolution_convert_fusion.1
  379.7 7.3 fusion.4
  387.0 4.2 convolution_convert_fusion
  391.1 91.9 %shard_map.326 = (f32[128,768]{1,0:T(8,128)}, bf16[4,2,192,1024]{3,2,1,0:T(8,128)(2,1)}, bf16[4,2,192,1024]{3,2,1,0:T(8,128)(2,1)}, bf16[4,2,192,1024]{3,2,1,0:T...) custom-call(bf16[1024,128]{1,0:T(8,128)(2,1)} %concatenate.56.parts_ref, ...), custom_call_target="tpu_custom_call" | custom-call | flops 75497472 | bytes 16777216 | tf_op jit(solution)/shard_map/pallas_call | solution.py:919
  483.0 158.5 %shard_map.327 = (bf16[1024,768]{1,0:T(8,128)(2,1)}, f32[8,128]{1,0:T(8,128)}, f32[768,128]{1,0:T(8,128)}, f32[768,128]{1,0:T(8,128)}, f32[16,768]{1,0:T(8,128)}...) custom-call(bf16[1024,128]{1,0:T(8,128)(2,1)} %concatenate.56.parts_, ...), custom_call_target="tpu_custom_call" | custom-call | flops 377487360 | bytes 16777216 | tf_op jit(solution)/shard_map/pallas_call | solution.py:919
  644.3 1.8 concatenate.58
  648.1 78.9 %shard_map.328 = (f32[8,128,1536]{2,1,0:T(8,128)}, f32[8,1536]{1,0:T(8,128)}, f32[192,1024]{1,0:T(8,128)}, f32[192,1024]{1,0:T(8,128)}, f32[192,1024]{1,0:T(8,12...) custom-call(bf16[1024,768]{1,0:T(8,128)(2,1)} %get-tuple-element.93., ...), custom_call_target="tpu_custom_call" | custom-call | flops 4831838208 | bytes 41943040 | tf_op jit(solution)/shard_map/pallas_call | solution.py:1587
  727.0 1.1 fusion.24
  730.1 3.1 collective-permute-done.5
  738.0 3.9 copy.199
  742.8 2.7 copy.200
  (190 shorter events, 43.7 us)
Async XLA Ops:
  7.2 153.2 %all-gather.2.cloned.1.call-start = ((), (), s32[]{:S(2)}) async-start(), calls=%async_computation | async-start | bytes 5308416 | tf_op jit(solution)/shard_map/all_gather | solution.py:1880
  19.4 1.9 copy-start.2
  66.4 1.7 copy-start.1
  70.2 2.6 copy-start
  72.0 1.7 copy-start.4
  72.8 3.5 copy-start.10
  73.7 4.1 copy-start.22
  73.7 10.2 %copy-start.6 = (bf16[8,112,256]{2,1,0:T(8,128)(2,1)S(1)}, bf16[8,112,256]{2,1,0:T(8,128)(2,1)}, u32[]{:S(2)}) copy-start(bf16[8,112,256]{2,1,0:T(8,128)(2,1)} %copy-done.5) | copy-start | bytes 1376260
  76.3 9.7 %collective-permute-start = (bf16[24,768]{1,0:T(8,128)(2,1)S(1)}, bf16[24,768]{1,0:T(8,128)(2,1)S(1)}, u32[]{:S(2)}, u32[]{:S(2)}) collective-permute-start(bf16[24,768]{1,0:T(8,128)(2,1)S(1)} %slice.252), channel_id=1, source_target_pairs={{0,4},{4,8},{8,12},{12,16},{16,20},{20,24},{24,28},{1,5},{5,9},{9,... | collective-permute-start | bytes 110600 | tf_op jit(solution)/shard_map/ppermute | solution.py:22
  78.1 7.8 %collective-permute-start.1 = (s32[24]{0:T(128)S(1)}, s32[24]{0:T(128)S(1)}, u32[]{:S(2)}, u32[]{:S(2)}) collective-permute-start(s32[24]{0:T(128)S(1)} %slice.197), channel_id=1, source_target_pairs={{0,4},{4,8},{8,12},{12,16},{16,20},{20,24},{24,28},{1,5},{5,9},{9,... | collective-permute-start | bytes 296 | tf_op jit(solution)/shard_map/ppermute | solution.py:22
  88.1 4.6 copy-start.14
  92.0 9.9 %copy-start.7 = (bf16[1024,768]{1,0:T(8,128)(2,1)}, bf16[1024,768]{1,0:T(8,128)(2,1)S(1)}, u32[]{:S(2)}) copy-start(bf16[1024,768]{1,0:T(8,128)(2,1)S(1)} %get-tuple-element.250.u_ref) | copy-start | bytes 4718596
  92.0 6.5 copy-start.15
  92.6 1.6 collective-permute-start.2
  94.3 9.2 %collective-permute-start.3 = (bf16[1024,128]{1,0:T(8,128)(2,1)S(1)}, bf16[1024,128]{1,0:T(8,128)(2,1)S(1)}, u32[]{:S(2)}, u32[]{:S(2)}) collective-permute-start(bf16[1024,128]{1,0:T(8,128)(2,1)S(1)} %add_convert_fusion), channel_id=1, source_target_pairs={{0,2},{1,3},{2,0},{3,1},{4,6},{5,7},{6,4},{7,5},{8,10},{9,11},{10,... | collective-permute-start | bytes 786440 | tf_op jit(solution)/shard_map/ppermute | solution.py:1666
  103.6 2.0 copy-start.9
  158.6 61.8 %copy-start.8 = (bf16[1024,768]{1,0:T(8,128)(2,1)S(1)}, bf16[1024,768]{1,0:T(8,128)(2,1)}, u32[]{:S(2)}) copy-start(bf16[1024,768]{1,0:T(8,128)(2,1)} %copy-done.7) | copy-start | bytes 4718596
  373.0 6.6 copy-start.24
  373.0 6.6 copy-start.25
  373.0 6.6 copy-start.26
  379.6 7.3 copy-start.11
  386.9 4.2 copy-start.13
  643.7 3.2 copy-start.23
  728.1 1.3 collective-permute-start.4
  729.4 3.8 collective-permute-start.5
  738.0 4.9 copy-start.12
  742.8 2.7 copy-start.21
  742.8 3.5 copy-start.20
  742.8 4.4 copy-start.19
  745.5 2.5 copy-start.18
  745.5 3.3 copy-start.17
  745.5 4.2 copy-start.16
  (2 other events, 2.1 us)
Sparse Core Ops, SparseCore 0:
  70.4 90.0 all-gather.1
